TPU v7x, 512 devices: a whole 4x8x8 slice. The times are simulated.
512 devices in a mesh: dp: 32 (over z, x), head: 16 (over y, core).
Axes of the slice: x: 4, y: 8, z: 8, core: 2. Of those that a mesh axis runs over, the one named last changes fastest.
Arguments:
- inputs: bfloat16 [16384, 4608], P('dp', 'head'), may hold values from -6 to 6
- w_query: bfloat16 [4608, 4096], P('dp', 'head'), may hold values from -0.3125 to 0.3125
- w_key: bfloat16 [4608, 2048], P('dp', 'head'), may hold values from -0.3125 to 0.3125
- w_value: bfloat16 [4608, 2048], P('dp', 'head'), may hold values from -0.09375 to 0.09375
- cotangent: bfloat16 [16384, 4096], P('dp', 'head'), may hold values from -150 to 150
- lengths: int32 [64], P('dp'), may hold values from 32 to 256, as said below
- sampled: int32 [64], P('dp'), may hold values 0 or 1
- step: int32 [1], replicated, may hold values from 1 to 15
- tree_noise: float32 [4, 2, 4608, 2048], P(None, None, 'dp', 'head'), may hold values from -1.75 to 1.75
Outputs:
- noisy_key_gradient: float32 [4608, 2048], P('dp', 'head')
- noisy_value_gradient: float32 [4608, 2048], P('dp', 'head')
Inputs may be any that keep to these rules, and one draw needn't show every extreme that they name: `lengths`: every draw has a sequence of exactly 256 and one of exactly 32 tokens.
All inputs are finite; a program needn't handle non-finite values. No bound on the sum of `sampled` on one device may be relied on, other than what follows from the above.
Results may differ from a plain program's by a relative error of at most 0.017.
Values may be sent and summed in bfloat16 or wider, within the bound.
No kernel may reach another device: no remote copies, remote signals or barrier semaphores. Data moves between devices by JAX's collectives and lax.ppermute only.
A program may use at most 64 MiB of HBM per device.

v0:
```python
import math

import jax
import jax.numpy as jnp
from jax import lax
from jax.sharding import PartitionSpec as P

D = 4608
H = 32
KV = 16
HD = 128


cap_value = 50.0


def rope_tables(length, dim):
    half = dim // 2
    freq = 10000.0 ** (-(jnp.arange(half, dtype=jnp.float32) * (2.0 / dim)))
    angle = jnp.arange(length, dtype=jnp.float32)[:, None] * freq[None, :]
    cosine = jnp.cos(angle)
    sine = jnp.sin(angle)
    return (jnp.concatenate([cosine, cosine], 1), jnp.concatenate([sine, sine], 1))


def rotate(vector, cosine, sine):
    half = vector.shape[-1] // 2
    turned = jnp.concatenate([-vector[..., half:], vector[..., :half]], -1)
    return vector * cosine + turned * sine


def unrotate(grad, cosine, sine):
    half = grad.shape[-1] // 2
    turned = jnp.concatenate([grad[..., half:], -grad[..., :half]], -1)
    return grad * cosine + turned * sine


def attend_back(query, key, value, cot, keep, cosine, sine, scale):
    batch, seq, heads_q, dim = query.shape
    heads_k = key.shape[2]
    group = heads_q // heads_k
    grouped = query.reshape(batch, seq, heads_k, group, dim)
    cot_grouped = cot.reshape(batch, seq, heads_k, group, dim)
    raw = jnp.einsum("bqkgd,bskd->bkgqs", grouped, key, preferred_element_type=jnp.float32) * scale
    bend = jnp.tanh(raw / cap_value)
    weights = jnp.where(keep[:, None, None], jnp.exp(cap_value * bend), 0.0)
    probs = weights / jnp.sum(weights, -1, keepdims=True)
    probs_b = probs.astype(jnp.bfloat16)
    noisy_value_gradient = jnp.einsum(
        "bkgqs,bqkgd->bskd", probs_b, cot_grouped, preferred_element_type=jnp.float32
    ).astype(jnp.bfloat16)
    grad_probs = jnp.einsum(
        "bqkgd,bskd->bkgqs", cot_grouped, value, preferred_element_type=jnp.float32
    )
    delta = jnp.sum(probs * grad_probs, -1, keepdims=True)
    grad_scores = (probs * (grad_probs - delta) * (1.0 - bend * bend) * scale).astype(jnp.bfloat16)
    noisy_key_gradient = jnp.einsum(
        "bkgqs,bqkgd->bskd", grad_scores, grouped, preferred_element_type=jnp.float32
    )
    noisy_key_gradient = unrotate(noisy_key_gradient, cosine[:, None, :], sine[:, None, :]).astype(
        jnp.bfloat16
    )
    return (
        noisy_key_gradient.reshape(batch, seq, heads_k * dim),
        noisy_value_gradient.reshape(batch, seq, heads_k * dim),
    )


def body(inputs, w_query, w_key, w_value, cotangent, lengths, sampled, step, tree_noise):
    whole = lax.all_gather(inputs, "head", axis=1, tiled=True)
    tokens = whole.shape[0]
    width = whole.shape[1]
    seq_dev = lengths.shape[0]
    length = tokens // seq_dev
    heads_q = w_query.shape[1] // HD
    heads_k = w_key.shape[1] // HD

    def add_rows(piece):
        return jnp.dot(whole, piece, preferred_element_type=jnp.float32)

    query = add_rows(lax.all_gather(w_query, "dp", axis=0, tiled=True))
    key = add_rows(lax.all_gather(w_key, "dp", axis=0, tiled=True))
    value = add_rows(lax.all_gather(w_value, "dp", axis=0, tiled=True))
    cosine, sine = rope_tables(length, HD)
    query = rotate(
        query.reshape(seq_dev, length, heads_q, HD), cosine[:, None, :], sine[:, None, :]
    ).astype(jnp.bfloat16)
    key = rotate(
        key.reshape(seq_dev, length, heads_k, HD), cosine[:, None, :], sine[:, None, :]
    ).astype(jnp.bfloat16)
    value = value.reshape(seq_dev, length, heads_k, HD).astype(jnp.bfloat16)
    position = jnp.arange(length, dtype=jnp.int32)
    valid = (position[None, :] < lengths[:, None]) & (sampled[:, None] > 0)
    cot = jnp.where(
        valid[:, :, None],
        cotangent.reshape(seq_dev, length, heads_q * HD),
        jnp.zeros((), jnp.bfloat16),
    )
    cot = cot.reshape(seq_dev, length, heads_q, HD)
    keep = (position[:, None] >= position[None, :])[None] & (
        position[None, None, :] < lengths[:, None, None]
    )
    scale = float(D // H) ** (-0.5)
    noisy_key_gradient, noisy_value_gradient = attend_back(
        query, key, value, cot, keep, cosine, sine, scale
    )
    sequence_batch = whole.reshape(seq_dev, length, width)
    input_inner_products = jnp.einsum(
        "gwv,gtv->gwt", sequence_batch, sequence_batch, preferred_element_type=jnp.float32
    )
    key_inner_products = jnp.einsum(
        "gwv,gtv->gwt", noisy_key_gradient, noisy_key_gradient, preferred_element_type=jnp.float32
    )
    value_inner_products = jnp.einsum(
        "gwv,gtv->gwt",
        noisy_value_gradient,
        noisy_value_gradient,
        preferred_element_type=jnp.float32,
    )
    partial_norms = jnp.stack(
        [
            jnp.sum(input_inner_products * key_inner_products, (1, 2)),
            jnp.sum(input_inner_products * value_inner_products, (1, 2)),
        ]
    )
    total_norms = lax.psum(partial_norms, "head")
    clip_bound = 2.0 * math.sqrt(D * KV * HD)
    factors = clip_bound / jnp.maximum(jnp.sqrt(total_norms), clip_bound)
    scaled_key = (factors[0][:, None, None] * noisy_key_gradient.astype(jnp.float32)).astype(
        jnp.bfloat16
    )
    scaled_value = (factors[1][:, None, None] * noisy_value_gradient.astype(jnp.float32)).astype(
        jnp.bfloat16
    )
    joined = jnp.concatenate([scaled_key, scaled_value], -1).reshape(tokens, 2 * w_key.shape[1])
    summed = lax.psum_scatter(
        lax.dot_general(
            whole, joined, (((0,), (0,)), ((), ())), preferred_element_type=jnp.float32
        ).astype(jnp.bfloat16),
        "dp",
        scatter_dimension=0,
        tiled=True,
    ).astype(jnp.float32)
    levels = tree_noise.shape[0]
    bits = (step[0] // 2 ** jnp.arange(levels, dtype=jnp.int32) % 2).astype(jnp.float32)
    noise = jnp.sum(bits[:, None, None, None] * tree_noise, 0)
    expected = 0.85 * (seq_dev * lax.axis_size("dp"))
    columns_k = w_key.shape[1]
    return (
        summed[:, :columns_k] / expected + noise[0],
        summed[:, columns_k:] / expected + noise[1],
    )


def solution(mesh):
    in_specs = (
        P("dp", "head"),
        P("dp", "head"),
        P("dp", "head"),
        P("dp", "head"),
        P("dp", "head"),
        P("dp"),
        P("dp"),
        P(),
        P(None, None, "dp", "head"),
    )
    out_specs = (P("dp", "head"), P("dp", "head"))
    return jax.shard_map(body, mesh=mesh, in_specs=in_specs, out_specs=out_specs, check_vma=False)
```

profile of v0, /device:TPU:1, one launch (start us, length us, event | category | flops | bytes accessed | tf_op | source)
XLA Modules:
  0.0 585.6 jit_solution(15100785141327677576)
XLA Ops:
  7.2 0.7 all-gather.7.cloned.1.call-update
  7.9 0.7 all-gather.5.cloned.1.call-update
  8.7 0.7 all-gather.9.cloned.1.call-update
  9.4 0.5 all-gather.11.cloned.1.call-update
  10.1 0.7 broadcast_compare_fusion
  11.3 1.0 reshape.277
  12.4 0.7 broadcast_and_fusion.1
  13.3 84.2 %all-gather.7.cloned.1.call-done = bf16[4608,256]{1,0:T(8,128)(2,1)} async-done(((bf16[144,256]{1,0:T(8,128)(2,1)}), bf16[4608,256]{1,0:T(8,128)(2,1)}) %all-gather.7.cloned.1.call-update) | async-done | bytes 2359312 | tf_op jit(solution)/shard_map/all_gather | solution.py:81
  97.5 48.3 %all-gather.5.cloned.1.call-done = bf16[512,4608]{0,1:T(8,128)(2,1)} async-done(((bf16[512,288]{0,1:T(8,128)(2,1)}), bf16[512,4608]{0,1:T(8,128)(2,1)}) %all-gather.5.cloned.1.call-update) | async-done | bytes 4718608 | tf_op jit(solution)/shard_map/all_gather | solution.py:70
  145.9 4.5 fusion.58
  150.9 74.8 %all-gather.9.cloned.1.call-done = bf16[4608,128]{1,0:T(8,128)(2,1)} async-done(((bf16[144,128]{1,0:T(8,128)(2,1)}), bf16[4608,128]{1,0:T(8,128)(2,1)}) %all-gather.9.cloned.1.call-update) | async-done | bytes 1179664 | tf_op jit(solution)/shard_map/all_gather | solution.py:82
  225.7 4.1 fusion.59
  230.1 0.5 fusion.8
  231.1 77.7 %all-gather.11.cloned.1.call-done = bf16[4608,128]{1,0:T(8,128)(2,1)} async-done(((bf16[144,128]{1,0:T(8,128)(2,1)}), bf16[4608,128]{1,0:T(8,128)(2,1)}) %all-gather.11.cloned.1.call-update) | async-done | bytes 1179664 | tf_op jit(solution)/shard_map/all_gather | solution.py:83
  308.7 4.1 convolution_convert_fusion.1
  313.2 0.7 convolution_bitcast_fusion.2
  314.1 6.8 %copy.47 = bf16[512,4608]{1,0:T(8,128)(2,1)} copy(bf16[512,4608]{0,1:T(8,128)(2,1)} %all-gather.5.cloned.1.call-done) | data formatting | bytes 9437184 | tf_op jit(solution)/shard_map/all_gather | solution.py:70
  320.9 5.2 fusion.57
  327.0 28.0 %psum.7 = f32[2,2]{1,0:T(2,128)S(1)} all-reduce(f32[2,2]{1,0:T(2,128)S(1)} %pad_maximum_fusion.2), channel_id=1, replica_groups=mesh['dp'=32,'head'=16] {'head'}, use_global_device_ids=true, to_apply=%region_4.5 | all-reduce | flops 4 | bytes 32 | tf_op jit(solution)/shard_map/psum | solution.py:126
  355.4 3.8 fusion
  359.3 2.5 copy.77
  362.7 214.8 %reduce-scatter.4.cloned.1.call-done = bf16[144,256]{1,0:T(8,128)(2,1)} async-done(((bf16[4608,256]{1,0:T(8,128)(2,1)}), bf16[144,256]{1,0:T(8,128)(2,1)}) %reduce-scatter.4.cloned.1.call-update) | async-done | bytes 73744 | tf_op jit(solution)/shard_map/reduce_scatter | solution.py:136
  577.5 0.9 convert_element_type.95
  578.4 0.7 fusion.38
  (40 shorter events, 4.4 us)
Async XLA Ops:
  7.2 90.4 %all-gather.7.cloned.1.call-start = ((), (), s32[]{:S(2)}) async-start(), calls=%async_computation.2 | async-start | bytes 2433024 | tf_op jit(solution)/shard_map/all_gather | solution.py:81
  7.9 138.0 %all-gather.5.cloned.1.call-start = ((), (), s32[]{:S(2)}) async-start(), calls=%async_computation.1 | async-start | bytes 5013504 | tf_op jit(solution)/shard_map/all_gather | solution.py:70
  8.6 217.0 %all-gather.9.cloned.1.call-start = ((), (), s32[]{:S(2)}) async-start(), calls=%async_computation.3 | async-start | bytes 1216512 | tf_op jit(solution)/shard_map/all_gather | solution.py:82
  9.4 299.3 %all-gather.11.cloned.1.call-start = ((), (), s32[]{:S(2)}) async-start(), calls=%async_computation.4 | async-start | bytes 1216512 | tf_op jit(solution)/shard_map/all_gather | solution.py:83
  10.0 567.5 %reduce-scatter.4.cloned.1.call-start = ((), (), s32[]{:S(2)}) async-start(), calls=%async_computation.5 | async-start | bytes 2433024 | tf_op jit(solution)/shard_map/reduce_scatter | solution.py:136
  359.3 3.3 copy-start
Sparse Core Ops, SparseCore 0:
  11.2 86.3 all-gather.6
  99.7 46.1 all-gather.4
  149.1 76.5 all-gather.8
  228.7 79.9 all-gather.10
  361.9 215.5 reduce-scatter.3
where the time goes:
time: 590 us; the launch traced here: 586 us
  waiting for transfers between devices  502 us (85%)
  blocking collectives  28 us (5%)
  matrix products  24.5 us (4%)
  between operations  14.6 us (2%)
  local copies, waits for them, and re-layouts  11.5 us (2%)
    reduce_scatter x1, waiting for transfers between devices, body(): lax.psum_scatter(lax.dot_general(whole, joined, (((0,), (0,)), ((), ())),...  215 us
    all_gather x1, waiting for transfers between devices, body(): query = add_rows(lax.all_gather(w_query, 'dp', axis=0, tiled=True))  84.2 us
    all_gather x1, waiting for transfers between devices, body(): value = add_rows(lax.all_gather(w_value, 'dp', axis=0, tiled=True))  77.7 us
    all_gather x1, waiting for transfers between devices, body(): key = add_rows(lax.all_gather(w_key, 'dp', axis=0, tiled=True))  74.8 us
    all_gather x1, waiting for transfers between devices, body(): whole = lax.all_gather(inputs, 'head', axis=1, tiled=True)  48.3 us
    psum x1, blocking collectives, body(): total_norms = lax.psum(partial_norms, 'head')  28 us
    dot_general x3, matrix products, add_rows(): return jnp.dot(whole, piece, preferred_element_type=jnp.float32)  12.7 us
  transfers between devices with their start and end apart: 5, of which 5 were waited for; matrix products, arithmetic and copies ran while one was open for 2% of the time, Pallas kernels for 0%

commit v1 on v0

v1 whole, which is shorter than its diff:
```python
import functools
import math

import jax
import jax.numpy as jnp
import numpy as np
from jax import lax
from jax.experimental import pallas as pl
from jax.experimental.pallas import tpu as pltpu
from jax.sharding import Mesh
from jax.sharding import PartitionSpec as P

D = 4608
H = 32
KV = 16
HD = 128
L = 256
NZ, NX, NY, NC = 8, 4, 8, 2
SHARD = D // (NY * NC)
PAIR = NC * SHARD
TOKENS = 2 * L
CAP = 50.0
SCALE = float(D // H) ** (-0.5)
CLIP = 2.0 * math.sqrt(D * KV * HD)
VMEM = 48 * 1024 * 1024
F32 = jnp.float32
BF16 = jnp.bfloat16

NN = (((1,), (0,)), ((), ()))
NT = (((1,), (1,)), ((), ()))


def dot(a, b, dims=NN):
    return lax.dot_general(a, b, dims, preferred_element_type=F32)


def ring(n, k):
    return [((i + k) % n, i) for i in range(n)]


def rope_tables(length, dim):
    half = dim // 2
    freq = 10000.0 ** (-(jnp.arange(half, dtype=F32) * (2.0 / dim)))
    angle = jnp.arange(length, dtype=F32)[:, None] * freq[None, :]
    cosine = jnp.cos(angle)
    sine = jnp.sin(angle)
    return jnp.concatenate([cosine, cosine], 1), jnp.concatenate([-sine, sine], 1)


def arrange_kernel(place, mine, other, x_t, x_tok, gram):
    k = pl.program_id(0)
    first = place[1] == 0
    a = mine[0]
    b = other[0]
    block = jnp.concatenate([jnp.where(first, a, b), jnp.where(first, b, a)], 0)
    x_t[...] = block
    rows = block.T
    x_tok[0] = rows

    @pl.when(k == 0)
    def _():
        gram[...] = jnp.zeros_like(gram)

    for s in range(2):
        part = rows[s * L : (s + 1) * L]
        gram[s] += dot(part, part, NT)


def arrange(place, mine, other):
    return pl.pallas_call(
        arrange_kernel,
        grid_spec=pltpu.PrefetchScalarGridSpec(
            num_scalar_prefetch=1,
            grid=(NY,),
            in_specs=[
                pl.BlockSpec((1, SHARD, TOKENS), lambda k, p: (k, 0, 0)),
                pl.BlockSpec((1, SHARD, TOKENS), lambda k, p: (k, 0, 0)),
            ],
            out_specs=[
                pl.BlockSpec((PAIR, TOKENS), lambda k, p: ((p[0] + k) % NY, 0)),
                pl.BlockSpec((1, TOKENS, PAIR), lambda k, p: ((p[0] + k) % NY, 0, 0)),
                pl.BlockSpec((2, L, L), lambda k, p: (0, 0, 0)),
            ],
        ),
        out_shape=[
            jax.ShapeDtypeStruct((D, TOKENS), BF16),
            jax.ShapeDtypeStruct((NY, TOKENS, PAIR), BF16),
            jax.ShapeDtypeStruct((2, L, L), F32),
        ],
        compiler_params=pltpu.CompilerParams(vmem_limit_bytes=VMEM),
        cost_estimate=pl.CostEstimate(
            flops=2 * 2 * L * L * D, bytes_accessed=3 * 2 * D * TOKENS, transcendentals=0
        ),
        name="arrange",
    )(place, mine, other)


def attend_kernel(info, x_tok, w, cot, cosine, sine, gram, dk_out, dv_out, norms, acc):
    k = pl.program_id(0)
    part = dot(x_tok[0], w[...])

    @pl.when(k == 0)
    def _():
        acc[...] = part

    @pl.when(k > 0)
    def _():
        acc[...] += part

    @pl.when(k == NY - 1)
    def _():
        cos = cosine[...]
        sin = sine[...]
        key_at = lax.broadcasted_iota(jnp.int32, (L, L), 0)
        query_at = lax.broadcasted_iota(jnp.int32, (L, L), 1)
        row_at = lax.broadcasted_iota(jnp.int32, (L, HD), 0)

        def rotated(u):
            return (u * cos + pltpu.roll(u, HD // 2, 1) * sin).astype(BF16)

        for s in range(2):
            rows = slice(s * L, (s + 1) * L)
            length = info[s]
            valid = (row_at < length) & (info[2 + s] > 0)
            keep = (key_at <= query_at) & (key_at < length)
            key = rotated(acc[rows, 2 * HD : 3 * HD])
            value = acc[rows, 3 * HD : 4 * HD].astype(BF16)
            dv = jnp.zeros((L, HD), F32)
            dk_rot = jnp.zeros((L, HD), F32)
            for j in range(2):
                query = rotated(acc[rows, j * HD : (j + 1) * HD])
                grad = jnp.where(valid, cot[rows, j * HD : (j + 1) * HD], jnp.zeros((), BF16))
                bend = jnp.tanh(dot(key, query, NT) * (SCALE / CAP))
                weights = jnp.where(keep, jnp.exp(CAP * bend), 0.0)
                probs = weights * (1.0 / jnp.sum(weights, 0, keepdims=True))
                dv += dot(probs.astype(BF16), grad)
                grad_probs = dot(value, grad, NT)
                delta = jnp.sum(probs * grad_probs, 0, keepdims=True)
                ds = probs * (grad_probs - delta) * ((1.0 - bend * bend) * SCALE)
                dk_rot += dot(ds.astype(BF16), query)
            dk = (dk_rot * cos - pltpu.roll(dk_rot, HD // 2, 1) * sin).astype(BF16)
            dv = dv.astype(BF16)
            dk_out[rows] = dk
            dv_out[rows] = dv
            for i, d in enumerate((dk, dv)):
                folded = jnp.sum(gram[s] * dot(d, d, NT), 0, keepdims=True)
                norms[2 * i + s : 2 * i + s + 1] = folded[:, :HD] + folded[:, HD:]


def attend(info, x_tok, w, cot, cosine, sine, gram):
    whole = lambda *shape: pl.BlockSpec(shape, lambda k, p: (0,) * len(shape))
    return pl.pallas_call(
        attend_kernel,
        grid_spec=pltpu.PrefetchScalarGridSpec(
            num_scalar_prefetch=1,
            grid=(NY,),
            in_specs=[
                pl.BlockSpec((1, TOKENS, PAIR), lambda k, p: (k, 0, 0)),
                pl.BlockSpec((PAIR, 4 * HD), lambda k, p: (k, 0)),
                whole(TOKENS, 2 * HD),
                whole(L, HD),
                whole(L, HD),
                whole(2, L, L),
            ],
            out_specs=[whole(TOKENS, HD), whole(TOKENS, HD), whole(4, HD)],
            scratch_shapes=[pltpu.VMEM((TOKENS, 4 * HD), F32)],
        ),
        out_shape=[
            jax.ShapeDtypeStruct((TOKENS, HD), BF16),
            jax.ShapeDtypeStruct((TOKENS, HD), BF16),
            jax.ShapeDtypeStruct((4, HD), F32),
        ],
        compiler_params=pltpu.CompilerParams(vmem_limit_bytes=VMEM),
        cost_estimate=pl.CostEstimate(
            flops=2 * TOKENS * 4 * HD * D + 4 * 12 * L * L * HD,
            bytes_accessed=4 * D * TOKENS,
            transcendentals=8 * L * L,
        ),
        name="attend",
    )(info, x_tok, w, cot, cosine, sine, gram)


def gradient_kernel(x_t, dk, dv, norms, out, scaled):
    @pl.when(pl.program_id(0) == 0)
    def _():
        for i, d in enumerate((dk, dv)):
            for s in range(2):
                total = jnp.sum(norms[:, 2 * i + s, :])
                factor = CLIP / jnp.maximum(jnp.sqrt(jnp.broadcast_to(total, (1, HD))), CLIP)
                rows = slice(s * L, (s + 1) * L)
                scaled[rows, i * HD : (i + 1) * HD] = (factor * d[rows].astype(F32)).astype(BF16)

    out[...] = dot(x_t[...], scaled[...]).astype(BF16)


def gradient(x_t, dk, dv, norms):
    whole = lambda *shape: pl.BlockSpec(shape, lambda k: (0,) * len(shape))
    return pl.pallas_call(
        gradient_kernel,
        grid=(NY,),
        in_specs=[
            pl.BlockSpec((PAIR, TOKENS), lambda k: (k, 0)),
            whole(TOKENS, HD),
            whole(TOKENS, HD),
            whole(NY, 4, HD),
        ],
        out_specs=pl.BlockSpec((PAIR, 2 * HD), lambda k: (k, 0)),
        out_shape=jax.ShapeDtypeStruct((D, 2 * HD), BF16),
        scratch_shapes=[pltpu.VMEM((TOKENS, 2 * HD), BF16)],
        compiler_params=pltpu.CompilerParams(vmem_limit_bytes=VMEM),
        cost_estimate=pl.CostEstimate(
            flops=2 * D * TOKENS * 2 * HD, bytes_accessed=3 * D * TOKENS, transcendentals=0
        ),
        name="gradient",
    )(x_t, dk, dv, norms)


def body(inputs, w_query, w_key, w_value, cotangent, lengths, sampled, step, tree_noise):
    w = jnp.concatenate([w_query, w_key, w_value], 1)
    w = lax.all_gather(w, "x", axis=0, tiled=True)
    w, shard = lax.optimization_barrier((w, inputs.T))
    w = lax.all_gather(w, "z", axis=0, tiled=True)

    mine = jnp.stack([shard] + [lax.ppermute(shard, "y", ring(NY, k)) for k in range(1, NY)])
    other = lax.ppermute(mine, "core", ring(NC, 1))
    place = jnp.stack([lax.axis_index("y"), lax.axis_index("core")]).astype(jnp.int32)
    x_t, x_tok, gram = arrange(place, mine, other)

    cosine, sine = rope_tables(L, HD)
    dk, dv, norms = attend(
        jnp.concatenate([lengths, sampled]), x_tok, w, cotangent, cosine, sine, gram
    )
    norms = lax.psum(norms, "core")
    norms = lax.all_to_all(jnp.broadcast_to(norms, (NY, 4, HD)), "y", 0, 0)
    terms = gradient(x_t, dk, dv, norms)
    terms = lax.all_to_all(terms.reshape(NZ * NX, D // (NZ * NX), 2 * HD), ("z", "x"), 0, 0)
    summed = jnp.sum(terms.astype(F32), 0)

    levels = tree_noise.shape[0]
    bits = (step[0] // 2 ** jnp.arange(levels, dtype=jnp.int32) % 2).astype(F32)
    noise = jnp.sum(bits[:, None, None, None] * tree_noise, 0)
    expected = 0.85 * (2 * NZ * NX)
    return summed[:, :HD] / expected + noise[0], summed[:, HD:] / expected + noise[1]


def solution(mesh):
    mesh = Mesh(np.asarray(mesh.devices).reshape(NZ, NX, NY, NC), ("z", "x", "y", "core"))
    dp, head = ("z", "x"), ("y", "core")
    in_specs = (
        P(dp, head),
        P(dp, head),
        P(dp, head),
        P(dp, head),
        P(dp, head),
        P(dp),
        P(dp),
        P(),
        P(None, None, dp, head),
    )
    out_specs = (P(dp, head), P(dp, head))
    return jax.shard_map(body, mesh=mesh, in_specs=in_specs, out_specs=out_specs, check_vma=False)
```

time: 590 us -> 216 us (0.37)
  waiting for transfers between devices: 502 us -> 98.3 us
  starting transfers between devices: 0.19 us -> 41.4 us
  Pallas kernels: 0 us -> 26.8 us
  matrix products: 24.5 us -> 0 us
  local copies, waits for them, and re-layouts: 11.5 us -> 3.51 us
    all_gather x4 -> x1, waiting for transfers between devices: 285 us -> 0.01 us  [body(): w = lax.all_gather(w, 'z', axis=0, tiled=True)]
    reduce_scatter x1 -> x0, waiting for transfers between devices: 215 us -> none  [body(): lax.psum_scatter(lax.dot_general(whole, joined, (((0,), (0,)), ((), ())),...]
    all_to_all x0 -> x1, waiting for transfers between devices: none -> 52.3 us  [body(): lax.all_to_all(terms.reshape(NZ * NX, D // (NZ * NX), 2 * HD), ('z', 'x')...]
    ppermute x0 -> x8, waiting for transfers between devices: none -> 46 us  [the longest x7 42.6 us: body(): lax.ppermute(shard, 'y', ring(NY, k))]
    ppermute x0 -> x8, starting transfers between devices: none -> 30.1 us  [the longest x7 27.7 us: body(): lax.ppermute(shard, 'y', ring(NY, k))]
    pallas_call x0 -> x3, Pallas kernels: none -> 26.8 us  [the longest x1 10.6 us: attend(): pl.pallas_call(attend_kernel, grid_spec=pltpu.PrefetchScalarGridSpec(num_...]
    psum x1, blocking collectives: 28 us -> 2.5 us  [body(): norms = lax.psum(norms, 'core')]
    dot_general x11 -> x0, matrix products: 24.5 us -> none  [the longest x3 12.7 us: add_rows(): return jnp.dot(whole, piece, preferred_element_type=jnp.float32)]
  transfers between devices with their start and end apart: 5 -> 10, of which waited for: 5 -> 6; matrix products, arithmetic and copies ran while one was open for 2% -> 1% of each run, Pallas kernels for 0% -> 4%
where the time goes in v1:
time: 216 us; the launch traced here: 212 us
  waiting for transfers between devices  98.3 us (46%)
  starting transfers between devices  41.4 us (19%)
  Pallas kernels  26.8 us (12%)
  blocking collectives  24.2 us (11%)
  between operations  14.9 us (7%)
  local copies, waits for them, and re-layouts  3.51 us (2%)
  other arithmetic  3.04 us (1%)
    all_to_all x1, waiting for transfers between devices, body(): lax.all_to_all(terms.reshape(NZ * NX, D // (NZ * NX), 2 * HD), ('z', 'x')...  52.3 us
    ppermute x7, waiting for transfers between devices, body(): lax.ppermute(shard, 'y', ring(NY, k))  42.6 us
    ppermute x7, starting transfers between devices, body(): lax.ppermute(shard, 'y', ring(NY, k))  27.7 us
    all_gather x1, blocking collectives, body(): w = lax.all_gather(w, 'x', axis=0, tiled=True)  12.5 us
    all_to_all x1, starting transfers between devices, body(): lax.all_to_all(terms.reshape(NZ * NX, D // (NZ * NX), 2 * HD), ('z', 'x')...  11.2 us
    pallas_call x1, Pallas kernels, attend(): pl.pallas_call(attend_kernel, grid_spec=pltpu.PrefetchScalarGridSpec(num_...  10.6 us
    all_to_all x1, blocking collectives, body(): norms = lax.all_to_all(jnp.broadcast_to(norms, (NY, 4, HD)), 'y', 0, 0)  9.19 us
    pallas_call x1, Pallas kernels, arrange(): pl.pallas_call(arrange_kernel, grid_spec=pltpu.PrefetchScalarGridSpec(num...  8.61 us
  transfers between devices with their start and end apart: 10, of which 6 were waited for; matrix products, arithmetic and copies ran while one was open for 1% of the time, Pallas kernels for 4%

profile of v1, /device:TPU:1, one launch (start us, length us, event | category | flops | bytes accessed | tf_op | source)
XLA Modules:
  0.0 212.1 jit_solution(11584018732744838519)
XLA Ops:
  7.2 1.0 pad_maximum_fusion
  8.2 12.5 %all_gather.6 = bf16[576,512]{1,0:T(8,128)(2,1)} all-gather(bf16[144,512]{1,0:T(8,128)(2,1)S(1)} %pad_maximum_fusion), channel_id=1, replica_groups=mesh['z'=8,'x'=4,'y'=8,'core'=2] {'x'}, dimensions={0}, use_global_device_ids=true | all-gather | bytes 737280 | tf_op jit(solution)/shard_map/all_gather | solution.py:220
  20.8 5.6 %collective-permute-start = (bf16[288,512]{1,0:T(8,128)(2,1)}, bf16[288,512]{1,0:T(8,128)(2,1)S(1)}, u32[]{:S(2)}, u32[]{:S(2)}) collective-permute-start(bf16[288,512]{1,0:T(8,128)(2,1)} %bitcast.31), channel_id=1, source_target_pairs={{2,0},{4,2},{6,4},{8,6},{10,8},{12,10},{14,12},{0,14},{3,1},{5,3},... | collective-permute-start | bytes 884744 | tf_op jit(solution)/shard_map/ppermute | solution.py:224
  26.4 3.8 %collective-permute-start.1 = (bf16[288,512]{1,0:T(8,128)(2,1)}, bf16[288,512]{1,0:T(8,128)(2,1)S(1)}, u32[]{:S(2)}, u32[]{:S(2)}) collective-permute-start(bf16[288,512]{1,0:T(8,128)(2,1)} %bitcast.32), channel_id=1, source_target_pairs={{4,0},{6,2},{8,4},{10,6},{12,8},{14,10},{0,12},{2,14},{5,1},{7,3},... | collective-permute-start | bytes 884744 | tf_op jit(solution)/shard_map/ppermute | solution.py:224
  30.1 2.8 %collective-permute-start.2 = (bf16[288,512]{1,0:T(8,128)(2,1)}, bf16[288,512]{1,0:T(8,128)(2,1)S(1)}, u32[]{:S(2)}, u32[]{:S(2)}) collective-permute-start(bf16[288,512]{1,0:T(8,128)(2,1)} %bitcast.33), channel_id=1, source_target_pairs={{6,0},{8,2},{10,4},{12,6},{14,8},{0,10},{2,12},{4,14},{7,1},{9,3},... | collective-permute-start | bytes 884744 | tf_op jit(solution)/shard_map/ppermute | solution.py:224
  32.9 5.7 %collective-permute-start.3 = (bf16[288,512]{1,0:T(8,128)(2,1)}, bf16[288,512]{1,0:T(8,128)(2,1)S(1)}, u32[]{:S(2)}, u32[]{:S(2)}) collective-permute-start(bf16[288,512]{1,0:T(8,128)(2,1)} %bitcast.34), channel_id=1, source_target_pairs={{8,0},{10,2},{12,4},{14,6},{0,8},{2,10},{4,12},{6,14},{9,1},{11,3}... | collective-permute-start | bytes 884744 | tf_op jit(solution)/shard_map/ppermute | solution.py:224
  38.6 1.9 collective-permute-start.4
  40.5 1.0 bitcast_dynamic-update-slice_fusion.7
  41.5 4.8 %collective-permute-start.5 = (bf16[288,512]{1,0:T(8,128)(2,1)}, bf16[288,512]{1,0:T(8,128)(2,1)S(1)}, u32[]{:S(2)}, u32[]{:S(2)}) collective-permute-start(bf16[288,512]{1,0:T(8,128)(2,1)} %bitcast.37), channel_id=1, source_target_pairs={{12,0},{14,2},{0,4},{2,6},{4,8},{6,10},{8,12},{10,14},{13,1},{15,3... | collective-permute-start | bytes 884744 | tf_op jit(solution)/shard_map/ppermute | solution.py:224
  46.4 3.2 %collective-permute-start.6 = (bf16[288,512]{1,0:T(8,128)(2,1)S(1)}, bf16[288,512]{1,0:T(8,128)(2,1)S(1)}, u32[]{:S(2)}, u32[]{:S(2)}) collective-permute-start(bf16[288,512]{1,0:T(8,128)(2,1)S(1)} %bitcast.38), channel_id=1, source_target_pairs={{14,0},{0,2},{2,4},{4,6},{6,8},{8,10},{10,12},{12,14},{15,1},{1,3}... | collective-permute-start | bytes 884744 | tf_op jit(solution)/shard_map/ppermute | solution.py:224
  49.6 4.0 %collective-permute-done.2 = bf16[288,512]{1,0:T(8,128)(2,1)S(1)} collective-permute-done((bf16[288,512]{1,0:T(8,128)(2,1)}, bf16[288,512]{1,0:T(8,128)(2,1)S(1)}, u32[]{:S(2)}, u32[]{:S(2)}) %collective-permute-start.2) | collective-permute-done | bytes 294944 | tf_op jit(solution)/shard_map/ppermute | solution.py:224
  53.7 17.2 %collective-permute-done.4 = bf16[288,512]{1,0:T(8,128)(2,1)S(1)} collective-permute-done((bf16[288,512]{1,0:T(8,128)(2,1)}, bf16[288,512]{1,0:T(8,128)(2,1)S(1)}, u32[]{:S(2)}, u32[]{:S(2)}) %collective-permute-start.4) | collective-permute-done | bytes 294944 | tf_op jit(solution)/shard_map/ppermute | solution.py:224
  70.9 6.3 %collective-permute-done.5 = bf16[288,512]{1,0:T(8,128)(2,1)S(1)} collective-permute-done((bf16[288,512]{1,0:T(8,128)(2,1)}, bf16[288,512]{1,0:T(8,128)(2,1)S(1)}, u32[]{:S(2)}, u32[]{:S(2)}) %collective-permute-start.5) | collective-permute-done | bytes 294944 | tf_op jit(solution)/shard_map/ppermute | solution.py:224
  77.2 15.1 %collective-permute-done.6 = bf16[288,512]{1,0:T(8,128)(2,1)S(1)} collective-permute-done((bf16[288,512]{1,0:T(8,128)(2,1)S(1)}, bf16[288,512]{1,0:T(8,128)(2,1)S(1)}, u32[]{:S(2)}, u32[]{:S(2)}) %collective-permute-start.6) | collective-permute-done | bytes 294944 | tf_op jit(solution)/shard_map/ppermute | solution.py:224
  92.3 2.4 %collective-permute-start.7 = (bf16[8,288,512]{2,1,0:T(8,128)(2,1)S(1)}, bf16[8,288,512]{2,1,0:T(8,128)(2,1)}, u32[]{:S(2)}, u32[]{:S(2)}) collective-permute-start(bf16[8,288,512]{2,1,0:T(8,128)(2,1)S(1)} %bitcast_dynamic-update-slice_fusion.mine), channel_id=1, source_target_pairs={{1,0},{0,1},{3,2},{2,3},{5,4},{4,5},{7,6},{6,7},{9,8},{8,9},{11,10... | collective-permute-start | bytes 7077896 | tf_op jit(solution)/shard_map/ppermute | solution.py:225
  95.6 3.4 %collective-permute-done.7.other = bf16[8,288,512]{2,1,0:T(8,128)(2,1)} collective-permute-done((bf16[8,288,512]{2,1,0:T(8,128)(2,1)S(1)}, bf16[8,288,512]{2,1,0:T(8,128)(2,1)}, u32[]{:S(2)}, u32[]{:S(2)}) %collective-permute-start.7) | collective-permute-done | bytes 2359328 | tf_op jit(solution)/shard_map/ppermute | solution.py:225
  99.0 8.6 %arrange.1 = (bf16[4608,512]{1,0:T(8,128)(2,1)}, bf16[8,512,576]{2,1,0:T(8,128)(2,1)}, f32[2,256,256]{2,1,0:T(8,128)S(1)}) custom-call(s32[2]{0:T(128)S(1)} %pad_add_fusion.place, bf16[8,288,512]{2,1,0:T(8,128)(2,1)S(1)} %bitcast_dynamic-update-slice_fusion.mine, bf16[8,288,512]{2,1,0:T(8,128)(2,1)} %collective-permute-done.7.other), custom_call_target="tpu_custom_call" | custom-call | flops 1207959552 | bytes 14155776 | tf_op jit(solution)/shard_map/arrange/pallas_call | solution.py:70
  107.6 2.3 %copy-done = bf16[4608,512]{1,0:T(8,128)(2,1)S(1)} copy-done((bf16[4608,512]{1,0:T(8,128)(2,1)S(1)}, bf16[4608,512]{1,0:T(8,128)(2,1)}, u32[]{:S(2)}) %copy-start) | copy-done | bytes 4718616
  109.9 10.6 %attend.1 = (bf16[512,128]{1,0:T(8,128)(2,1)S(1)}, bf16[512,128]{1,0:T(8,128)(2,1)S(1)}, f32[4,128]{1,0:T(4,128)S(1)}) custom-call(s32[4]{0:T(128)S(1)} %pad_add_fusion.1.info, bf16[8,512,576]{2,1,0:T(8,128)(2,1)} %get-tuple-element.12.x_tok, bf16[4608,512]{1,0:T(8,128)(2,1)S(1)} %copy-done, bf16[512,256]{1,0:T(8,128)(2,1)S(1)} %copy-done.1, ...), custom_call_target="tpu_custom_call" | custom-call | flops 2818572288 | bytes 9437184 | tf_op jit(solution)/shard_map/attend/pallas_call | solution.py:152
  120.6 2.5 %psum.7 = f32[4,128]{1,0:T(4,128)S(1)} all-reduce(f32[4,128]{1,0:T(4,128)S(1)} %get-tuple-element.17), channel_id=1, replica_groups=mesh['z'=8,'x'=4,'y'=8,'core'=2] {'core'}, use_global_device_ids=true, to_apply=%region_0.0 | all-reduce | flops 512 | bytes 4096 | tf_op jit(solution)/shard_map/psum | solution.py:233
  123.1 9.2 %all_to_all.10.norms = f32[8,4,128]{2,1,0:T(4,128)S(1)} all-to-all(f32[8,4,128]{2,1,0:T(4,128)S(1)} %broadcast_in_dim.4), channel_id=1, replica_groups=mesh['z'=8,'x'=4,'y'=8,'core'=2] {'y'}, dimensions={0} | all-to-all | bytes 32768 | tf_op jit(solution)/shard_map/all_to_all | solution.py:234
  132.3 7.5 %gradient.1 = bf16[4608,256]{1,0:T(8,128)(2,1)} custom-call(bf16[4608,512]{1,0:T(8,128)(2,1)} %get-tuple-element.11.x_t, bf16[512,128]{1,0:T(8,128)(2,1)S(1)} %get-tuple-element.15.dk, bf16[512,128]{1,0:T(8,128)(2,1)S(1)} %get-tuple-element.16.dv, f32[8,4,128]{2,1,0:T(4,128)S(1)} %all_to_all.10.norms), custom_call_target="tpu_custom_call" | custom-call | flops 1207959552 | bytes 7077888 | tf_op jit(solution)/shard_map/gradient/pallas_call | solution.py:198
  139.8 11.2 %all-to-all-start.1 = ((bf16[32,144,256]{2,1,0:T(8,128)(2,1)}), bf16[32,144,256]{2,1,0:T(8,128)(2,1)S(1)}, u32[]{:S(2)}, u32[]{:S(2)}) async-start(bf16[32,144,256]{2,1,0:T(8,128)(2,1)} %bitcast.11), calls=%async_computation.1 | async-start | bytes 4718592 | tf_op jit(solution)/shard_map/all_to_all | solution.py:236
  151.9 52.3 %all-to-all-done.1 = bf16[32,144,256]{2,1,0:T(8,128)(2,1)S(1)} async-done(((bf16[32,144,256]{2,1,0:T(8,128)(2,1)}), bf16[32,144,256]{2,1,0:T(8,128)(2,1)S(1)}, u32[]{:S(2)}, u32[]{:S(2)}) %all-to-all-start.1) | async-done | bytes 2359328 | tf_op jit(solution)/shard_map/all_to_all | solution.py:236
  (34 shorter events, 2.3 us)
Async XLA Ops:
  7.2 39.2 %copy-start.3 = (bf16[512,288]{0,1:T(8,128)(2,1)S(1)}, bf16[512,288]{0,1:T(8,128)(2,1)}, u32[]{:S(2)}) copy-start(bf16[512,288]{0,1:T(8,128)(2,1)} %param.9) | copy-start | bytes 884740
  7.2 100.4 %all-gather.2.cloned.1.call-start = ((), (), s32[]{:S(2)}) async-start(), calls=%async_computation.2 | async-start | bytes 5308416 | tf_op jit(solution)/shard_map/all_gather | solution.py:222
  20.8 74.1 %copy-start.4 = (s32[2]{0:T(128)S(1)}, s32[2]{0:T(128)}, u32[]{:S(2)}) copy-start(s32[2]{0:T(128)} %param.15) | copy-start | bytes 28
  20.8 74.0 %copy-start.5 = (s32[2]{0:T(128)S(1)}, s32[2]{0:T(128)}, u32[]{:S(2)}) copy-start(s32[2]{0:T(128)} %param.14) | copy-start | bytes 28
  20.8 20.7 %collective-permute-start = (bf16[288,512]{1,0:T(8,128)(2,1)}, bf16[288,512]{1,0:T(8,128)(2,1)S(1)}, u32[]{:S(2)}, u32[]{:S(2)}) collective-permute-start(bf16[288,512]{1,0:T(8,128)(2,1)} %bitcast.31), channel_id=1, source_target_pairs={{2,0},{4,2},{6,4},{8,6},{10,8},{12,10},{14,12},{0,14},{3,1},{5,3},... | collective-permute-start | bytes 884744 | tf_op jit(solution)/shard_map/ppermute | solution.py:224
  26.4 20.0 %collective-permute-start.1 = (bf16[288,512]{1,0:T(8,128)(2,1)}, bf16[288,512]{1,0:T(8,128)(2,1)S(1)}, u32[]{:S(2)}, u32[]{:S(2)}) collective-permute-start(bf16[288,512]{1,0:T(8,128)(2,1)} %bitcast.32), channel_id=1, source_target_pairs={{4,0},{6,2},{8,4},{10,6},{12,8},{14,10},{0,12},{2,14},{5,1},{7,3},... | collective-permute-start | bytes 884744 | tf_op jit(solution)/shard_map/ppermute | solution.py:224
  30.1 23.5 %collective-permute-start.2 = (bf16[288,512]{1,0:T(8,128)(2,1)}, bf16[288,512]{1,0:T(8,128)(2,1)S(1)}, u32[]{:S(2)}, u32[]{:S(2)}) collective-permute-start(bf16[288,512]{1,0:T(8,128)(2,1)} %bitcast.33), channel_id=1, source_target_pairs={{6,0},{8,2},{10,4},{12,6},{14,8},{0,10},{2,12},{4,14},{7,1},{9,3},... | collective-permute-start | bytes 884744 | tf_op jit(solution)/shard_map/ppermute | solution.py:224
  32.9 20.7 %collective-permute-start.3 = (bf16[288,512]{1,0:T(8,128)(2,1)}, bf16[288,512]{1,0:T(8,128)(2,1)S(1)}, u32[]{:S(2)}, u32[]{:S(2)}) collective-permute-start(bf16[288,512]{1,0:T(8,128)(2,1)} %bitcast.34), channel_id=1, source_target_pairs={{8,0},{10,2},{12,4},{14,6},{0,8},{2,10},{4,12},{6,14},{9,1},{11,3}... | collective-permute-start | bytes 884744 | tf_op jit(solution)/shard_map/ppermute | solution.py:224
  38.6 32.3 %collective-permute-start.4 = (bf16[288,512]{1,0:T(8,128)(2,1)}, bf16[288,512]{1,0:T(8,128)(2,1)S(1)}, u32[]{:S(2)}, u32[]{:S(2)}) collective-permute-start(bf16[288,512]{1,0:T(8,128)(2,1)} %bitcast.35), channel_id=1, source_target_pairs={{10,0},{12,2},{14,4},{0,6},{2,8},{4,10},{6,12},{8,14},{11,1},{13,3... | collective-permute-start | bytes 884744 | tf_op jit(solution)/shard_map/ppermute | solution.py:224
  41.5 35.7 %collective-permute-start.5 = (bf16[288,512]{1,0:T(8,128)(2,1)}, bf16[288,512]{1,0:T(8,128)(2,1)S(1)}, u32[]{:S(2)}, u32[]{:S(2)}) collective-permute-start(bf16[288,512]{1,0:T(8,128)(2,1)} %bitcast.37), channel_id=1, source_target_pairs={{12,0},{14,2},{0,4},{2,6},{4,8},{6,10},{8,12},{10,14},{13,1},{15,3... | collective-permute-start | bytes 884744 | tf_op jit(solution)/shard_map/ppermute | solution.py:224
  46.4 45.9 %collective-permute-start.6 = (bf16[288,512]{1,0:T(8,128)(2,1)S(1)}, bf16[288,512]{1,0:T(8,128)(2,1)S(1)}, u32[]{:S(2)}, u32[]{:S(2)}) collective-permute-start(bf16[288,512]{1,0:T(8,128)(2,1)S(1)} %bitcast.38), channel_id=1, source_target_pairs={{14,0},{0,2},{2,4},{4,6},{6,8},{8,10},{10,12},{12,14},{15,1},{1,3}... | collective-permute-start | bytes 884744 | tf_op jit(solution)/shard_map/ppermute | solution.py:224
  92.3 6.7 %collective-permute-start.7 = (bf16[8,288,512]{2,1,0:T(8,128)(2,1)S(1)}, bf16[8,288,512]{2,1,0:T(8,128)(2,1)}, u32[]{:S(2)}, u32[]{:S(2)}) collective-permute-start(bf16[8,288,512]{2,1,0:T(8,128)(2,1)S(1)} %bitcast_dynamic-update-slice_fusion.mine), channel_id=1, source_target_pairs={{1,0},{0,1},{3,2},{2,3},{5,4},{4,5},{7,6},{6,7},{9,8},{8,9},{11,10... | collective-permute-start | bytes 7077896 | tf_op jit(solution)/shard_map/ppermute | solution.py:225
  95.5 12.1 %copy-start.1 = (bf16[512,256]{1,0:T(8,128)(2,1)S(1)}, bf16[512,256]{1,0:T(8,128)(2,1)}, u32[]{:S(2)}) copy-start(bf16[512,256]{1,0:T(8,128)(2,1)} %cot.1) | copy-start | bytes 786436
  107.6 2.3 %copy-start = (bf16[4608,512]{1,0:T(8,128)(2,1)S(1)}, bf16[4608,512]{1,0:T(8,128)(2,1)}, u32[]{:S(2)}) copy-start(bf16[4608,512]{1,0:T(8,128)(2,1)} %all-gather.2.cloned.1.call-done.w) | copy-start | bytes 14155780
  139.8 12.0 %copy-start.2 = (f32[4,2,144,128]{3,2,1,0:T(8,128)S(1)}, f32[4,2,144,128]{3,2,1,0:T(8,128)}, u32[]{:S(2)}) copy-start(f32[4,2,144,128]{3,2,1,0:T(8,128)} %param.17) | copy-start | bytes 1769476
  139.8 64.5 %all-to-all-start.1 = ((bf16[32,144,256]{2,1,0:T(8,128)(2,1)}), bf16[32,144,256]{2,1,0:T(8,128)(2,1)S(1)}, u32[]{:S(2)}, u32[]{:S(2)}) async-start(bf16[32,144,256]{2,1,0:T(8,128)(2,1)} %bitcast.11), calls=%async_computation.1 | async-start | bytes 4718592 | tf_op jit(solution)/shard_map/all_to_all | solution.py:236
Sparse Core Ops, SparseCore 0:
  20.9 70.2 all-gather.1

commit v2 on v1

v2 whole, which is shorter than its diff:
```python
import functools
import math

import jax
import jax.numpy as jnp
import numpy as np
from jax import lax
from jax.experimental import pallas as pl
from jax.experimental.pallas import tpu as pltpu
from jax.sharding import Mesh
from jax.sharding import PartitionSpec as P

D = 4608
H = 32
KV = 16
HD = 128
L = 256
NZ, NX, NY, NC = 8, 4, 8, 2
SHARD = D // (NY * NC)
PAIR = NC * SHARD
ROWS = D // (NZ * NX)
TOKENS = 2 * L
CAP = 50.0
SCALE = float(D // H) ** (-0.5)
CLIP = 2.0 * math.sqrt(D * KV * HD)
CHUNK = 2 * PAIR
FETCH = 768
VMEM = 32 * 1024 * 1024
VMEM_MOST = 54 * 1024 * 1024
F32 = jnp.float32
BF16 = jnp.bfloat16

NN = (((1,), (0,)), ((), ()))
NT = (((1,), (1,)), ((), ()))


def dot(a, b, dims=NN):
    return lax.dot_general(a, b, dims, preferred_element_type=F32)


def ring(n, k):
    return [((i + k) % n, i) for i in range(n)]


def rope_tables(length, dim):
    half = dim // 2
    freq = 10000.0 ** (-(jnp.arange(half, dtype=F32) * (2.0 / dim)))
    angle = jnp.arange(length, dtype=F32)[:, None] * freq[None, :]
    cosine = jnp.cos(angle)
    sine = jnp.sin(angle)
    return jnp.concatenate([cosine, cosine], 1), jnp.concatenate([-sine, sine], 1)


def arrange_kernel(place, mine, other, x_tok, gram, held, sems):
    first = place[1] == 0
    for m in range(NY // 2):
        columns = slice(m * CHUNK, (m + 1) * CHUNK)
        parts = []
        for half in range(2):
            at = lax.rem(2 * m + half + NY - place[0], NY)
            a = mine[at]
            b = other[at]
            parts += [jnp.where(first, a, b), jnp.where(first, b, a)]
        rows = jnp.concatenate(parts, 0).T
        held[:, columns] = rows
        pltpu.make_async_copy(held.at[:, columns], x_tok.at[:, columns], sems.at[m]).start()
        for s in range(2):
            part = rows[s * L : (s + 1) * L]
            product = dot(part, part, NT)
            gram[s] = product if m == 0 else gram[s] + product
    for m in range(NY // 2):
        columns = slice(m * CHUNK, (m + 1) * CHUNK)
        pltpu.make_async_copy(held.at[:, columns], x_tok.at[:, columns], sems.at[m]).wait()


def arrange(place, mine, other):
    vmem = pl.BlockSpec(memory_space=pltpu.VMEM)
    return pl.pallas_call(
        arrange_kernel,
        in_specs=[pl.BlockSpec(memory_space=pltpu.SMEM), vmem, vmem],
        out_specs=[pl.BlockSpec(memory_space=pl.ANY), vmem],
        out_shape=[
            jax.ShapeDtypeStruct((TOKENS, D), BF16),
            jax.ShapeDtypeStruct((2, L, L), F32),
        ],
        scratch_shapes=[
            pltpu.VMEM((TOKENS, D), BF16),
            pltpu.SemaphoreType.DMA((NY // 2,)),
        ],
        compiler_params=pltpu.CompilerParams(vmem_limit_bytes=VMEM_MOST),
        cost_estimate=pl.CostEstimate(
            flops=2 * 2 * L * L * D, bytes_accessed=2 * 2 * D * TOKENS, transcendentals=0
        ),
        name="arrange",
    )(place, mine, other)


def attend_kernel(
    info, x_tok, w, cot, cosine, sine, gram, grads, norms, x_held, w_held, acc, sems
):
    def fetch(m):
        part = pl.ds(m * FETCH, FETCH)
        return (
            pltpu.make_async_copy(x_tok.at[:, part], x_held.at[:, part], sems.at[0, m]),
            pltpu.make_async_copy(w.at[part], w_held.at[part], sems.at[1, m]),
        )

    for m in range(D // FETCH):
        for copy in fetch(m):
            copy.start()
    acc[...] = jnp.zeros_like(acc)

    for m in range(D // FETCH):
        for copy in fetch(m):
            copy.wait()
        part = pl.ds(m * FETCH, FETCH)
        acc[...] += dot(x_held[:, part], w_held[part])

    cos = cosine[...]
    sin = sine[...]
    key_at = lax.broadcasted_iota(jnp.int32, (L, L), 0)
    query_at = lax.broadcasted_iota(jnp.int32, (L, L), 1)
    row_at = lax.broadcasted_iota(jnp.int32, (L, HD), 0)

    def rotated(u):
        return (u * cos + pltpu.roll(u, HD // 2, 1) * sin).astype(BF16)

    for s in range(2):
        rows = slice(s * L, (s + 1) * L)
        length = info[s]
        valid = (row_at < length) & (info[2 + s] > 0)
        keep = (key_at <= query_at) & (key_at < length)
        key = rotated(acc[rows, 2 * HD : 3 * HD])
        value = acc[rows, 3 * HD : 4 * HD].astype(BF16)
        dv = jnp.zeros((L, HD), F32)
        dk_rot = jnp.zeros((L, HD), F32)
        for j in range(2):
            query = rotated(acc[rows, j * HD : (j + 1) * HD])
            grad = jnp.where(valid, cot[rows, j * HD : (j + 1) * HD], jnp.zeros((), BF16))
            bend = jnp.tanh(dot(key, query, NT) * (SCALE / CAP))
            weights = jnp.where(keep, jnp.exp(CAP * bend), 0.0)
            probs = weights * (1.0 / jnp.sum(weights, 0, keepdims=True))
            dv += dot(probs.astype(BF16), grad)
            grad_probs = dot(value, grad, NT)
            delta = jnp.sum(probs * grad_probs, 0, keepdims=True)
            ds = probs * (grad_probs - delta) * ((1.0 - bend * bend) * SCALE)
            dk_rot += dot(ds.astype(BF16), query)
        dk = (dk_rot * cos - pltpu.roll(dk_rot, HD // 2, 1) * sin).astype(BF16)
        dv = dv.astype(BF16)
        for i, d in enumerate((dk, dv)):
            grads[rows, i * HD : (i + 1) * HD] = d
            folded = jnp.sum(gram[s] * dot(d, d, NT), 0, keepdims=True)
            norms[2 * i + s : 2 * i + s + 1] = folded[:, :HD] + folded[:, HD:]


def attend(info, x_tok, w, cot, cosine, sine, gram):
    vmem = pl.BlockSpec(memory_space=pltpu.VMEM)
    return pl.pallas_call(
        attend_kernel,
        in_specs=[pl.BlockSpec(memory_space=pltpu.SMEM)]
        + [pl.BlockSpec(memory_space=pl.ANY)] * 2
        + [vmem] * 4,
        out_specs=[vmem] * 2,
        out_shape=[
            jax.ShapeDtypeStruct((TOKENS, 2 * HD), BF16),
            jax.ShapeDtypeStruct((4, HD), F32),
        ],
        scratch_shapes=[
            pltpu.VMEM((TOKENS, D), BF16),
            pltpu.VMEM((D, 4 * HD), BF16),
            pltpu.VMEM((TOKENS, 4 * HD), F32),
            pltpu.SemaphoreType.DMA((2, D // FETCH)),
        ],
        compiler_params=pltpu.CompilerParams(vmem_limit_bytes=VMEM_MOST),
        cost_estimate=pl.CostEstimate(
            flops=2 * TOKENS * 4 * HD * D + 4 * 12 * L * L * HD,
            bytes_accessed=4 * D * TOKENS,
            transcendentals=8 * L * L,
        ),
        name="attend",
    )(info, x_tok, w, cot, cosine, sine, gram)


def gradient_kernel(place, mine, other, grads, norms, out, scaled):
    for i in range(2):
        for s in range(2):
            total = jnp.sum(norms[:, 2 * i + s, :])
            factor = CLIP / jnp.maximum(jnp.sqrt(jnp.broadcast_to(total, (1, HD))), CLIP)
            rows = slice(s * L, (s + 1) * L)
            columns = slice(i * HD, (i + 1) * HD)
            scaled[rows, columns] = (factor * grads[rows, columns].astype(F32)).astype(BF16)

    @pl.loop(0, NY, unroll=NY)
    def _(k):
        at = lax.rem(place[0] + k, NY)
        for held, core in ((mine, place[1]), (other, 1 - place[1])):
            part = dot(held[k], scaled[...]).astype(BF16)
            out[2 * core, at] = part[:ROWS]
            out[2 * core + 1, at] = part[ROWS:]


def gradient(place, mine, other, grads, norms):
    vmem = pl.BlockSpec(memory_space=pltpu.VMEM)
    return pl.pallas_call(
        gradient_kernel,
        in_specs=[pl.BlockSpec(memory_space=pltpu.SMEM)] + [vmem] * 4,
        out_specs=vmem,
        out_shape=jax.ShapeDtypeStruct((NX, NZ, ROWS, 2 * HD), BF16),
        scratch_shapes=[pltpu.VMEM((TOKENS, 2 * HD), BF16)],
        compiler_params=pltpu.CompilerParams(vmem_limit_bytes=VMEM),
        cost_estimate=pl.CostEstimate(
            flops=2 * D * TOKENS * 2 * HD, bytes_accessed=3 * D * TOKENS, transcendentals=0
        ),
        name="gradient",
    )(place, mine, other, grads, norms)


def gather_y(shard):
    hop = lambda a, k: lax.ppermute(a, "y", ring(NY, k))
    up, down = [shard], [shard]
    for _ in range(3):
        up.append(hop(up[-1], 1))
        down.append(hop(down[-1], 7))
    return jnp.stack(up + [hop(up[-1], 1)] + down[:0:-1])


def reduce_rows(terms):
    terms = lax.all_to_all(terms, "x", 0, 0)
    terms = jnp.sum(terms.astype(F32), 0).astype(BF16)
    terms = lax.all_to_all(terms, "z", 0, 0)
    return jnp.sum(terms.astype(F32), 0)


def body(inputs, w_query, w_key, w_value, cotangent, lengths, sampled, step, tree_noise):
    w = jnp.concatenate([w_query, w_key, w_value], 1)
    w = lax.all_gather(w, "x", axis=0, tiled=True)
    w, shard = lax.optimization_barrier((w, inputs.T))
    w = lax.all_gather(w, "z", axis=0, tiled=True)

    mine = gather_y(shard)
    other = lax.ppermute(mine, "core", ring(NC, 1))
    place = jnp.stack([lax.axis_index("y"), lax.axis_index("core")]).astype(jnp.int32)
    x_tok, gram = arrange(place, mine, other)

    cosine, sine = rope_tables(L, HD)
    grads, norms = attend(
        jnp.concatenate([lengths, sampled]), x_tok, w, cotangent, cosine, sine, gram
    )
    norms = lax.psum(norms, "core")
    norms = lax.all_to_all(jnp.broadcast_to(norms, (NY, 4, HD)), "y", 0, 0)
    terms = gradient(place, mine, other, grads, norms)
    summed = reduce_rows(terms)

    levels = tree_noise.shape[0]
    bits = (step[0] // 2 ** jnp.arange(levels, dtype=jnp.int32) % 2).astype(F32)
    noise = jnp.sum(bits[:, None, None, None] * tree_noise, 0)
    expected = 0.85 * (2 * NZ * NX)
    return summed[:, :HD] / expected + noise[0], summed[:, HD:] / expected + noise[1]


def solution(mesh):
    mesh = Mesh(np.asarray(mesh.devices).reshape(NZ, NX, NY, NC), ("z", "x", "y", "core"))
    dp, head = ("z", "x"), ("y", "core")
    in_specs = (
        P(dp, head),
        P(dp, head),
        P(dp, head),
        P(dp, head),
        P(dp, head),
        P(dp),
        P(dp),
        P(),
        P(None, None, dp, head),
    )
    out_specs = (P(dp, head), P(dp, head))
    return jax.shard_map(body, mesh=mesh, in_specs=in_specs, out_specs=out_specs, check_vma=False)
```

time: 216 us -> 181 us (0.84); the launches traced: 212 us -> 179 us
  waiting for transfers between devices: 98.3 us -> 41.2 us
  blocking collectives: 24.2 us -> 58.9 us
  Pallas kernels: 26.8 us -> 17.6 us
  other arithmetic: 3.04 us -> 5.76 us
  starting transfers between devices: 41.4 us -> 38.8 us
    all_to_all x1, waiting for transfers between devices: 52.3 us -> 15.3 us  [reduce_rows(): terms = lax.all_to_all(terms, 'z', 0, 0)]
    all_to_all x0 -> x1, blocking collectives: none -> 30.6 us  [reduce_rows(): terms = lax.all_to_all(terms, 'x', 0, 0)]
    ppermute x7, waiting for transfers between devices: 42.6 us -> 16.3 us  [gather_y(): hop = lambda a, k: lax.ppermute(a, 'y', ring(NY, k))]
    ppermute x1, starting transfers between devices: 2.4 us -> 11.9 us  [body(): other = lax.ppermute(mine, 'core', ring(NC, 1))]
    pallas_call x3, Pallas kernels: 26.8 us -> 17.6 us  [the longest x1 8.52 us: attend(): pl.pallas_call(attend_kernel, in_specs=[pl.BlockSpec(memory_space=pltpu.S...]
    all_gather x1, waiting for transfers between devices: 0.01 us -> 7.77 us  [body(): w = lax.all_gather(w, 'z', axis=0, tiled=True)]
    all_to_all x1, starting transfers between devices: 11.2 us -> 3.85 us  [reduce_rows(): terms = lax.all_to_all(terms, 'z', 0, 0)]
    ppermute x7, starting transfers between devices: 27.7 us -> 23 us  [gather_y(): hop = lambda a, k: lax.ppermute(a, 'y', ring(NY, k))]
  transfers between devices with their start and end apart: 10 -> 10, of which waited for: 6 -> 7; matrix products, arithmetic and copies ran while one was open for 1% -> 2% of each run, Pallas kernels for 4% -> 3%
where the time goes in v2:
time: 181 us; the launch traced here: 179 us
  blocking collectives  58.9 us (33%)
  waiting for transfers between devices  41.2 us (23%)
  starting transfers between devices  38.8 us (21%)
  Pallas kernels  17.6 us (10%)
  between operations  14.9 us (8%)
  other arithmetic  5.76 us (3%)
  local copies, waits for them, and re-layouts  2.12 us (1%)
    all_to_all x1, blocking collectives, reduce_rows(): terms = lax.all_to_all(terms, 'x', 0, 0)  30.6 us
    ppermute x7, starting transfers between devices, gather_y(): hop = lambda a, k: lax.ppermute(a, 'y', ring(NY, k))  23 us
    ppermute x7, waiting for transfers between devices, gather_y(): hop = lambda a, k: lax.ppermute(a, 'y', ring(NY, k))  16.3 us
    all_to_all x1, waiting for transfers between devices, reduce_rows(): terms = lax.all_to_all(terms, 'z', 0, 0)  15.3 us
    all_to_all x1, blocking collectives, body(): norms = lax.all_to_all(jnp.broadcast_to(norms, (NY, 4, HD)), 'y', 0, 0)  12.9 us
    all_gather x1, blocking collectives, body(): w = lax.all_gather(w, 'x', axis=0, tiled=True)  12.5 us
    ppermute x1, starting transfers between devices, body(): other = lax.ppermute(mine, 'core', ring(NC, 1))  11.9 us
    pallas_call x1, Pallas kernels, attend(): pl.pallas_call(attend_kernel, in_specs=[pl.BlockSpec(memory_space=pltpu.S...  8.52 us
  transfers between devices with their start and end apart: 10, of which 7 were waited for; matrix products, arithmetic and copies ran while one was open for 2% of the time, Pallas kernels for 3%

profile of v2, /device:TPU:1, one launch (start us, length us, event | category | flops | bytes accessed | tf_op | source)
XLA Modules:
  0.0 179.3 jit_solution(10600868126108328204)
XLA Ops:
  8.2 12.5 %all_gather.6 = bf16[576,512]{1,0:T(8,128)(2,1)} all-gather(bf16[144,512]{1,0:T(8,128)(2,1)S(1)} %pad_maximum_fusion), channel_id=1, replica_groups=mesh['z'=8,'x'=4,'y'=8,'core'=2] {'x'}, dimensions={0}, use_global_device_ids=true | all-gather | bytes 737280 | tf_op jit(solution)/shard_map/all_gather | solution.py:236
  20.7 5.6 %collective-permute-start = (bf16[288,512]{1,0:T(8,128)(2,1)}, bf16[288,512]{1,0:T(8,128)(2,1)S(1)}, u32[]{:S(2)}, u32[]{:S(2)}) collective-permute-start(bf16[288,512]{1,0:T(8,128)(2,1)} %bitcast.30), channel_id=1, source_target_pairs={{2,0},{4,2},{6,4},{8,6},{10,8},{12,10},{14,12},{0,14},{3,1},{5,3},... | collective-permute-start | bytes 884744 | tf_op jit(solution)/shard_map/ppermute | solution.py:219
  26.3 1.9 %collective-permute-start.4 = (bf16[288,512]{1,0:T(8,128)(2,1)}, bf16[288,512]{1,0:T(8,128)(2,1)S(1)}, u32[]{:S(2)}, u32[]{:S(2)}) collective-permute-start(bf16[288,512]{1,0:T(8,128)(2,1)} %bitcast.31), channel_id=1, source_target_pairs={{14,0},{0,2},{2,4},{4,6},{6,8},{8,10},{10,12},{12,14},{15,1},{1,3}... | collective-permute-start | bytes 884744 | tf_op jit(solution)/shard_map/ppermute | solution.py:219
  28.2 2.0 %collective-permute-done = bf16[288,512]{1,0:T(8,128)(2,1)S(1)} collective-permute-done((bf16[288,512]{1,0:T(8,128)(2,1)}, bf16[288,512]{1,0:T(8,128)(2,1)S(1)}, u32[]{:S(2)}, u32[]{:S(2)}) %collective-permute-start) | collective-permute-done | bytes 294944 | tf_op jit(solution)/shard_map/ppermute | solution.py:219
  30.3 4.9 %collective-permute-start.1 = (bf16[288,512]{1,0:T(8,128)(2,1)S(1)}, bf16[288,512]{1,0:T(8,128)(2,1)S(1)}, u32[]{:S(2)}, u32[]{:S(2)}) collective-permute-start(bf16[288,512]{1,0:T(8,128)(2,1)S(1)} %collective-permute-done), channel_id=1, source_target_pairs={{2,0},{4,2},{6,4},{8,6},{10,8},{12,10},{14,12},{0,14},{3,1},{5,3},... | collective-permute-start | bytes 884744 | tf_op jit(solution)/shard_map/ppermute | solution.py:219
  35.2 1.9 %collective-permute-start.5 = (bf16[288,512]{1,0:T(8,128)(2,1)S(1)}, bf16[288,512]{1,0:T(8,128)(2,1)S(1)}, u32[]{:S(2)}, u32[]{:S(2)}) collective-permute-start(bf16[288,512]{1,0:T(8,128)(2,1)S(1)} %collective-permute-done.4), channel_id=1, source_target_pairs={{14,0},{0,2},{2,4},{4,6},{6,8},{8,10},{10,12},{12,14},{15,1},{1,3}... | collective-permute-start | bytes 884744 | tf_op jit(solution)/shard_map/ppermute | solution.py:219
  37.1 3.4 %collective-permute-done.1 = bf16[288,512]{1,0:T(8,128)(2,1)S(1)} collective-permute-done((bf16[288,512]{1,0:T(8,128)(2,1)S(1)}, bf16[288,512]{1,0:T(8,128)(2,1)S(1)}, u32[]{:S(2)}, u32[]{:S(2)}) %collective-permute-start.1) | collective-permute-done | bytes 294944 | tf_op jit(solution)/shard_map/ppermute | solution.py:219
  40.5 3.3 %collective-permute-start.2 = (bf16[288,512]{1,0:T(8,128)(2,1)S(1)}, bf16[288,512]{1,0:T(8,128)(2,1)S(1)}, u32[]{:S(2)}, u32[]{:S(2)}) collective-permute-start(bf16[288,512]{1,0:T(8,128)(2,1)S(1)} %collective-permute-done.1), channel_id=1, source_target_pairs={{2,0},{4,2},{6,4},{8,6},{10,8},{12,10},{14,12},{0,14},{3,1},{5,3},... | collective-permute-start | bytes 884744 | tf_op jit(solution)/shard_map/ppermute | solution.py:219
  44.9 2.0 %collective-permute-start.6 = (bf16[288,512]{1,0:T(8,128)(2,1)S(1)}, bf16[288,512]{1,0:T(8,128)(2,1)S(1)}, u32[]{:S(2)}, u32[]{:S(2)}) collective-permute-start(bf16[288,512]{1,0:T(8,128)(2,1)S(1)} %collective-permute-done.5), channel_id=1, source_target_pairs={{14,0},{0,2},{2,4},{4,6},{6,8},{8,10},{10,12},{12,14},{15,1},{1,3}... | collective-permute-start | bytes 884744 | tf_op jit(solution)/shard_map/ppermute | solution.py:219
  46.9 4.4 %collective-permute-done.2 = bf16[288,512]{1,0:T(8,128)(2,1)S(1)} collective-permute-done((bf16[288,512]{1,0:T(8,128)(2,1)S(1)}, bf16[288,512]{1,0:T(8,128)(2,1)S(1)}, u32[]{:S(2)}, u32[]{:S(2)}) %collective-permute-start.2) | collective-permute-done | bytes 294944 | tf_op jit(solution)/shard_map/ppermute | solution.py:219
  51.3 3.4 %collective-permute-start.3 = (bf16[288,512]{1,0:T(8,128)(2,1)S(1)}, bf16[288,512]{1,0:T(8,128)(2,1)S(1)}, u32[]{:S(2)}, u32[]{:S(2)}) collective-permute-start(bf16[288,512]{1,0:T(8,128)(2,1)S(1)} %collective-permute-done.2), channel_id=1, source_target_pairs={{2,0},{4,2},{6,4},{8,6},{10,8},{12,10},{14,12},{0,14},{3,1},{5,3},... | collective-permute-start | bytes 884744 | tf_op jit(solution)/shard_map/ppermute | solution.py:219
  54.8 6.4 %collective-permute-done.3 = bf16[288,512]{1,0:T(8,128)(2,1)S(1)} collective-permute-done((bf16[288,512]{1,0:T(8,128)(2,1)S(1)}, bf16[288,512]{1,0:T(8,128)(2,1)S(1)}, u32[]{:S(2)}, u32[]{:S(2)}) %collective-permute-start.3) | collective-permute-done | bytes 294944 | tf_op jit(solution)/shard_map/ppermute | solution.py:219
  61.3 11.9 %collective-permute-start.7 = (bf16[8,288,512]{2,1,0:T(8,128)(2,1)S(1)}, bf16[8,288,512]{2,1,0:T(8,128)(2,1)}, u32[]{:S(2)}, u32[]{:S(2)}) collective-permute-start(bf16[8,288,512]{2,1,0:T(8,128)(2,1)S(1)} %bitcast_dynamic-update-slice_fusion.mine), channel_id=1, source_target_pairs={{1,0},{0,1},{3,2},{2,3},{5,4},{4,5},{7,6},{6,7},{9,8},{8,9},{11,10... | collective-permute-start | bytes 7077896 | tf_op jit(solution)/shard_map/ppermute | solution.py:241
  75.7 1.7 collective-permute-done.7.other
  77.5 5.9 %arrange.1 = (bf16[512,4608]{1,0:T(8,128)(2,1)}, f32[2,256,256]{2,1,0:T(8,128)}) custom-call(s32[2]{0:T(128)} %pad_add_fusion.place, bf16[8,288,512]{2,1,0:T(8,128)(2,1)} %copy-done, bf16[8,288,512]{2,1,0:T(8,128)(2,1)} %collective-permute-done.7.other), custom_call_target="tpu_custom_call" | custom-call | flops 1207959552 | bytes 9437184 | tf_op jit(solution)/shard_map/arrange/pallas_call | solution.py:78
  83.4 7.8 %all-gather.2.cloned.1.call-done.w = bf16[4608,512]{1,0:T(8,128)(2,1)} async-done(((bf16[576,512]{1,0:T(8,128)(2,1)}), bf16[4608,512]{1,0:T(8,128)(2,1)}) %all-gather.2.cloned.1.call-update) | async-done | bytes 4718608 | tf_op jit(solution)/shard_map/all_gather | solution.py:238
  91.2 8.5 %attend.1 = (bf16[512,256]{1,0:T(8,128)(2,1)}, f32[4,128]{1,0:T(4,128)}) custom-call(s32[4]{0:T(128)} %pad_add_fusion.1.info, bf16[512,4608]{1,0:T(8,128)(2,1)} %get-tuple-element.9.x_tok, bf16[4608,512]{1,0:T(8,128)(2,1)} %all-gather.2.cloned.1.call-done.w, bf16[512,256]{1,0:T(8,128)(2,1)} %cot.1, f32[256,128]{1,0:T(8,128)} %get-tuple-element.19.cosine, ...), custom_call_target="tpu_custom_call" | custom-call | flops 2818572288 | bytes 9437184 | tf_op jit(solution)/shard_map/attend/pallas_call | solution.py:158
  99.7 2.9 %psum.7 = f32[4,128]{1,0:T(4,128)S(1)} all-reduce(f32[4,128]{1,0:T(4,128)} %get-tuple-element.13), channel_id=1, replica_groups=mesh['z'=8,'x'=4,'y'=8,'core'=2] {'core'}, use_global_device_ids=true, to_apply=%region_0.0 | all-reduce | flops 512 | bytes 4096 | tf_op jit(solution)/shard_map/psum | solution.py:249
  102.6 12.9 %all_to_all.15.norms = f32[8,4,128]{2,1,0:T(4,128)S(1)} all-to-all(f32[8,4,128]{2,1,0:T(4,128)S(1)} %broadcast_in_dim.4), channel_id=1, replica_groups=mesh['z'=8,'x'=4,'y'=8,'core'=2] {'y'}, dimensions={0} | all-to-all | bytes 32768 | tf_op jit(solution)/shard_map/all_to_all | solution.py:250
  116.5 3.2 %gradient.1 = bf16[4,8,144,256]{3,2,1,0:T(8,128)(2,1)S(1)} custom-call(s32[2]{0:T(128)S(1)} %copy-done.3, bf16[8,288,512]{2,1,0:T(8,128)(2,1)S(1)} %copy-done.1, bf16[8,288,512]{2,1,0:T(8,128)(2,1)} %collective-permute-done.7.other, bf16[512,256]{1,0:T(8,128)(2,1)S(1)} %copy-done.2, f32[8,4,128]{2,1,0:T(4,128)S(1)} %all_to_all.15.norms), custom_call_target="tpu_custom_call" | custom-call | flops 1207959552 | bytes 7077888 | tf_op jit(solution)/shard_map/gradient/pallas_call | solution.py:204
  119.7 30.6 %all_to_all.16 = bf16[4,8,144,256]{3,2,1,0:T(8,128)(2,1)S(1)} all-to-all(bf16[4,8,144,256]{3,2,1,0:T(8,128)(2,1)S(1)} %gradient.1), channel_id=1, replica_groups=mesh['z'=8,'x'=4,'y'=8,'core'=2] {'x'}, dimensions={0} | all-to-all | bytes 4718592 | tf_op jit(solution)/shard_map/all_to_all | solution.py:228
  150.3 1.3 reduce_sum.30
  151.6 3.9 %all-to-all-start.2 = ((bf16[8,144,256]{2,1,0:T(8,128)(2,1)}), bf16[8,144,256]{2,1,0:T(8,128)(2,1)S(1)}, u32[]{:S(2)}, u32[]{:S(2)}) async-start(bf16[8,144,256]{2,1,0:T(8,128)(2,1)} %reduce_sum.30), calls=%async_computation.2 | async-start | bytes 1179648 | tf_op jit(solution)/shard_map/all_to_all | solution.py:230
  156.4 15.3 %all-to-all-done.2 = bf16[8,144,256]{2,1,0:T(8,128)(2,1)S(1)} async-done(((bf16[8,144,256]{2,1,0:T(8,128)(2,1)}), bf16[8,144,256]{2,1,0:T(8,128)(2,1)S(1)}, u32[]{:S(2)}, u32[]{:S(2)}) %all-to-all-start.2) | async-done | bytes 589856 | tf_op jit(solution)/shard_map/all_to_all | solution.py:230
  (38 shorter events, 6.6 us)
Async XLA Ops:
  7.2 84.0 %all-gather.2.cloned.1.call-start = ((), (), s32[]{:S(2)}) async-start(), calls=%async_computation.3 | async-start | bytes 5308416 | tf_op jit(solution)/shard_map/all_gather | solution.py:238
  20.7 53.1 %copy-start.5 = (s32[2]{0:T(128)S(1)}, s32[2]{0:T(128)}, u32[]{:S(2)}) copy-start(s32[2]{0:T(128)} %param.15) | copy-start | bytes 28
  20.7 53.1 %copy-start.6 = (s32[2]{0:T(128)S(1)}, s32[2]{0:T(128)}, u32[]{:S(2)}) copy-start(s32[2]{0:T(128)} %param.14) | copy-start | bytes 28
  20.7 9.5 %collective-permute-start = (bf16[288,512]{1,0:T(8,128)(2,1)}, bf16[288,512]{1,0:T(8,128)(2,1)S(1)}, u32[]{:S(2)}, u32[]{:S(2)}) collective-permute-start(bf16[288,512]{1,0:T(8,128)(2,1)} %bitcast.30), channel_id=1, source_target_pairs={{2,0},{4,2},{6,4},{8,6},{10,8},{12,10},{14,12},{0,14},{3,1},{5,3},... | collective-permute-start | bytes 884744 | tf_op jit(solution)/shard_map/ppermute | solution.py:219
  26.3 8.9 %collective-permute-start.4 = (bf16[288,512]{1,0:T(8,128)(2,1)}, bf16[288,512]{1,0:T(8,128)(2,1)S(1)}, u32[]{:S(2)}, u32[]{:S(2)}) collective-permute-start(bf16[288,512]{1,0:T(8,128)(2,1)} %bitcast.31), channel_id=1, source_target_pairs={{14,0},{0,2},{2,4},{4,6},{6,8},{8,10},{10,12},{12,14},{15,1},{1,3}... | collective-permute-start | bytes 884744 | tf_op jit(solution)/shard_map/ppermute | solution.py:219
  30.3 10.3 %collective-permute-start.1 = (bf16[288,512]{1,0:T(8,128)(2,1)S(1)}, bf16[288,512]{1,0:T(8,128)(2,1)S(1)}, u32[]{:S(2)}, u32[]{:S(2)}) collective-permute-start(bf16[288,512]{1,0:T(8,128)(2,1)S(1)} %collective-permute-done), channel_id=1, source_target_pairs={{2,0},{4,2},{6,4},{8,6},{10,8},{12,10},{14,12},{0,14},{3,1},{5,3},... | collective-permute-start | bytes 884744 | tf_op jit(solution)/shard_map/ppermute | solution.py:219
  35.2 9.7 %collective-permute-start.5 = (bf16[288,512]{1,0:T(8,128)(2,1)S(1)}, bf16[288,512]{1,0:T(8,128)(2,1)S(1)}, u32[]{:S(2)}, u32[]{:S(2)}) collective-permute-start(bf16[288,512]{1,0:T(8,128)(2,1)S(1)} %collective-permute-done.4), channel_id=1, source_target_pairs={{14,0},{0,2},{2,4},{4,6},{6,8},{8,10},{10,12},{12,14},{15,1},{1,3}... | collective-permute-start | bytes 884744 | tf_op jit(solution)/shard_map/ppermute | solution.py:219
  40.5 10.7 %collective-permute-start.2 = (bf16[288,512]{1,0:T(8,128)(2,1)S(1)}, bf16[288,512]{1,0:T(8,128)(2,1)S(1)}, u32[]{:S(2)}, u32[]{:S(2)}) collective-permute-start(bf16[288,512]{1,0:T(8,128)(2,1)S(1)} %collective-permute-done.1), channel_id=1, source_target_pairs={{2,0},{4,2},{6,4},{8,6},{10,8},{12,10},{14,12},{0,14},{3,1},{5,3},... | collective-permute-start | bytes 884744 | tf_op jit(solution)/shard_map/ppermute | solution.py:219
  44.9 16.3 %collective-permute-start.6 = (bf16[288,512]{1,0:T(8,128)(2,1)S(1)}, bf16[288,512]{1,0:T(8,128)(2,1)S(1)}, u32[]{:S(2)}, u32[]{:S(2)}) collective-permute-start(bf16[288,512]{1,0:T(8,128)(2,1)S(1)} %collective-permute-done.5), channel_id=1, source_target_pairs={{14,0},{0,2},{2,4},{4,6},{6,8},{8,10},{10,12},{12,14},{15,1},{1,3}... | collective-permute-start | bytes 884744 | tf_op jit(solution)/shard_map/ppermute | solution.py:219
  51.3 10.0 %collective-permute-start.3 = (bf16[288,512]{1,0:T(8,128)(2,1)S(1)}, bf16[288,512]{1,0:T(8,128)(2,1)S(1)}, u32[]{:S(2)}, u32[]{:S(2)}) collective-permute-start(bf16[288,512]{1,0:T(8,128)(2,1)S(1)} %collective-permute-done.2), channel_id=1, source_target_pairs={{2,0},{4,2},{6,4},{8,6},{10,8},{12,10},{14,12},{0,14},{3,1},{5,3},... | collective-permute-start | bytes 884744 | tf_op jit(solution)/shard_map/ppermute | solution.py:219
  61.3 16.2 %copy-start = (bf16[8,288,512]{2,1,0:T(8,128)(2,1)}, bf16[8,288,512]{2,1,0:T(8,128)(2,1)S(1)}, u32[]{:S(2)}) copy-start(bf16[8,288,512]{2,1,0:T(8,128)(2,1)S(1)} %bitcast_dynamic-update-slice_fusion.mine) | copy-start | bytes 7077892
  61.3 16.1 %collective-permute-start.7 = (bf16[8,288,512]{2,1,0:T(8,128)(2,1)S(1)}, bf16[8,288,512]{2,1,0:T(8,128)(2,1)}, u32[]{:S(2)}, u32[]{:S(2)}) collective-permute-start(bf16[8,288,512]{2,1,0:T(8,128)(2,1)S(1)} %bitcast_dynamic-update-slice_fusion.mine), channel_id=1, source_target_pairs={{1,0},{0,1},{3,2},{2,3},{5,4},{4,5},{7,6},{6,7},{9,8},{8,9},{11,10... | collective-permute-start | bytes 7077896 | tf_op jit(solution)/shard_map/ppermute | solution.py:241
  91.2 24.4 %copy-start.1 = (bf16[8,288,512]{2,1,0:T(8,128)(2,1)S(1)}, bf16[8,288,512]{2,1,0:T(8,128)(2,1)}, u32[]{:S(2)}) copy-start(bf16[8,288,512]{2,1,0:T(8,128)(2,1)} %copy-done) | copy-start | bytes 7077892
  91.2 24.4 %copy-start.3 = (s32[2]{0:T(128)S(1)}, s32[2]{0:T(128)}, u32[]{:S(2)}) copy-start(s32[2]{0:T(128)} %pad_add_fusion.place) | copy-start | bytes 28
  115.5 1.0 copy-start.2
  150.3 6.0 %copy-start.4 = (f32[4,2,144,128]{3,2,1,0:T(8,128)S(1)}, f32[4,2,144,128]{3,2,1,0:T(8,128)}, u32[]{:S(2)}) copy-start(f32[4,2,144,128]{3,2,1,0:T(8,128)} %param.17) | copy-start | bytes 1769476
  151.6 20.1 %all-to-all-start.2 = ((bf16[8,144,256]{2,1,0:T(8,128)(2,1)}), bf16[8,144,256]{2,1,0:T(8,128)(2,1)S(1)}, u32[]{:S(2)}, u32[]{:S(2)}) async-start(bf16[8,144,256]{2,1,0:T(8,128)(2,1)} %reduce_sum.30), calls=%async_computation.2 | async-start | bytes 1179648 | tf_op jit(solution)/shard_map/all_to_all | solution.py:230
Sparse Core Ops, SparseCore 0:
  20.8 70.2 all-gather.1

commit v3 on v2

v3 whole, which is shorter than its diff:
```python
import functools
import math

import jax
import jax.numpy as jnp
import numpy as np
from jax import lax
from jax.experimental import pallas as pl
from jax.experimental.pallas import tpu as pltpu
from jax.sharding import Mesh
from jax.sharding import PartitionSpec as P

D = 4608
H = 32
KV = 16
HD = 128
L = 256
NZ, NX, NY, NC = 8, 4, 8, 2
SHARD = D // (NY * NC)
PAIR = NC * SHARD
ROWS = D // (NZ * NX)
TOKENS = 2 * L
CAP = 50.0
SCALE = float(D // H) ** (-0.5)
CLIP = 2.0 * math.sqrt(D * KV * HD)
CHUNK = 2 * PAIR
VMEM = 32 * 1024 * 1024
VMEM_ATTEND = 52 * 1024 * 1024
VMEM_MOST = 58 * 1024 * 1024
F32 = jnp.float32
BF16 = jnp.bfloat16

NN = (((1,), (0,)), ((), ()))
NT = (((1,), (1,)), ((), ()))


def dot(a, b, dims=NN):
    return lax.dot_general(a, b, dims, preferred_element_type=F32)


def ring(n, k):
    return [((i + k) % n, i) for i in range(n)]


def rope_tables(length, dim):
    half = dim // 2
    freq = 10000.0 ** (-(jnp.arange(half, dtype=F32) * (2.0 / dim)))
    angle = jnp.arange(length, dtype=F32)[:, None] * freq[None, :]
    cosine = jnp.cos(angle)
    sine = jnp.sin(angle)
    return jnp.concatenate([cosine, cosine], 1), jnp.concatenate([-sine, sine], 1)


def gram_kernel(place, mine, other, gram, own):
    x = place[2]
    half = pl.ds(pl.multiple_of(lax.rem(x, 2) * ROWS, ROWS), ROWS)
    here = x // 2 == place[1]
    for m in range(NY // 2):
        for k in (2 * m, 2 * m + 1):
            own[lax.rem(place[0] + k, NY)] = jnp.where(here, mine[k, half], other[k, half])
        parts = [mine[2 * m], other[2 * m], mine[2 * m + 1], other[2 * m + 1]]
        rows = jnp.concatenate(parts, 0).T
        for s in range(2):
            part = rows[s * L : (s + 1) * L]
            product = dot(part, part, NT)
            gram[s] = product if m == 0 else gram[s] + product


def gram_of(place, mine, other):
    vmem = pl.BlockSpec(memory_space=pltpu.VMEM)
    return pl.pallas_call(
        gram_kernel,
        in_specs=[pl.BlockSpec(memory_space=pltpu.SMEM)] + [vmem] * 2,
        out_specs=[vmem] * 2,
        out_shape=[
            jax.ShapeDtypeStruct((2, L, L), F32),
            jax.ShapeDtypeStruct((NZ, ROWS, TOKENS), BF16),
        ],
        compiler_params=pltpu.CompilerParams(vmem_limit_bytes=VMEM),
        cost_estimate=pl.CostEstimate(
            flops=2 * 2 * L * L * D, bytes_accessed=2 * D * TOKENS, transcendentals=0
        ),
        name="gram",
    )(place, mine, other)


def attend_kernel(
    info, place, mine, other, w, cot, cosine, sine, gram, grads, norms, x_tok, held, acc, sems
):
    def fetch(m):
        part = pl.ds(m * CHUNK, CHUNK)
        return pltpu.make_async_copy(w.at[part], held.at[part], sems.at[m])

    for m in range(NY // 2):
        fetch(m).start()
    first = place[1] == 0
    for m in range(NY // 2):
        parts = []
        for half in range(2):
            at = lax.rem(2 * m + half + NY - place[0], NY)
            a, b = mine[at], other[at]
            parts += [jnp.where(first, a, b), jnp.where(first, b, a)]
        x_tok[:, m * CHUNK : (m + 1) * CHUNK] = jnp.concatenate(parts, 0).T
    for m in range(NY // 2):
        fetch(m).wait()
        part = slice(m * CHUNK, (m + 1) * CHUNK)
        product = dot(x_tok[:, part], held[part])
        acc[...] = product if m == 0 else acc[...] + product

    cos = cosine[...]
    sin = sine[...]
    key_at = lax.broadcasted_iota(jnp.int32, (L, L), 0)
    query_at = lax.broadcasted_iota(jnp.int32, (L, L), 1)
    row_at = lax.broadcasted_iota(jnp.int32, (L, HD), 0)

    def rotated(u):
        return (u * cos + pltpu.roll(u, HD // 2, 1) * sin).astype(BF16)

    for s in range(2):
        rows = slice(s * L, (s + 1) * L)
        length = info[s]
        valid = (row_at < length) & (info[2 + s] > 0)
        keep = (key_at <= query_at) & (key_at < length)
        key = rotated(acc[rows, 2 * HD : 3 * HD])
        value = acc[rows, 3 * HD : 4 * HD].astype(BF16)
        dv = jnp.zeros((L, HD), F32)
        dk_rot = jnp.zeros((L, HD), F32)
        for j in range(2):
            query = rotated(acc[rows, j * HD : (j + 1) * HD])
            grad = jnp.where(valid, cot[rows, j * HD : (j + 1) * HD], jnp.zeros((), BF16))
            bend = jnp.tanh(dot(key, query, NT) * (SCALE / CAP))
            weights = jnp.where(keep, jnp.exp(CAP * bend), 0.0)
            probs = weights * (1.0 / jnp.sum(weights, 0, keepdims=True))
            dv += dot(probs.astype(BF16), grad)
            grad_probs = dot(value, grad, NT)
            delta = jnp.sum(probs * grad_probs, 0, keepdims=True)
            ds = probs * (grad_probs - delta) * ((1.0 - bend * bend) * SCALE)
            dk_rot += dot(ds.astype(BF16), query)
        dk = (dk_rot * cos - pltpu.roll(dk_rot, HD // 2, 1) * sin).astype(BF16)
        dv = dv.astype(BF16)
        for i, d in enumerate((dk, dv)):
            grads[rows, i * HD : (i + 1) * HD] = d
            folded = jnp.sum(gram[s] * dot(d, d, NT), 0, keepdims=True)
            norms[2 * i + s : 2 * i + s + 1] = folded[:, :HD] + folded[:, HD:]


def attend(info, place, mine, other, w, cot, cosine, sine, gram):
    smem = pl.BlockSpec(memory_space=pltpu.SMEM)
    vmem = pl.BlockSpec(memory_space=pltpu.VMEM)
    return pl.pallas_call(
        attend_kernel,
        in_specs=[smem] * 2 + [vmem] * 2 + [pl.BlockSpec(memory_space=pl.ANY)] + [vmem] * 4,
        out_specs=[vmem] * 2,
        out_shape=[
            jax.ShapeDtypeStruct((TOKENS, 2 * HD), BF16),
            jax.ShapeDtypeStruct((4, HD), F32),
        ],
        scratch_shapes=[
            pltpu.VMEM((TOKENS, D), BF16),
            pltpu.VMEM((D, 4 * HD), BF16),
            pltpu.VMEM((TOKENS, 4 * HD), F32),
            pltpu.SemaphoreType.DMA((NY // 2,)),
        ],
        compiler_params=pltpu.CompilerParams(vmem_limit_bytes=VMEM_ATTEND),
        cost_estimate=pl.CostEstimate(
            flops=2 * TOKENS * 4 * HD * D + 4 * 12 * L * L * HD,
            bytes_accessed=4 * D * TOKENS,
            transcendentals=8 * L * L,
        ),
        name="attend",
    )(info, place, mine, other, w, cot, cosine, sine, gram)


def clip_kernel(place, norms, *refs):
    grads, scaled = refs[:NX], refs[NX]
    for j in range(NX):
        x = lax.rem(place[2] + j, NX)
        sums = jnp.sum(jnp.sum(norms[x], 0), 1, keepdims=True)
        factors = CLIP / jnp.maximum(jnp.sqrt(sums), CLIP)
        for s in range(2):
            rows = slice(s * L, (s + 1) * L)
            for i in range(2):
                columns = slice(i * HD, (i + 1) * HD)
                factor = factors[2 * i + s : 2 * i + s + 1, :]
                part = factor * grads[j][rows, columns].astype(F32)
                scaled[j * TOKENS + s * L : j * TOKENS + (s + 1) * L, columns] = part.astype(BF16)


def clip(place, norms, grads):
    vmem = pl.BlockSpec(memory_space=pltpu.VMEM)
    return pl.pallas_call(
        clip_kernel,
        in_specs=[pl.BlockSpec(memory_space=pltpu.SMEM)] + [vmem] * (NX + 1),
        out_specs=vmem,
        out_shape=jax.ShapeDtypeStruct((NX * TOKENS, 2 * HD), BF16),
        compiler_params=pltpu.CompilerParams(vmem_limit_bytes=VMEM),
        name="clip",
    )(place, norms, *grads)


def gradient_kernel(features, own, scaled, out, held, sems):
    def fetch(j, s):
        columns = pl.ds((2 * (j - 1) + s) * L, L)
        return pltpu.make_async_copy(
            features.at[:, s, j - 1], held.at[:, :, columns], sems.at[2 * (j - 1) + s]
        )

    for j in range(1, NX):
        for s in range(2):
            fetch(j, s).start()
    total = dot(own[...].reshape(NZ * ROWS, TOKENS), scaled[:TOKENS])
    for j in range(1, NX):
        for s in range(2):
            fetch(j, s).wait()
        rows = held[:, :, (j - 1) * TOKENS : j * TOKENS].reshape(NZ * ROWS, TOKENS)
        total += dot(rows, scaled[j * TOKENS : (j + 1) * TOKENS])
    out[...] = total.astype(BF16).reshape(NZ, ROWS, 2 * HD)


def gradient(features, own, scaled):
    vmem = pl.BlockSpec(memory_space=pltpu.VMEM)
    return pl.pallas_call(
        gradient_kernel,
        in_specs=[pl.BlockSpec(memory_space=pl.ANY)] + [vmem] * 2,
        out_specs=vmem,
        out_shape=jax.ShapeDtypeStruct((NZ, ROWS, 2 * HD), BF16),
        scratch_shapes=[
            pltpu.VMEM((NZ, ROWS, (NX - 1) * TOKENS), BF16),
            pltpu.SemaphoreType.DMA((2 * (NX - 1),)),
        ],
        compiler_params=pltpu.CompilerParams(vmem_limit_bytes=VMEM_MOST),
        cost_estimate=pl.CostEstimate(
            flops=2 * D * TOKENS * 2 * HD, bytes_accessed=3 * D * TOKENS, transcendentals=0
        ),
        name="gradient",
    )(features, own, scaled)


def hop(a, axis, size, k):
    return lax.ppermute(a, axis, ring(size, k))


def together(*arrays):
    return lax.optimization_barrier(arrays)


def gather_features(shard):
    at_first = lax.axis_index("core") == 0
    x = lax.axis_index("x")
    up = [shard, hop(shard, "y", NY, 1)]
    down = [shard, hop(shard, "y", NY, 7)]
    up[1], down[1], part = together(up[1], down[1], shard)
    first, second = part[:, :L], part[:, L:]
    keep = jnp.where(at_first, first, second)
    come = hop(jnp.where(at_first, second, first), "core", NC, 1)
    up.append(hop(up[1], "y", NY, 1))
    down.append(hop(down[1], "y", NY, 7))
    up[2], down[2], come = together(up[2], down[2], come)
    pair = jnp.where(at_first, jnp.concatenate([keep, come], 0), jnp.concatenate([come, keep], 0))
    piece = lambda k: lax.dynamic_slice_in_dim(pair, lax.rem(x + k, NX) * ROWS, ROWS, 0)
    owned = [hop(piece(NX - k), "x", NX, k) for k in range(1, NX)]
    up.append(hop(up[2], "y", NY, 1))
    down.append(hop(down[2], "y", NY, 7))
    up[3], down[3], *owned = together(up[3], down[3], *owned)
    up.append(hop(up[3], "y", NY, 1))
    owned = lax.all_gather(jnp.stack(owned), ("y", "core"), axis=0)
    return jnp.stack(up + down[:0:-1]), owned.reshape(NY, NC, NX - 1, ROWS, L)


def body(inputs, w_query, w_key, w_value, cotangent, lengths, sampled, step, tree_noise):
    w = jnp.concatenate([w_query, w_key, w_value], 1)
    w = lax.all_gather(w, "x", axis=0, tiled=True)
    w, shard = together(w, inputs.T)
    w = lax.all_gather(w, "z", axis=0, tiled=True)

    mine, owned = gather_features(shard)
    other = hop(mine, "core", NC, 1)
    place = jnp.stack([lax.axis_index(a) for a in ("y", "core", "x")]).astype(jnp.int32)
    gram, own = gram_of(place, mine, other)

    cosine, sine = rope_tables(L, HD)
    grads, norms = attend(
        jnp.concatenate([lengths, sampled]), place, mine, other, w, cotangent, cosine, sine, gram
    )
    grads = [grads] + [hop(grads, "x", NX, k) for k in range(1, NX)]
    norms = lax.psum(norms, "core")
    norms = lax.all_to_all(jnp.broadcast_to(norms, (NX * NY, 4, HD)), ("x", "y"), 0, 0)
    scaled = clip(place, norms.reshape(NX, NY, 4, HD), grads)
    terms = gradient(owned, own, scaled)
    terms = lax.all_to_all(terms, "z", 0, 0)
    summed = jnp.sum(terms.astype(F32), 0)

    levels = tree_noise.shape[0]
    bits = (step[0] // 2 ** jnp.arange(levels, dtype=jnp.int32) % 2).astype(F32)
    noise = jnp.sum(bits[:, None, None, None] * tree_noise, 0)
    expected = 0.85 * (2 * NZ * NX)
    return summed[:, :HD] / expected + noise[0], summed[:, HD:] / expected + noise[1]


def solution(mesh):
    mesh = Mesh(np.asarray(mesh.devices).reshape(NZ, NX, NY, NC), ("z", "x", "y", "core"))
    dp, head = ("z", "x"), ("y", "core")
    in_specs = (
        P(dp, head),
        P(dp, head),
        P(dp, head),
        P(dp, head),
        P(dp, head),
        P(dp),
        P(dp),
        P(),
        P(None, None, dp, head),
    )
    out_specs = (P(dp, head), P(dp, head))
    return jax.shard_map(body, mesh=mesh, in_specs=in_specs, out_specs=out_specs, check_vma=False)
```

time: 181 us -> 178 us (0.983)
  blocking collectives: 58.9 us -> 33.5 us
  starting transfers between devices: 38.8 us -> 59.3 us
  Pallas kernels: 17.6 us -> 19.7 us
  local copies, waits for them, and re-layouts: 2.12 us -> 4.17 us
    all_to_all x2 -> x1, blocking collectives: 43.5 us -> 17.5 us  [body(): lax.all_to_all(jnp.broadcast_to(norms, (NX * NY, 4, HD)), ('x', 'y'), 0, 0)]
    ppermute x8 -> x15, starting transfers between devices: 34.9 us -> 52 us  [hop(): return lax.ppermute(a, axis, ring(size, k))]
    all_gather x1, waiting for transfers between devices: 7.77 us -> 0.01 us  [body(): w = lax.all_gather(w, 'z', axis=0, tiled=True)]
    all_gather x0 -> x1, waiting for transfers between devices: none -> 3.51 us  [gather_features(): owned = lax.all_gather(jnp.stack(owned), ('y', 'core'), axis=0)]
    all_to_all x1, starting transfers between devices: 3.85 us -> 7.2 us  [body(): terms = lax.all_to_all(terms, 'z', 0, 0)]
    all_to_all x1, waiting for transfers between devices: 15.3 us -> 18.5 us  [body(): terms = lax.all_to_all(terms, 'z', 0, 0)]
    pallas_call x3 -> x4, Pallas kernels: 17.6 us -> 19.7 us  [the longest x1 8.89 us: attend(): pl.pallas_call(attend_kernel, in_specs=[smem] * 2 + [vmem] * 2 + [pl.Bloc...]
    unnamed x21 -> x29, local copies, waits for them, and re-layouts: 2.09 us -> 4.11 us
  transfers between devices with their start and end apart: 10 -> 18, of which waited for: 7 -> 9; matrix products, arithmetic and copies ran while one was open for 2% -> 3% of each run, Pallas kernels for 3% -> 7%
where the time goes in v3:
time: 178 us; the launch traced here: 177 us
  starting transfers between devices  59.3 us (33%)
  waiting for transfers between devices  40.4 us (23%)
  blocking collectives  33.5 us (19%)
  Pallas kernels  19.7 us (11%)
  between operations  15.1 us (8%)
  other arithmetic  4.69 us (3%)
  local copies, waits for them, and re-layouts  4.17 us (2%)
    ppermute x15, starting transfers between devices, hop(): return lax.ppermute(a, axis, ring(size, k))  52 us
    all_to_all x1, waiting for transfers between devices, body(): terms = lax.all_to_all(terms, 'z', 0, 0)  18.5 us
    ppermute x15, waiting for transfers between devices, hop(): return lax.ppermute(a, axis, ring(size, k))  18.4 us
    all_to_all x1, blocking collectives, body(): lax.all_to_all(jnp.broadcast_to(norms, (NX * NY, 4, HD)), ('x', 'y'), 0, 0)  17.5 us
    all_gather x1, blocking collectives, body(): w = lax.all_gather(w, 'x', axis=0, tiled=True)  12.5 us
    pallas_call x1, Pallas kernels, attend(): pl.pallas_call(attend_kernel, in_specs=[smem] * 2 + [vmem] * 2 + [pl.Bloc...  8.89 us
    all_to_all x1, starting transfers between devices, body(): terms = lax.all_to_all(terms, 'z', 0, 0)  7.2 us
    pallas_call x1, Pallas kernels, gradient(): pl.pallas_call(gradient_kernel, in_specs=[pl.BlockSpec(memory_space=pl.AN...  6.6 us
  transfers between devices with their start and end apart: 18, of which 9 were waited for; matrix products, arithmetic and copies ran while one was open for 3% of the time, Pallas kernels for 7%

profile of v3, /device:TPU:1, one launch (start us, length us, event | category | flops | bytes accessed | tf_op | source)
XLA Modules:
  0.0 176.8 jit_solution(10817362443279223077)
XLA Ops:
  8.2 12.5 %all_gather.12 = bf16[576,512]{1,0:T(8,128)(2,1)} all-gather(bf16[144,512]{1,0:T(8,128)(2,1)S(1)} %pad_maximum_fusion.1), channel_id=1, replica_groups=mesh['z'=8,'x'=4,'y'=8,'core'=2] {'x'}, dimensions={0}, use_global_device_ids=true | all-gather | bytes 737280 | tf_op jit(solution)/shard_map/all_gather | solution.py:272
  20.8 5.6 %collective-permute-start = (bf16[288,512]{1,0:T(8,128)(2,1)}, bf16[288,512]{1,0:T(8,128)(2,1)S(1)}, u32[]{:S(2)}, u32[]{:S(2)}) collective-permute-start(bf16[288,512]{1,0:T(8,128)(2,1)} %bitcast.38), channel_id=1, source_target_pairs={{2,0},{4,2},{6,4},{8,6},{10,8},{12,10},{14,12},{0,14},{3,1},{5,3},... | collective-permute-start | bytes 884744 | tf_op jit(solution)/shard_map/ppermute | solution.py:240
  30.4 4.9 %collective-permute-done.1 = bf16[288,512]{1,0:T(8,128)(2,1)S(1)} collective-permute-done((bf16[288,512]{1,0:T(8,128)(2,1)}, bf16[288,512]{1,0:T(8,128)(2,1)S(1)}, u32[]{:S(2)}, u32[]{:S(2)}) %collective-permute-start.1) | collective-permute-done | bytes 294944 | tf_op jit(solution)/shard_map/ppermute | solution.py:240
  37.3 3.2 %collective-permute-start.3 = (bf16[288,512]{1,0:T(8,128)(2,1)S(1)}, bf16[288,512]{1,0:T(8,128)(2,1)S(1)}, u32[]{:S(2)}, u32[]{:S(2)}) collective-permute-start(bf16[288,512]{1,0:T(8,128)(2,1)S(1)} %collective-permute-done.1), channel_id=1, source_target_pairs={{14,0},{0,2},{2,4},{4,6},{6,8},{8,10},{10,12},{12,14},{15,1},{1,3}... | collective-permute-start | bytes 884744 | tf_op jit(solution)/shard_map/ppermute | solution.py:240
  41.6 8.2 %collective-permute-start.4 = (bf16[288,256]{1,0:T(8,128)(2,1)S(1)}, bf16[288,256]{1,0:T(8,128)(2,1)S(1)}, u32[]{:S(2)}, u32[]{:S(2)}) collective-permute-start(bf16[288,256]{1,0:T(8,128)(2,1)S(1)} %get-tuple-element.42), channel_id=1, source_target_pairs={{1,0},{0,1},{3,2},{2,3},{5,4},{4,5},{7,6},{6,7},{9,8},{8,9},{11,10... | collective-permute-start | bytes 442376 | tf_op jit(solution)/shard_map/ppermute | solution.py:240
  50.8 2.8 %collective-permute-start.5 = (bf16[288,512]{1,0:T(8,128)(2,1)S(1)}, bf16[288,512]{1,0:T(8,128)(2,1)}, u32[]{:S(2)}, u32[]{:S(2)}) collective-permute-start(bf16[288,512]{1,0:T(8,128)(2,1)S(1)} %collective-permute-done.2), channel_id=1, source_target_pairs={{2,0},{4,2},{6,4},{8,6},{10,8},{12,10},{14,12},{0,14},{3,1},{5,3},... | collective-permute-start | bytes 884744 | tf_op jit(solution)/shard_map/ppermute | solution.py:240
  53.6 2.4 %collective-permute-start.6 = (bf16[288,512]{1,0:T(8,128)(2,1)S(1)}, bf16[288,512]{1,0:T(8,128)(2,1)S(1)}, u32[]{:S(2)}, u32[]{:S(2)}) collective-permute-start(bf16[288,512]{1,0:T(8,128)(2,1)S(1)} %collective-permute-done.3), channel_id=1, source_target_pairs={{14,0},{0,2},{2,4},{4,6},{6,8},{8,10},{10,12},{12,14},{15,1},{1,3}... | collective-permute-start | bytes 884744 | tf_op jit(solution)/shard_map/ppermute | solution.py:240
  56.2 3.0 %collective-permute-start.7 = (bf16[144,256]{1,0:T(8,128)(2,1)S(1)}, bf16[144,256]{1,0:T(8,128)(2,1)S(1)}, u32[]{:S(2)}, u32[]{:S(2)}) collective-permute-start(bf16[144,256]{1,0:T(8,128)(2,1)S(1)} %get-tuple-element.40), channel_id=1, source_target_pairs={{16,0},{32,16},{48,32},{0,48},{17,1},{33,17},{49,33},{1,49},{18,2}... | collective-permute-start | bytes 221192 | tf_op jit(solution)/shard_map/ppermute | solution.py:240
  59.2 2.5 %collective-permute-start.8 = (bf16[144,256]{1,0:T(8,128)(2,1)S(1)}, bf16[144,256]{1,0:T(8,128)(2,1)S(1)}, u32[]{:S(2)}, u32[]{:S(2)}) collective-permute-start(bf16[144,256]{1,0:T(8,128)(2,1)S(1)} %get-tuple-element.39), channel_id=1, source_target_pairs={{32,0},{48,16},{0,32},{16,48},{33,1},{49,17},{1,33},{17,49},{34,2}... | collective-permute-start | bytes 221192 | tf_op jit(solution)/shard_map/ppermute | solution.py:240
  65.9 2.6 %collective-permute-done.9 = bf16[144,256]{1,0:T(8,128)(2,1)S(1)} collective-permute-done((bf16[144,256]{1,0:T(8,128)(2,1)S(1)}, bf16[144,256]{1,0:T(8,128)(2,1)S(1)}, u32[]{:S(2)}, u32[]{:S(2)}) %collective-permute-start.9) | collective-permute-done | bytes 73760 | tf_op jit(solution)/shard_map/ppermute | solution.py:240
  69.4 5.1 %collective-permute-start.10 = (bf16[288,512]{1,0:T(8,128)(2,1)}, bf16[288,512]{1,0:T(8,128)(2,1)S(1)}, u32[]{:S(2)}, u32[]{:S(2)}) collective-permute-start(bf16[288,512]{1,0:T(8,128)(2,1)} %collective-permute-done.5), channel_id=1, source_target_pairs={{2,0},{4,2},{6,4},{8,6},{10,8},{12,10},{14,12},{0,14},{3,1},{5,3},... | collective-permute-start | bytes 884744 | tf_op jit(solution)/shard_map/ppermute | solution.py:240
  76.5 2.6 %collective-permute-done.10 = bf16[288,512]{1,0:T(8,128)(2,1)S(1)} collective-permute-done((bf16[288,512]{1,0:T(8,128)(2,1)}, bf16[288,512]{1,0:T(8,128)(2,1)S(1)}, u32[]{:S(2)}, u32[]{:S(2)}) %collective-permute-start.10) | collective-permute-done | bytes 294944 | tf_op jit(solution)/shard_map/ppermute | solution.py:240
  79.2 5.1 %collective-permute-start.11 = (bf16[8,288,512]{2,1,0:T(8,128)(2,1)S(1)}, bf16[8,288,512]{2,1,0:T(8,128)(2,1)}, u32[]{:S(2)}, u32[]{:S(2)}) collective-permute-start(bf16[8,288,512]{2,1,0:T(8,128)(2,1)S(1)} %bitcast_dynamic-update-slice_fusion.mine), channel_id=1, source_target_pairs={{1,0},{0,1},{3,2},{2,3},{5,4},{4,5},{7,6},{6,7},{9,8},{8,9},{11,10... | collective-permute-start | bytes 7077896 | tf_op jit(solution)/shard_map/ppermute | solution.py:240
  85.2 3.4 %collective-permute-done.11.other = bf16[8,288,512]{2,1,0:T(8,128)(2,1)} collective-permute-done((bf16[8,288,512]{2,1,0:T(8,128)(2,1)S(1)}, bf16[8,288,512]{2,1,0:T(8,128)(2,1)}, u32[]{:S(2)}, u32[]{:S(2)}) %collective-permute-start.11) | collective-permute-done | bytes 2359328 | tf_op jit(solution)/shard_map/ppermute | solution.py:240
  88.6 3.3 %gram.1 = (f32[2,256,256]{2,1,0:T(8,128)S(1)}, bf16[8,144,512]{2,1,0:T(8,128)(2,1)S(1)}) custom-call(s32[3]{0:T(128)S(1)} %pad_add_fusion.place, bf16[8,288,512]{2,1,0:T(8,128)(2,1)S(1)} %bitcast_dynamic-update-slice_fusion.mine, bf16[8,288,512]{2,1,0:T(8,128)(2,1)} %collective-permute-done.11.other), custom_call_target="tpu_custom_call" | custom-call | flops 1207959552 | bytes 4718592 | tf_op jit(solution)/shard_map/gram/pallas_call | solution.py:71
  93.0 8.9 %attend.1 = (bf16[512,256]{1,0:T(8,128)(2,1)S(1)}, f32[4,128]{1,0:T(4,128)S(1)}) custom-call(s32[4]{0:T(128)S(1)} %pad_add_fusion.1.info, s32[3]{0:T(128)S(1)} %pad_add_fusion.place, bf16[8,288,512]{2,1,0:T(8,128)(2,1)} %copy-done, bf16[8,288,512]{2,1,0:T(8,128)(2,1)} %collective-permute-done.11.other, bf16[4608,512]{1,0:T(8,128)(2,1)} %all-gather.4.cloned.1.call-done.w, ...), custom_call_target="tpu_custom_call" | custom-call | flops 2818572288 | bytes 9437184 | tf_op jit(solution)/shard_map/attend/pallas_call | solution.py:150
  101.9 2.8 %collective-permute-start.12 = (bf16[512,256]{1,0:T(8,128)(2,1)S(1)}, bf16[512,256]{1,0:T(8,128)(2,1)S(1)}, u32[]{:S(2)}, u32[]{:S(2)}) collective-permute-start(bf16[512,256]{1,0:T(8,128)(2,1)S(1)} %get-tuple-element.35.refs_0_), channel_id=1, source_target_pairs={{16,0},{32,16},{48,32},{0,48},{17,1},{33,17},{49,33},{1,49},{18,2}... | collective-permute-start | bytes 786440 | tf_op jit(solution)/shard_map/ppermute | solution.py:240
  106.9 2.8 %collective-permute-start.14 = (bf16[512,256]{1,0:T(8,128)(2,1)S(1)}, bf16[512,256]{1,0:T(8,128)(2,1)S(1)}, u32[]{:S(2)}, u32[]{:S(2)}) collective-permute-start(bf16[512,256]{1,0:T(8,128)(2,1)S(1)} %get-tuple-element.35.refs_0_), channel_id=1, source_target_pairs={{48,0},{0,16},{16,32},{32,48},{49,1},{1,17},{17,33},{33,49},{50,2}... | collective-permute-start | bytes 786440 | tf_op jit(solution)/shard_map/ppermute | solution.py:240
  109.7 3.4 %psum.7 = f32[4,128]{1,0:T(4,128)S(1)} all-reduce(f32[4,128]{1,0:T(4,128)S(1)} %get-tuple-element.34), channel_id=1, replica_groups=mesh['z'=8,'x'=4,'y'=8,'core'=2] {'core'}, use_global_device_ids=true, to_apply=%region_0.1 | all-reduce | flops 512 | bytes 4096 | tf_op jit(solution)/shard_map/psum | solution.py:286
  113.1 17.5 %all_to_all.10 = f32[32,4,128]{2,1,0:T(4,128)S(1)} all-to-all(f32[32,4,128]{2,1,0:T(4,128)S(1)} %broadcast_in_dim.4), channel_id=1, replica_groups=mesh['z'=8,'x'=4,'y'=8,'core'=2] {'x','y'}, dimensions={0} | all-to-all | bytes 131072 | tf_op jit(solution)/shard_map/all_to_all | solution.py:287
  132.5 3.5 %all-gather.6.cloned.1.call-done = bf16[48,144,256]{2,1,0:T(8,128)(2,1)} async-done(((bf16[3,144,256]{2,1,0:T(8,128)(2,1)}), bf16[48,144,256]{2,1,0:T(8,128)(2,1)}) %all-gather.6.cloned.1.call-update) | async-done | bytes 3538960 | tf_op jit(solution)/shard_map/all_gather | solution.py:266
  136.0 6.6 %gradient.1 = bf16[8,144,256]{2,1,0:T(8,128)(2,1)} custom-call(bf16[8,2,3,144,256]{4,3,2,1,0:T(8,128)(2,1)} %bitcast.37, bf16[8,144,512]{2,1,0:T(8,128)(2,1)} %copy-done.2, bf16[2048,256]{1,0:T(8,128)(2,1)} %copy-done.1), custom_call_target="tpu_custom_call" | custom-call | flops 1207959552 | bytes 7077888 | tf_op jit(solution)/shard_map/gradient/pallas_call | solution.py:222
  142.6 7.2 %all-to-all-start.1 = ((bf16[8,144,256]{2,1,0:T(8,128)(2,1)}), bf16[8,144,256]{2,1,0:T(8,128)(2,1)S(1)}, u32[]{:S(2)}, u32[]{:S(2)}) async-start(bf16[8,144,256]{2,1,0:T(8,128)(2,1)} %gradient.1), calls=%async_computation.1 | async-start | bytes 1179648 | tf_op jit(solution)/shard_map/all_to_all | solution.py:290
  150.7 18.5 %all-to-all-done.1 = bf16[8,144,256]{2,1,0:T(8,128)(2,1)S(1)} async-done(((bf16[8,144,256]{2,1,0:T(8,128)(2,1)}), bf16[8,144,256]{2,1,0:T(8,128)(2,1)S(1)}, u32[]{:S(2)}, u32[]{:S(2)}) %all-to-all-start.1) | async-done | bytes 589856 | tf_op jit(solution)/shard_map/all_to_all | solution.py:290
  (66 shorter events, 23.2 us)
Async XLA Ops:
  7.2 62.1 %copy-start.4 = (bf16[512,288]{0,1:T(8,128)(2,1)S(1)}, bf16[512,288]{0,1:T(8,128)(2,1)}, u32[]{:S(2)}) copy-start(bf16[512,288]{0,1:T(8,128)(2,1)} %param.9) | copy-start | bytes 884740
  7.2 85.8 %all-gather.4.cloned.1.call-start = ((), (), s32[]{:S(2)}) async-start(), calls=%async_computation.2 | async-start | bytes 5308416 | tf_op jit(solution)/shard_map/all_gather | solution.py:274
  20.8 115.2 %all-gather.6.cloned.1.call-start = ((), (), s32[]{:S(2)}) async-start(), calls=%async_computation.3 | async-start | bytes 3760128 | tf_op jit(solution)/shard_map/all_gather | solution.py:266
  20.8 9.5 %collective-permute-start = (bf16[288,512]{1,0:T(8,128)(2,1)}, bf16[288,512]{1,0:T(8,128)(2,1)S(1)}, u32[]{:S(2)}, u32[]{:S(2)}) collective-permute-start(bf16[288,512]{1,0:T(8,128)(2,1)} %bitcast.38), channel_id=1, source_target_pairs={{2,0},{4,2},{6,4},{8,6},{10,8},{12,10},{14,12},{0,14},{3,1},{5,3},... | collective-permute-start | bytes 884744 | tf_op jit(solution)/shard_map/ppermute | solution.py:240
  26.4 8.9 %collective-permute-start.1 = (bf16[288,512]{1,0:T(8,128)(2,1)}, bf16[288,512]{1,0:T(8,128)(2,1)S(1)}, u32[]{:S(2)}, u32[]{:S(2)}) collective-permute-start(bf16[288,512]{1,0:T(8,128)(2,1)} %bitcast.39), channel_id=1, source_target_pairs={{14,0},{0,2},{2,4},{4,6},{6,8},{8,10},{10,12},{12,14},{15,1},{1,3}... | collective-permute-start | bytes 884744 | tf_op jit(solution)/shard_map/ppermute | solution.py:240
  35.3 15.5 %collective-permute-start.2 = (bf16[288,512]{1,0:T(8,128)(2,1)S(1)}, bf16[288,512]{1,0:T(8,128)(2,1)S(1)}, u32[]{:S(2)}, u32[]{:S(2)}) collective-permute-start(bf16[288,512]{1,0:T(8,128)(2,1)S(1)} %collective-permute-done), channel_id=1, source_target_pairs={{2,0},{4,2},{6,4},{8,6},{10,8},{12,10},{14,12},{0,14},{3,1},{5,3},... | collective-permute-start | bytes 884744 | tf_op jit(solution)/shard_map/ppermute | solution.py:240
  37.3 13.4 %collective-permute-start.3 = (bf16[288,512]{1,0:T(8,128)(2,1)S(1)}, bf16[288,512]{1,0:T(8,128)(2,1)S(1)}, u32[]{:S(2)}, u32[]{:S(2)}) collective-permute-start(bf16[288,512]{1,0:T(8,128)(2,1)S(1)} %collective-permute-done.1), channel_id=1, source_target_pairs={{14,0},{0,2},{2,4},{4,6},{6,8},{8,10},{10,12},{12,14},{15,1},{1,3}... | collective-permute-start | bytes 884744 | tf_op jit(solution)/shard_map/ppermute | solution.py:240
  41.6 9.2 %collective-permute-start.4 = (bf16[288,256]{1,0:T(8,128)(2,1)S(1)}, bf16[288,256]{1,0:T(8,128)(2,1)S(1)}, u32[]{:S(2)}, u32[]{:S(2)}) collective-permute-start(bf16[288,256]{1,0:T(8,128)(2,1)S(1)} %get-tuple-element.42), channel_id=1, source_target_pairs={{1,0},{0,1},{3,2},{2,3},{5,4},{4,5},{7,6},{6,7},{9,8},{8,9},{11,10... | collective-permute-start | bytes 442376 | tf_op jit(solution)/shard_map/ppermute | solution.py:240
  50.8 18.5 %copy-start.6 = (bf16[288,512]{1,0:T(8,128)(2,1)}, bf16[288,512]{1,0:T(8,128)(2,1)S(1)}, u32[]{:S(2)}) copy-start(bf16[288,512]{1,0:T(8,128)(2,1)S(1)} %collective-permute-done.2) | copy-start | bytes 884740
  50.8 17.7 %collective-permute-start.5 = (bf16[288,512]{1,0:T(8,128)(2,1)S(1)}, bf16[288,512]{1,0:T(8,128)(2,1)}, u32[]{:S(2)}, u32[]{:S(2)}) collective-permute-start(bf16[288,512]{1,0:T(8,128)(2,1)S(1)} %collective-permute-done.2), channel_id=1, source_target_pairs={{2,0},{4,2},{6,4},{8,6},{10,8},{12,10},{14,12},{0,14},{3,1},{5,3},... | collective-permute-start | bytes 884744 | tf_op jit(solution)/shard_map/ppermute | solution.py:240
  53.6 14.8 %collective-permute-start.6 = (bf16[288,512]{1,0:T(8,128)(2,1)S(1)}, bf16[288,512]{1,0:T(8,128)(2,1)S(1)}, u32[]{:S(2)}, u32[]{:S(2)}) collective-permute-start(bf16[288,512]{1,0:T(8,128)(2,1)S(1)} %collective-permute-done.3), channel_id=1, source_target_pairs={{14,0},{0,2},{2,4},{4,6},{6,8},{8,10},{10,12},{12,14},{15,1},{1,3}... | collective-permute-start | bytes 884744 | tf_op jit(solution)/shard_map/ppermute | solution.py:240
  56.2 7.8 %collective-permute-start.7 = (bf16[144,256]{1,0:T(8,128)(2,1)S(1)}, bf16[144,256]{1,0:T(8,128)(2,1)S(1)}, u32[]{:S(2)}, u32[]{:S(2)}) collective-permute-start(bf16[144,256]{1,0:T(8,128)(2,1)S(1)} %get-tuple-element.40), channel_id=1, source_target_pairs={{16,0},{32,16},{48,32},{0,48},{17,1},{33,17},{49,33},{1,49},{18,2}... | collective-permute-start | bytes 221192 | tf_op jit(solution)/shard_map/ppermute | solution.py:240
  59.2 6.6 %collective-permute-start.8 = (bf16[144,256]{1,0:T(8,128)(2,1)S(1)}, bf16[144,256]{1,0:T(8,128)(2,1)S(1)}, u32[]{:S(2)}, u32[]{:S(2)}) collective-permute-start(bf16[144,256]{1,0:T(8,128)(2,1)S(1)} %get-tuple-element.39), channel_id=1, source_target_pairs={{32,0},{48,16},{0,32},{16,48},{33,1},{49,17},{1,33},{17,49},{34,2}... | collective-permute-start | bytes 221192 | tf_op jit(solution)/shard_map/ppermute | solution.py:240
  61.7 6.7 %collective-permute-start.9 = (bf16[144,256]{1,0:T(8,128)(2,1)S(1)}, bf16[144,256]{1,0:T(8,128)(2,1)S(1)}, u32[]{:S(2)}, u32[]{:S(2)}) collective-permute-start(bf16[144,256]{1,0:T(8,128)(2,1)S(1)} %get-tuple-element.38), channel_id=1, source_target_pairs={{48,0},{0,16},{16,32},{32,48},{49,1},{1,17},{17,33},{33,49},{50,2}... | collective-permute-start | bytes 221192 | tf_op jit(solution)/shard_map/ppermute | solution.py:240
  69.3 15.1 %copy-start.9 = (s32[2]{0:T(128)S(1)}, s32[2]{0:T(128)}, u32[]{:S(2)}) copy-start(s32[2]{0:T(128)} %param.15) | copy-start | bytes 28
  69.3 15.1 %copy-start.10 = (s32[2]{0:T(128)S(1)}, s32[2]{0:T(128)}, u32[]{:S(2)}) copy-start(s32[2]{0:T(128)} %param.14) | copy-start | bytes 28
  69.4 9.7 %collective-permute-start.10 = (bf16[288,512]{1,0:T(8,128)(2,1)}, bf16[288,512]{1,0:T(8,128)(2,1)S(1)}, u32[]{:S(2)}, u32[]{:S(2)}) collective-permute-start(bf16[288,512]{1,0:T(8,128)(2,1)} %collective-permute-done.5), channel_id=1, source_target_pairs={{2,0},{4,2},{6,4},{8,6},{10,8},{12,10},{14,12},{0,14},{3,1},{5,3},... | collective-permute-start | bytes 884744 | tf_op jit(solution)/shard_map/ppermute | solution.py:240
  79.2 12.7 %copy-start = (bf16[8,288,512]{2,1,0:T(8,128)(2,1)}, bf16[8,288,512]{2,1,0:T(8,128)(2,1)S(1)}, u32[]{:S(2)}) copy-start(bf16[8,288,512]{2,1,0:T(8,128)(2,1)S(1)} %bitcast_dynamic-update-slice_fusion.mine) | copy-start | bytes 7077892
  79.2 9.4 %collective-permute-start.11 = (bf16[8,288,512]{2,1,0:T(8,128)(2,1)S(1)}, bf16[8,288,512]{2,1,0:T(8,128)(2,1)}, u32[]{:S(2)}, u32[]{:S(2)}) collective-permute-start(bf16[8,288,512]{2,1,0:T(8,128)(2,1)S(1)} %bitcast_dynamic-update-slice_fusion.mine), channel_id=1, source_target_pairs={{1,0},{0,1},{3,2},{2,3},{5,4},{4,5},{7,6},{6,7},{9,8},{8,9},{11,10... | collective-permute-start | bytes 7077896 | tf_op jit(solution)/shard_map/ppermute | solution.py:240
  101.9 28.7 %collective-permute-start.12 = (bf16[512,256]{1,0:T(8,128)(2,1)S(1)}, bf16[512,256]{1,0:T(8,128)(2,1)S(1)}, u32[]{:S(2)}, u32[]{:S(2)}) collective-permute-start(bf16[512,256]{1,0:T(8,128)(2,1)S(1)} %get-tuple-element.35.refs_0_), channel_id=1, source_target_pairs={{16,0},{32,16},{48,32},{0,48},{17,1},{33,17},{49,33},{1,49},{18,2}... | collective-permute-start | bytes 786440 | tf_op jit(solution)/shard_map/ppermute | solution.py:240
  104.6 26.0 %collective-permute-start.13 = (bf16[512,256]{1,0:T(8,128)(2,1)S(1)}, bf16[512,256]{1,0:T(8,128)(2,1)S(1)}, u32[]{:S(2)}, u32[]{:S(2)}) collective-permute-start(bf16[512,256]{1,0:T(8,128)(2,1)S(1)} %get-tuple-element.35.refs_0_), channel_id=1, source_target_pairs={{32,0},{48,16},{0,32},{16,48},{33,1},{49,17},{1,33},{17,49},{34,2}... | collective-permute-start | bytes 786440 | tf_op jit(solution)/shard_map/ppermute | solution.py:240
  106.9 23.7 %collective-permute-start.14 = (bf16[512,256]{1,0:T(8,128)(2,1)S(1)}, bf16[512,256]{1,0:T(8,128)(2,1)S(1)}, u32[]{:S(2)}, u32[]{:S(2)}) collective-permute-start(bf16[512,256]{1,0:T(8,128)(2,1)S(1)} %get-tuple-element.35.refs_0_), channel_id=1, source_target_pairs={{48,0},{0,16},{16,32},{32,48},{49,1},{1,17},{17,33},{33,49},{50,2}... | collective-permute-start | bytes 786440 | tf_op jit(solution)/shard_map/ppermute | solution.py:240
  136.0 14.6 %copy-start.5 = (f32[4,2,144,128]{3,2,1,0:T(8,128)S(1)}, f32[4,2,144,128]{3,2,1,0:T(8,128)}, u32[]{:S(2)}) copy-start(f32[4,2,144,128]{3,2,1,0:T(8,128)} %param.17) | copy-start | bytes 1769476
  142.6 26.6 %all-to-all-start.1 = ((bf16[8,144,256]{2,1,0:T(8,128)(2,1)}), bf16[8,144,256]{2,1,0:T(8,128)(2,1)S(1)}, u32[]{:S(2)}, u32[]{:S(2)}) async-start(bf16[8,144,256]{2,1,0:T(8,128)(2,1)} %gradient.1), calls=%async_computation.1 | async-start | bytes 1179648 | tf_op jit(solution)/shard_map/all_to_all | solution.py:290
  (5 other events, 20.4 us)
Sparse Core Ops, SparseCore 0:
  20.9 70.2 all-gather.3
  93.3 42.6 all-gather.5

commit v4 on v3

--- a/solution.py
+++ b/solution.py
@@ -25,8 +25,6 @@
 CLIP = 2.0 * math.sqrt(D * KV * HD)
 CHUNK = 2 * PAIR
 VMEM = 32 * 1024 * 1024
-VMEM_ATTEND = 52 * 1024 * 1024
-VMEM_MOST = 58 * 1024 * 1024
 F32 = jnp.float32
 BF16 = jnp.bfloat16
 
@@ -51,61 +49,52 @@
     return jnp.concatenate([cosine, cosine], 1), jnp.concatenate([-sine, sine], 1)
 
 
-def gram_kernel(place, mine, other, gram, own):
-    x = place[2]
-    half = pl.ds(pl.multiple_of(lax.rem(x, 2) * ROWS, ROWS), ROWS)
-    here = x // 2 == place[1]
-    for m in range(NY // 2):
-        for k in (2 * m, 2 * m + 1):
-            own[lax.rem(place[0] + k, NY)] = jnp.where(here, mine[k, half], other[k, half])
-        parts = [mine[2 * m], other[2 * m], mine[2 * m + 1], other[2 * m + 1]]
+def arrange_kernel(place, x_t, x_tok, gram, own):
+    for z in range(NZ):
+        at = z * PAIR + place[2] * ROWS
+        own[z] = x_t[pl.ds(pl.multiple_of(at, ROWS), ROWS)]
+    for m in range(NZ // 2):
+        parts = []
+        for r in (2 * m, 2 * m + 1):
+            at = lax.rem(r + place[3], NZ) * PAIR
+            parts.append(x_t[pl.ds(pl.multiple_of(at, PAIR), PAIR)])
         rows = jnp.concatenate(parts, 0).T
+        x_tok[:, m * CHUNK : (m + 1) * CHUNK] = rows
         for s in range(2):
             part = rows[s * L : (s + 1) * L]
             product = dot(part, part, NT)
             gram[s] = product if m == 0 else gram[s] + product
 
 
-def gram_of(place, mine, other):
-    vmem = pl.BlockSpec(memory_space=pltpu.VMEM)
-    return pl.pallas_call(
-        gram_kernel,
-        in_specs=[pl.BlockSpec(memory_space=pltpu.SMEM)] + [vmem] * 2,
-        out_specs=[vmem] * 2,
+def arrange(place, x_t):
+    vmem = pl.BlockSpec(memory_space=pltpu.VMEM)
+    return pl.pallas_call(
+        arrange_kernel,
+        in_specs=[pl.BlockSpec(memory_space=pltpu.SMEM), vmem],
+        out_specs=[vmem] * 3,
         out_shape=[
+            jax.ShapeDtypeStruct((TOKENS, D), BF16),
             jax.ShapeDtypeStruct((2, L, L), F32),
             jax.ShapeDtypeStruct((NZ, ROWS, TOKENS), BF16),
         ],
         compiler_params=pltpu.CompilerParams(vmem_limit_bytes=VMEM),
         cost_estimate=pl.CostEstimate(
-            flops=2 * 2 * L * L * D, bytes_accessed=2 * D * TOKENS, transcendentals=0
+            flops=2 * 2 * L * L * D, bytes_accessed=2 * 2 * D * TOKENS, transcendentals=0
         ),
-        name="gram",
-    )(place, mine, other)
-
-
-def attend_kernel(
-    info, place, mine, other, w, cot, cosine, sine, gram, grads, norms, x_tok, held, acc, sems
-):
-    def fetch(m):
-        part = pl.ds(m * CHUNK, CHUNK)
-        return pltpu.make_async_copy(w.at[part], held.at[part], sems.at[m])
-
-    for m in range(NY // 2):
-        fetch(m).start()
-    first = place[1] == 0
-    for m in range(NY // 2):
-        parts = []
-        for half in range(2):
-            at = lax.rem(2 * m + half + NY - place[0], NY)
-            a, b = mine[at], other[at]
-            parts += [jnp.where(first, a, b), jnp.where(first, b, a)]
-        x_tok[:, m * CHUNK : (m + 1) * CHUNK] = jnp.concatenate(parts, 0).T
-    for m in range(NY // 2):
-        fetch(m).wait()
-        part = slice(m * CHUNK, (m + 1) * CHUNK)
-        product = dot(x_tok[:, part], held[part])
-        acc[...] = product if m == 0 else acc[...] + product
+        name="arrange",
+    )(place, x_t)
+
+
+def attend_kernel(info, x_tok, *refs):
+    w = refs[: NZ + 1]
+    cot, cosine, sine, gram, grads, norms, acc = refs[NZ + 1 :]
+    blocks = [w[r][...] for r in range(4)]
+    blocks += [jnp.concatenate([w[4][...], w[5][...]], 0)]
+    blocks += [w[r][...] for r in range(6, 9)]
+    for m in range(NZ // 2):
+        pair = jnp.concatenate(blocks[2 * m : 2 * m + 2], 0)
+        part = dot(x_tok[:, m * CHUNK : (m + 1) * CHUNK], pair)
+        acc[...] = part if m == 0 else acc[...] + part
 
     cos = cosine[...]
     sin = sine[...]
@@ -144,31 +133,25 @@
             norms[2 * i + s : 2 * i + s + 1] = folded[:, :HD] + folded[:, HD:]
 
 
-def attend(info, place, mine, other, w, cot, cosine, sine, gram):
-    smem = pl.BlockSpec(memory_space=pltpu.SMEM)
+def attend(info, x_tok, w, cot, cosine, sine, gram):
     vmem = pl.BlockSpec(memory_space=pltpu.VMEM)
     return pl.pallas_call(
         attend_kernel,
-        in_specs=[smem] * 2 + [vmem] * 2 + [pl.BlockSpec(memory_space=pl.ANY)] + [vmem] * 4,
+        in_specs=[pl.BlockSpec(memory_space=pltpu.SMEM)] + [vmem] * (NZ + 6),
         out_specs=[vmem] * 2,
         out_shape=[
             jax.ShapeDtypeStruct((TOKENS, 2 * HD), BF16),
             jax.ShapeDtypeStruct((4, HD), F32),
         ],
-        scratch_shapes=[
-            pltpu.VMEM((TOKENS, D), BF16),
-            pltpu.VMEM((D, 4 * HD), BF16),
-            pltpu.VMEM((TOKENS, 4 * HD), F32),
-            pltpu.SemaphoreType.DMA((NY // 2,)),
-        ],
-        compiler_params=pltpu.CompilerParams(vmem_limit_bytes=VMEM_ATTEND),
+        scratch_shapes=[pltpu.VMEM((TOKENS, 4 * HD), F32)],
+        compiler_params=pltpu.CompilerParams(vmem_limit_bytes=VMEM),
         cost_estimate=pl.CostEstimate(
             flops=2 * TOKENS * 4 * HD * D + 4 * 12 * L * L * HD,
             bytes_accessed=4 * D * TOKENS,
             transcendentals=8 * L * L,
         ),
         name="attend",
-    )(info, place, mine, other, w, cot, cosine, sine, gram)
+    )(info, x_tok, *w, cot, cosine, sine, gram)
 
 
 def clip_kernel(place, norms, *refs):
@@ -212,8 +195,7 @@
     for j in range(1, NX):
         for s in range(2):
             fetch(j, s).wait()
-        rows = held[:, :, (j - 1) * TOKENS : j * TOKENS].reshape(NZ * ROWS, TOKENS)
-        total += dot(rows, scaled[j * TOKENS : (j + 1) * TOKENS])
+    total += dot(held[...].reshape(NZ * ROWS, (NX - 1) * TOKENS), scaled[TOKENS:])
     out[...] = total.astype(BF16).reshape(NZ, ROWS, 2 * HD)
 
 
@@ -228,7 +210,7 @@
             pltpu.VMEM((NZ, ROWS, (NX - 1) * TOKENS), BF16),
             pltpu.SemaphoreType.DMA((2 * (NX - 1),)),
         ],
-        compiler_params=pltpu.CompilerParams(vmem_limit_bytes=VMEM_MOST),
+        compiler_params=pltpu.CompilerParams(vmem_limit_bytes=VMEM),
         cost_estimate=pl.CostEstimate(
             flops=2 * D * TOKENS * 2 * HD, bytes_accessed=3 * D * TOKENS, transcendentals=0
         ),
@@ -244,46 +226,42 @@
     return lax.optimization_barrier(arrays)
 
 
-def gather_features(shard):
+def gather(w, shard):
+    above = lambda a: hop(a, "z", NZ, 1)
+    below = lambda a: hop(a, "z", NZ, 7)
     at_first = lax.axis_index("core") == 0
     x = lax.axis_index("x")
-    up = [shard, hop(shard, "y", NY, 1)]
-    down = [shard, hop(shard, "y", NY, 7)]
-    up[1], down[1], part = together(up[1], down[1], shard)
+    x_t = lax.all_gather(shard, ("y", "core"), axis=0, tiled=True)
+    w, part = together(lax.all_gather(w, "x", axis=0, tiled=True), shard)
+
     first, second = part[:, :L], part[:, L:]
     keep = jnp.where(at_first, first, second)
     come = hop(jnp.where(at_first, second, first), "core", NC, 1)
-    up.append(hop(up[1], "y", NY, 1))
-    down.append(hop(down[1], "y", NY, 7))
-    up[2], down[2], come = together(up[2], down[2], come)
+    v1, e1, come = together(above(w), below(w), come)
+
     pair = jnp.where(at_first, jnp.concatenate([keep, come], 0), jnp.concatenate([come, keep], 0))
     piece = lambda k: lax.dynamic_slice_in_dim(pair, lax.rem(x + k, NX) * ROWS, ROWS, 0)
     owned = [hop(piece(NX - k), "x", NX, k) for k in range(1, NX)]
-    up.append(hop(up[2], "y", NY, 1))
-    down.append(hop(down[2], "y", NY, 7))
-    up[3], down[3], *owned = together(up[3], down[3], *owned)
-    up.append(hop(up[3], "y", NY, 1))
+    v2, e2, x_t, *owned = together(above(v1), below(e1), x_t, *owned)
     owned = lax.all_gather(jnp.stack(owned), ("y", "core"), axis=0)
-    return jnp.stack(up + down[:0:-1]), owned.reshape(NY, NC, NX - 1, ROWS, L)
+
+    v3, e3 = together(above(v2), below(e2))
+    far = [above(v3[:SHARD]), below(e3[SHARD:])]
+    return [w, v1, v2, v3, *far, e3, e2, e1], x_t, owned.reshape(NY, NC, NX - 1, ROWS, L)
 
 
 def body(inputs, w_query, w_key, w_value, cotangent, lengths, sampled, step, tree_noise):
     w = jnp.concatenate([w_query, w_key, w_value], 1)
-    w = lax.all_gather(w, "x", axis=0, tiled=True)
-    w, shard = together(w, inputs.T)
-    w = lax.all_gather(w, "z", axis=0, tiled=True)
-
-    mine, owned = gather_features(shard)
-    other = hop(mine, "core", NC, 1)
-    place = jnp.stack([lax.axis_index(a) for a in ("y", "core", "x")]).astype(jnp.int32)
-    gram, own = gram_of(place, mine, other)
+    w, x_t, owned = gather(w, inputs.T)
+    place = jnp.stack([lax.axis_index(a) for a in ("y", "core", "x", "z")]).astype(jnp.int32)
+    x_tok, gram, own = arrange(place, x_t)
 
     cosine, sine = rope_tables(L, HD)
     grads, norms = attend(
-        jnp.concatenate([lengths, sampled]), place, mine, other, w, cotangent, cosine, sine, gram
+        jnp.concatenate([lengths, sampled]), x_tok, w, cotangent, cosine, sine, gram
     )
     grads = [grads] + [hop(grads, "x", NX, k) for k in range(1, NX)]
-    norms = lax.psum(norms, "core")
+    norms, owned = together(lax.psum(norms, "core"), owned)
     norms = lax.all_to_all(jnp.broadcast_to(norms, (NX * NY, 4, HD)), ("x", "y"), 0, 0)
     scaled = clip(place, norms.reshape(NX, NY, 4, HD), grads)
     terms = gradient(owned, own, scaled)

time: 178 us -> 171 us (0.961)
  blocking collectives: 33.5 us -> 19.7 us
  waiting for transfers between devices: 40.4 us -> 48.6 us
  Pallas kernels: 19.7 us -> 12.2 us
  starting transfers between devices: 59.3 us -> 65 us
    all_to_all x1 -> x0, blocking collectives: 17.5 us -> none  [body(): lax.all_to_all(jnp.broadcast_to(norms, (NX * NY, 4, HD)), ('x', 'y'), 0, 0)]
    all_to_all x0 -> x1, starting transfers between devices: none -> 9.28 us  [body(): lax.all_to_all(jnp.broadcast_to(norms, (NX * NY, 4, HD)), ('x', 'y'), 0, 0)]
    all_to_all x0 -> x1, waiting for transfers between devices: none -> 8.93 us  [body(): lax.all_to_all(jnp.broadcast_to(norms, (NX * NY, 4, HD)), ('x', 'y'), 0, 0)]
    psum x1, blocking collectives: 3.38 us -> 8.54 us  [body(): norms, owned = together(lax.psum(norms, 'core'), owned)]
    pallas_call x1, Pallas kernels: 6.6 us -> 2.62 us  [gradient(): pl.pallas_call(gradient_kernel, in_specs=[pl.BlockSpec(memory_space=pl.AN...]
    pallas_call x2, Pallas kernels: 12.2 us -> 8.33 us  [the longest x1 6.08 us: attend(): pl.pallas_call(attend_kernel, in_specs=[pl.BlockSpec(memory_space=pltpu.S...]
    ppermute x15, waiting for transfers between devices: 18.4 us -> 22.2 us  [hop(): return lax.ppermute(a, axis, ring(size, k))]
    all_to_all x1, starting transfers between devices: 7.2 us -> 3.55 us  [body(): terms = lax.all_to_all(terms, 'z', 0, 0)]
  transfers between devices with their start and end apart: 18 -> 19, of which waited for: 9 -> 10; matrix products, arithmetic and copies ran while one was open for 3% -> 2% of each run, Pallas kernels for 7% -> 5%
where the time goes in v4:
time: 171 us
  starting transfers between devices  65 us (38%)
  waiting for transfers between devices  48.6 us (28%)
  blocking collectives  19.7 us (12%)
  between operations  15.1 us (9%)
  Pallas kernels  12.2 us (7%)
  local copies, waits for them, and re-layouts  5.15 us (3%)
  other arithmetic  4.76 us (3%)
    ppermute x15, starting transfers between devices, hop(): return lax.ppermute(a, axis, ring(size, k))  52 us
    ppermute x15, waiting for transfers between devices, hop(): return lax.ppermute(a, axis, ring(size, k))  22.2 us
    all_to_all x1, waiting for transfers between devices, body(): terms = lax.all_to_all(terms, 'z', 0, 0)  16.8 us
    all_gather x1, blocking collectives, gather(): w, part = together(lax.all_gather(w, 'x', axis=0, tiled=True), shard)  11.2 us
    all_to_all x1, starting transfers between devices, body(): lax.all_to_all(jnp.broadcast_to(norms, (NX * NY, 4, HD)), ('x', 'y'), 0, 0)  9.28 us
    all_to_all x1, waiting for transfers between devices, body(): lax.all_to_all(jnp.broadcast_to(norms, (NX * NY, 4, HD)), ('x', 'y'), 0, 0)  8.93 us
    psum x1, blocking collectives, body(): norms, owned = together(lax.psum(norms, 'core'), owned)  8.54 us
    pallas_call x1, Pallas kernels, attend(): pl.pallas_call(attend_kernel, in_specs=[pl.BlockSpec(memory_space=pltpu.S...  6.08 us
  transfers between devices with their start and end apart: 19, of which 10 were waited for; matrix products, arithmetic and copies ran while one was open for 2% of the time, Pallas kernels for 5%

profile of v4, /device:TPU:1, one launch (start us, length us, event | category | flops | bytes accessed | tf_op | source)
XLA Modules:
  0.0 170.5 jit_solution(19786876240136376)
XLA Ops:
  8.9 11.2 %all_gather.12.refs_0_ = bf16[576,512]{1,0:T(8,128)(2,1)S(1)} all-gather(bf16[144,512]{1,0:T(8,128)(2,1)S(1)} %pad_maximum_fusion.1), channel_id=1, replica_groups=mesh['z'=8,'x'=4,'y'=8,'core'=2] {'x'}, dimensions={0}, use_global_device_ids=true | all-gather | bytes 737280 | tf_op jit(solution)/shard_map/all_gather | solution.py:235
  20.1 11.9 %collective-permute-start = (bf16[576,512]{1,0:T(8,128)(2,1)S(1)}, bf16[576,512]{1,0:T(8,128)(2,1)S(1)}, u32[]{:S(2)}, u32[]{:S(2)}) collective-permute-start(bf16[576,512]{1,0:T(8,128)(2,1)S(1)} %all_gather.12.refs_0_), channel_id=1, source_target_pairs={{64,0},{128,64},{192,128},{256,192},{320,256},{384,320},{448,384},... | collective-permute-start | bytes 1769480 | tf_op jit(solution)/shard_map/ppermute | solution.py:222
  35.0 4.5 %collective-permute-start.2 = (bf16[288,256]{1,0:T(8,128)(2,1)S(1)}, bf16[288,256]{1,0:T(8,128)(2,1)S(1)}, u32[]{:S(2)}, u32[]{:S(2)}) collective-permute-start(bf16[288,256]{1,0:T(8,128)(2,1)S(1)} %get-tuple-element.48), channel_id=1, source_target_pairs={{1,0},{0,1},{3,2},{2,3},{5,4},{4,5},{7,6},{6,7},{9,8},{8,9},{11,10... | collective-permute-start | bytes 442376 | tf_op jit(solution)/shard_map/ppermute | solution.py:222
  42.4 5.2 %collective-permute-done.1.refs_8_ = bf16[576,512]{1,0:T(8,128)(2,1)S(1)} collective-permute-done((bf16[576,512]{1,0:T(8,128)(2,1)S(1)}, bf16[576,512]{1,0:T(8,128)(2,1)S(1)}, u32[]{:S(2)}, u32[]{:S(2)}) %collective-permute-start.1) | collective-permute-done | bytes 589856 | tf_op jit(solution)/shard_map/ppermute | solution.py:222
  49.4 3.4 %collective-permute-start.4 = (bf16[576,512]{1,0:T(8,128)(2,1)S(1)}, bf16[576,512]{1,0:T(8,128)(2,1)S(1)}, u32[]{:S(2)}, u32[]{:S(2)}) collective-permute-start(bf16[576,512]{1,0:T(8,128)(2,1)S(1)} %collective-permute-done.1.refs_8_), channel_id=1, source_target_pairs={{448,0},{0,64},{64,128},{128,192},{192,256},{256,320},{320,384},{3... | collective-permute-start | bytes 1769480 | tf_op jit(solution)/shard_map/ppermute | solution.py:222
  54.9 3.1 %collective-permute-start.6 = (bf16[144,256]{1,0:T(8,128)(2,1)S(1)}, bf16[144,256]{1,0:T(8,128)(2,1)S(1)}, u32[]{:S(2)}, u32[]{:S(2)}) collective-permute-start(bf16[144,256]{1,0:T(8,128)(2,1)S(1)} %get-tuple-element.45), channel_id=1, source_target_pairs={{32,0},{48,16},{0,32},{16,48},{33,1},{49,17},{1,33},{17,49},{34,2}... | collective-permute-start | bytes 221192 | tf_op jit(solution)/shard_map/ppermute | solution.py:222
  58.0 2.8 %collective-permute-start.7 = (bf16[144,256]{1,0:T(8,128)(2,1)S(1)}, bf16[144,256]{1,0:T(8,128)(2,1)S(1)}, u32[]{:S(2)}, u32[]{:S(2)}) collective-permute-start(bf16[144,256]{1,0:T(8,128)(2,1)S(1)} %get-tuple-element.44), channel_id=1, source_target_pairs={{48,0},{0,16},{16,32},{32,48},{49,1},{1,17},{17,33},{33,49},{50,2}... | collective-permute-start | bytes 221192 | tf_op jit(solution)/shard_map/ppermute | solution.py:222
  61.5 3.1 %collective-permute-done.7 = bf16[144,256]{1,0:T(8,128)(2,1)S(1)} collective-permute-done((bf16[144,256]{1,0:T(8,128)(2,1)S(1)}, bf16[144,256]{1,0:T(8,128)(2,1)S(1)}, u32[]{:S(2)}, u32[]{:S(2)}) %collective-permute-start.7) | collective-permute-done | bytes 73760 | tf_op jit(solution)/shard_map/ppermute | solution.py:222
  65.6 3.1 %collective-permute-start.8 = (bf16[576,512]{1,0:T(8,128)(2,1)S(1)}, bf16[576,512]{1,0:T(8,128)(2,1)S(1)}, u32[]{:S(2)}, u32[]{:S(2)}) collective-permute-start(bf16[576,512]{1,0:T(8,128)(2,1)S(1)} %collective-permute-done.3.refs_2_), channel_id=1, source_target_pairs={{64,0},{128,64},{192,128},{256,192},{320,256},{384,320},{448,384},... | collective-permute-start | bytes 1769480 | tf_op jit(solution)/shard_map/ppermute | solution.py:222
  71.5 5.2 %collective-permute-done.8.refs_3_ = bf16[576,512]{1,0:T(8,128)(2,1)S(1)} collective-permute-done((bf16[576,512]{1,0:T(8,128)(2,1)S(1)}, bf16[576,512]{1,0:T(8,128)(2,1)S(1)}, u32[]{:S(2)}, u32[]{:S(2)}) %collective-permute-start.8) | collective-permute-done | bytes 589856 | tf_op jit(solution)/shard_map/ppermute | solution.py:222
  76.7 4.3 %collective-permute-done.9.refs_6_ = bf16[576,512]{1,0:T(8,128)(2,1)S(1)} collective-permute-done((bf16[576,512]{1,0:T(8,128)(2,1)S(1)}, bf16[576,512]{1,0:T(8,128)(2,1)S(1)}, u32[]{:S(2)}, u32[]{:S(2)}) %collective-permute-start.9) | collective-permute-done | bytes 589856 | tf_op jit(solution)/shard_map/ppermute | solution.py:222
  83.0 3.4 %collective-permute-start.11 = (bf16[288,512]{1,0:T(8,128)(2,1)S(1)}, bf16[288,512]{1,0:T(8,128)(2,1)S(1)}, u32[]{:S(2)}, u32[]{:S(2)}) collective-permute-start(bf16[288,512]{1,0:T(8,128)(2,1)S(1)} %slice.27), channel_id=1, source_target_pairs={{448,0},{0,64},{64,128},{128,192},{192,256},{256,320},{320,384},{3... | collective-permute-start | bytes 884744 | tf_op jit(solution)/shard_map/ppermute | solution.py:222
  86.6 2.4 %copy-done = bf16[4608,512]{1,0:T(8,128)(2,1)S(1)} copy-done((bf16[4608,512]{1,0:T(8,128)(2,1)S(1)}, bf16[4608,512]{1,0:T(8,128)(2,1)}, u32[]{:S(2)}) %copy-start) | copy-done | bytes 4718616
  89.1 2.2 %arrange.1 = (bf16[512,4608]{1,0:T(8,128)(2,1)S(1)}, f32[2,256,256]{2,1,0:T(8,128)S(1)}, bf16[8,144,512]{2,1,0:T(8,128)(2,1)S(1)}) custom-call(s32[4]{0:T(128)S(1)} %pad_add_fusion.1.place, bf16[4608,512]{1,0:T(8,128)(2,1)S(1)} %copy-done), custom_call_target="tpu_custom_call" | custom-call | flops 1207959552 | bytes 9437184 | tf_op jit(solution)/shard_map/arrange/pallas_call | solution.py:71
  92.1 6.1 %attend.1 = (bf16[512,256]{1,0:T(8,128)(2,1)}, f32[4,128]{1,0:T(4,128)S(1)}) custom-call(s32[4]{0:T(128)S(1)} %pad_add_fusion.info, bf16[512,4608]{1,0:T(8,128)(2,1)S(1)} %get-tuple-element.28.x_tok, bf16[576,512]{1,0:T(8,128)(2,1)S(1)} %all_gather.12.refs_0_, bf16[576,512]{1,0:T(8,128)(2,1)S(1)} %collective-permute-done.refs_1_, ...), custom_call_target="tpu_custom_call" | custom-call | flops 2818572288 | bytes 9437184 | tf_op jit(solution)/shard_map/attend/pallas_call | solution.py:138
  98.2 5.1 %collective-permute-start.12 = (bf16[512,256]{1,0:T(8,128)(2,1)}, bf16[512,256]{1,0:T(8,128)(2,1)S(1)}, u32[]{:S(2)}, u32[]{:S(2)}) collective-permute-start(bf16[512,256]{1,0:T(8,128)(2,1)} %get-tuple-element.41.refs_0_), channel_id=1, source_target_pairs={{16,0},{32,16},{48,32},{0,48},{17,1},{33,17},{49,33},{1,49},{18,2}... | collective-permute-start | bytes 786440 | tf_op jit(solution)/shard_map/ppermute | solution.py:222
  103.3 2.8 %collective-permute-start.13 = (bf16[512,256]{1,0:T(8,128)(2,1)}, bf16[512,256]{1,0:T(8,128)(2,1)S(1)}, u32[]{:S(2)}, u32[]{:S(2)}) collective-permute-start(bf16[512,256]{1,0:T(8,128)(2,1)} %get-tuple-element.41.refs_0_), channel_id=1, source_target_pairs={{32,0},{48,16},{0,32},{16,48},{33,1},{49,17},{1,33},{17,49},{34,2}... | collective-permute-start | bytes 786440 | tf_op jit(solution)/shard_map/ppermute | solution.py:222
  106.1 2.2 %collective-permute-start.14 = (bf16[512,256]{1,0:T(8,128)(2,1)}, bf16[512,256]{1,0:T(8,128)(2,1)S(1)}, u32[]{:S(2)}, u32[]{:S(2)}) collective-permute-start(bf16[512,256]{1,0:T(8,128)(2,1)} %get-tuple-element.41.refs_0_), channel_id=1, source_target_pairs={{48,0},{0,16},{16,32},{32,48},{49,1},{1,17},{17,33},{33,49},{50,2}... | collective-permute-start | bytes 786440 | tf_op jit(solution)/shard_map/ppermute | solution.py:222
  108.3 8.5 %psum.7 = f32[4,128]{1,0:T(4,128)S(1)} all-reduce(f32[4,128]{1,0:T(4,128)S(1)} %get-tuple-element.34), channel_id=1, replica_groups=mesh['z'=8,'x'=4,'y'=8,'core'=2] {'core'}, use_global_device_ids=true, to_apply=%region_0.1 | all-reduce | flops 512 | bytes 4096 | tf_op jit(solution)/shard_map/psum | solution.py:264
  117.5 9.3 %all-to-all-start = ((f32[32,4,128]{2,1,0:T(4,128)}), f32[32,4,128]{2,1,0:T(4,128)S(1)}, u32[]{:S(2)}, u32[]{:S(2)}) async-start(f32[32,4,128]{2,1,0:T(4,128)} %broadcast_in_dim.4), calls=%async_computation | async-start | bytes 131072 | tf_op jit(solution)/shard_map/all_to_all | solution.py:265
  126.8 8.9 %all-to-all-done = f32[32,4,128]{2,1,0:T(4,128)S(1)} async-done(((f32[32,4,128]{2,1,0:T(4,128)}), f32[32,4,128]{2,1,0:T(4,128)S(1)}, u32[]{:S(2)}, u32[]{:S(2)}) %all-to-all-start) | async-done | bytes 65568 | tf_op jit(solution)/shard_map/all_to_all | solution.py:265
  139.1 2.6 %gradient.1 = bf16[8,144,256]{2,1,0:T(8,128)(2,1)} custom-call(bf16[8,2,3,144,256]{4,3,2,1,0:T(8,128)(2,1)S(1)} %bitcast.21, bf16[8,144,512]{2,1,0:T(8,128)(2,1)S(1)} %get-tuple-element.39.own, bf16[2048,256]{1,0:T(8,128)(2,1)S(1)} %clip.1.scaled), custom_call_target="tpu_custom_call" | custom-call | flops 1207959552 | bytes 7077888 | tf_op jit(solution)/shard_map/gradient/pallas_call | solution.py:204
  141.7 3.5 %all-to-all-start.1 = ((bf16[8,144,256]{2,1,0:T(8,128)(2,1)}), bf16[8,144,256]{2,1,0:T(8,128)(2,1)S(1)}, u32[]{:S(2)}, u32[]{:S(2)}) async-start(bf16[8,144,256]{2,1,0:T(8,128)(2,1)} %gradient.1), calls=%async_computation.1 | async-start | bytes 1179648 | tf_op jit(solution)/shard_map/all_to_all | solution.py:268
  146.2 16.8 %all-to-all-done.1 = bf16[8,144,256]{2,1,0:T(8,128)(2,1)S(1)} async-done(((bf16[8,144,256]{2,1,0:T(8,128)(2,1)}), bf16[8,144,256]{2,1,0:T(8,128)(2,1)S(1)}, u32[]{:S(2)}, u32[]{:S(2)}) %all-to-all-start.1) | async-done | bytes 589856 | tf_op jit(solution)/shard_map/all_to_all | solution.py:268
  (63 shorter events, 23.8 us)
Async XLA Ops:
  7.2 63.8 %copy-start.11 = (s32[2]{0:T(128)S(1)}, s32[2]{0:T(128)}, u32[]{:S(2)}) copy-start(s32[2]{0:T(128)} %param.14) | copy-start | bytes 28
  7.2 63.8 %copy-start.10 = (s32[2]{0:T(128)S(1)}, s32[2]{0:T(128)}, u32[]{:S(2)}) copy-start(s32[2]{0:T(128)} %param.15) | copy-start | bytes 28
  7.2 57.5 %all-gather.4.cloned.1.call-start = ((), (), s32[]{:S(2)}) async-start(), calls=%async_computation.2 | async-start | bytes 5013504 | tf_op jit(solution)/shard_map/all_gather | solution.py:234
  7.9 108.9 %all-gather.6.cloned.1.call-start = ((), (), s32[]{:S(2)}) async-start(), calls=%async_computation.3 | async-start | bytes 3760128 | tf_op jit(solution)/shard_map/all_gather | solution.py:246
  20.1 22.3 %collective-permute-start = (bf16[576,512]{1,0:T(8,128)(2,1)S(1)}, bf16[576,512]{1,0:T(8,128)(2,1)S(1)}, u32[]{:S(2)}, u32[]{:S(2)}) collective-permute-start(bf16[576,512]{1,0:T(8,128)(2,1)S(1)} %all_gather.12.refs_0_), channel_id=1, source_target_pairs={{64,0},{128,64},{192,128},{256,192},{320,256},{384,320},{448,384},... | collective-permute-start | bytes 1769480 | tf_op jit(solution)/shard_map/ppermute | solution.py:222
  32.1 15.5 %collective-permute-start.1 = (bf16[576,512]{1,0:T(8,128)(2,1)S(1)}, bf16[576,512]{1,0:T(8,128)(2,1)S(1)}, u32[]{:S(2)}, u32[]{:S(2)}) collective-permute-start(bf16[576,512]{1,0:T(8,128)(2,1)S(1)} %all_gather.12.refs_0_), channel_id=1, source_target_pairs={{448,0},{0,64},{64,128},{128,192},{192,256},{256,320},{320,384},{3... | collective-permute-start | bytes 1769480 | tf_op jit(solution)/shard_map/ppermute | solution.py:222
  35.0 5.5 %collective-permute-start.2 = (bf16[288,256]{1,0:T(8,128)(2,1)S(1)}, bf16[288,256]{1,0:T(8,128)(2,1)S(1)}, u32[]{:S(2)}, u32[]{:S(2)}) collective-permute-start(bf16[288,256]{1,0:T(8,128)(2,1)S(1)} %get-tuple-element.48), channel_id=1, source_target_pairs={{1,0},{0,1},{3,2},{2,3},{5,4},{4,5},{7,6},{6,7},{9,8},{8,9},{11,10... | collective-permute-start | bytes 442376 | tf_op jit(solution)/shard_map/ppermute | solution.py:222
  47.5 17.1 %collective-permute-start.3 = (bf16[576,512]{1,0:T(8,128)(2,1)S(1)}, bf16[576,512]{1,0:T(8,128)(2,1)S(1)}, u32[]{:S(2)}, u32[]{:S(2)}) collective-permute-start(bf16[576,512]{1,0:T(8,128)(2,1)S(1)} %collective-permute-done.refs_1_), channel_id=1, source_target_pairs={{64,0},{128,64},{192,128},{256,192},{320,256},{384,320},{448,384},... | collective-permute-start | bytes 1769480 | tf_op jit(solution)/shard_map/ppermute | solution.py:222
  49.4 15.2 %collective-permute-start.4 = (bf16[576,512]{1,0:T(8,128)(2,1)S(1)}, bf16[576,512]{1,0:T(8,128)(2,1)S(1)}, u32[]{:S(2)}, u32[]{:S(2)}) collective-permute-start(bf16[576,512]{1,0:T(8,128)(2,1)S(1)} %collective-permute-done.1.refs_8_), channel_id=1, source_target_pairs={{448,0},{0,64},{64,128},{128,192},{192,256},{256,320},{320,384},{3... | collective-permute-start | bytes 1769480 | tf_op jit(solution)/shard_map/ppermute | solution.py:222
  53.0 7.8 %collective-permute-start.5 = (bf16[144,256]{1,0:T(8,128)(2,1)S(1)}, bf16[144,256]{1,0:T(8,128)(2,1)S(1)}, u32[]{:S(2)}, u32[]{:S(2)}) collective-permute-start(bf16[144,256]{1,0:T(8,128)(2,1)S(1)} %get-tuple-element.46), channel_id=1, source_target_pairs={{16,0},{32,16},{48,32},{0,48},{17,1},{33,17},{49,33},{1,49},{18,2}... | collective-permute-start | bytes 221192 | tf_op jit(solution)/shard_map/ppermute | solution.py:222
  54.9 6.6 %collective-permute-start.6 = (bf16[144,256]{1,0:T(8,128)(2,1)S(1)}, bf16[144,256]{1,0:T(8,128)(2,1)S(1)}, u32[]{:S(2)}, u32[]{:S(2)}) collective-permute-start(bf16[144,256]{1,0:T(8,128)(2,1)S(1)} %get-tuple-element.45), channel_id=1, source_target_pairs={{32,0},{48,16},{0,32},{16,48},{33,1},{49,17},{1,33},{17,49},{34,2}... | collective-permute-start | bytes 221192 | tf_op jit(solution)/shard_map/ppermute | solution.py:222
  58.0 6.6 %collective-permute-start.7 = (bf16[144,256]{1,0:T(8,128)(2,1)S(1)}, bf16[144,256]{1,0:T(8,128)(2,1)S(1)}, u32[]{:S(2)}, u32[]{:S(2)}) collective-permute-start(bf16[144,256]{1,0:T(8,128)(2,1)S(1)} %get-tuple-element.44), channel_id=1, source_target_pairs={{48,0},{0,16},{16,32},{32,48},{49,1},{1,17},{17,33},{33,49},{50,2}... | collective-permute-start | bytes 221192 | tf_op jit(solution)/shard_map/ppermute | solution.py:222
  64.6 21.9 %copy-start.4 = (bf16[576,512]{1,0:T(8,128)(2,1)}, bf16[576,512]{1,0:T(8,128)(2,1)S(1)}, u32[]{:S(2)}) copy-start(bf16[576,512]{1,0:T(8,128)(2,1)S(1)} %collective-permute-done.3.refs_2_) | copy-start | bytes 1769476
  64.6 21.9 %copy-start.6 = (bf16[576,512]{1,0:T(8,128)(2,1)}, bf16[576,512]{1,0:T(8,128)(2,1)S(1)}, u32[]{:S(2)}) copy-start(bf16[576,512]{1,0:T(8,128)(2,1)S(1)} %collective-permute-done.4.refs_7_) | copy-start | bytes 1769476
  65.6 11.1 %collective-permute-start.8 = (bf16[576,512]{1,0:T(8,128)(2,1)S(1)}, bf16[576,512]{1,0:T(8,128)(2,1)S(1)}, u32[]{:S(2)}, u32[]{:S(2)}) collective-permute-start(bf16[576,512]{1,0:T(8,128)(2,1)S(1)} %collective-permute-done.3.refs_2_), channel_id=1, source_target_pairs={{64,0},{128,64},{192,128},{256,192},{320,256},{384,320},{448,384},... | collective-permute-start | bytes 1769480 | tf_op jit(solution)/shard_map/ppermute | solution.py:222
  68.7 12.3 %collective-permute-start.9 = (bf16[576,512]{1,0:T(8,128)(2,1)S(1)}, bf16[576,512]{1,0:T(8,128)(2,1)S(1)}, u32[]{:S(2)}, u32[]{:S(2)}) collective-permute-start(bf16[576,512]{1,0:T(8,128)(2,1)S(1)} %collective-permute-done.4.refs_7_), channel_id=1, source_target_pairs={{448,0},{0,64},{64,128},{128,192},{192,256},{256,320},{320,384},{3... | collective-permute-start | bytes 1769480 | tf_op jit(solution)/shard_map/ppermute | solution.py:222
  70.9 21.2 %copy-start.3 = (bf16[576,512]{1,0:T(8,128)(2,1)S(1)}, bf16[576,512]{1,0:T(8,128)(2,1)}, u32[]{:S(2)}) copy-start(bf16[576,512]{1,0:T(8,128)(2,1)} %copy-done.2) | copy-start | bytes 1769476
  81.1 10.2 %collective-permute-start.10 = (bf16[288,512]{1,0:T(8,128)(2,1)S(1)}, bf16[288,512]{1,0:T(8,128)(2,1)S(1)}, u32[]{:S(2)}, u32[]{:S(2)}) collective-permute-start(bf16[288,512]{1,0:T(8,128)(2,1)S(1)} %slice.26), channel_id=1, source_target_pairs={{64,0},{128,64},{192,128},{256,192},{320,256},{384,320},{448,384},... | collective-permute-start | bytes 884744 | tf_op jit(solution)/shard_map/ppermute | solution.py:222
  83.0 9.1 %collective-permute-start.11 = (bf16[288,512]{1,0:T(8,128)(2,1)S(1)}, bf16[288,512]{1,0:T(8,128)(2,1)S(1)}, u32[]{:S(2)}, u32[]{:S(2)}) collective-permute-start(bf16[288,512]{1,0:T(8,128)(2,1)S(1)} %slice.27), channel_id=1, source_target_pairs={{448,0},{0,64},{64,128},{128,192},{192,256},{256,320},{320,384},{3... | collective-permute-start | bytes 884744 | tf_op jit(solution)/shard_map/ppermute | solution.py:222
  98.2 28.6 %collective-permute-start.12 = (bf16[512,256]{1,0:T(8,128)(2,1)}, bf16[512,256]{1,0:T(8,128)(2,1)S(1)}, u32[]{:S(2)}, u32[]{:S(2)}) collective-permute-start(bf16[512,256]{1,0:T(8,128)(2,1)} %get-tuple-element.41.refs_0_), channel_id=1, source_target_pairs={{16,0},{32,16},{48,32},{0,48},{17,1},{33,17},{49,33},{1,49},{18,2}... | collective-permute-start | bytes 786440 | tf_op jit(solution)/shard_map/ppermute | solution.py:222
  103.3 23.5 %collective-permute-start.13 = (bf16[512,256]{1,0:T(8,128)(2,1)}, bf16[512,256]{1,0:T(8,128)(2,1)S(1)}, u32[]{:S(2)}, u32[]{:S(2)}) collective-permute-start(bf16[512,256]{1,0:T(8,128)(2,1)} %get-tuple-element.41.refs_0_), channel_id=1, source_target_pairs={{32,0},{48,16},{0,32},{16,48},{33,1},{49,17},{1,33},{17,49},{34,2}... | collective-permute-start | bytes 786440 | tf_op jit(solution)/shard_map/ppermute | solution.py:222
  106.1 20.7 %collective-permute-start.14 = (bf16[512,256]{1,0:T(8,128)(2,1)}, bf16[512,256]{1,0:T(8,128)(2,1)S(1)}, u32[]{:S(2)}, u32[]{:S(2)}) collective-permute-start(bf16[512,256]{1,0:T(8,128)(2,1)} %get-tuple-element.41.refs_0_), channel_id=1, source_target_pairs={{48,0},{0,16},{16,32},{32,48},{49,1},{1,17},{17,33},{33,49},{50,2}... | collective-permute-start | bytes 786440 | tf_op jit(solution)/shard_map/ppermute | solution.py:222
  117.5 18.2 %all-to-all-start = ((f32[32,4,128]{2,1,0:T(4,128)}), f32[32,4,128]{2,1,0:T(4,128)S(1)}, u32[]{:S(2)}, u32[]{:S(2)}) async-start(f32[32,4,128]{2,1,0:T(4,128)} %broadcast_in_dim.4), calls=%async_computation | async-start | bytes 131072 | tf_op jit(solution)/shard_map/all_to_all | solution.py:265
  141.7 21.2 %all-to-all-start.1 = ((bf16[8,144,256]{2,1,0:T(8,128)(2,1)}), bf16[8,144,256]{2,1,0:T(8,128)(2,1)S(1)}, u32[]{:S(2)}, u32[]{:S(2)}) async-start(bf16[8,144,256]{2,1,0:T(8,128)(2,1)} %gradient.1), calls=%async_computation.1 | async-start | bytes 1179648 | tf_op jit(solution)/shard_map/all_to_all | solution.py:268
  (7 other events, 56.8 us)
Sparse Core Ops, SparseCore 0:
  10.1 51.2 all-gather.3
  65.7 44.6 all-gather.5

commit v5 on v4

--- a/solution.py
+++ b/solution.py
@@ -24,6 +24,7 @@
 SCALE = float(D // H) ** (-0.5)
 CLIP = 2.0 * math.sqrt(D * KV * HD)
 CHUNK = 2 * PAIR
+ORDER = (0, 1, 2, 3, 5, 6, 7, 4)
 VMEM = 32 * 1024 * 1024
 F32 = jnp.float32
 BF16 = jnp.bfloat16
@@ -55,7 +56,7 @@
         own[z] = x_t[pl.ds(pl.multiple_of(at, ROWS), ROWS)]
     for m in range(NZ // 2):
         parts = []
-        for r in (2 * m, 2 * m + 1):
+        for r in ORDER[2 * m : 2 * m + 2]:
             at = lax.rem(r + place[3], NZ) * PAIR
             parts.append(x_t[pl.ds(pl.multiple_of(at, PAIR), PAIR)])
         rows = jnp.concatenate(parts, 0).T
@@ -85,16 +86,32 @@
     )(place, x_t)
 
 
-def attend_kernel(info, x_tok, *refs):
-    w = refs[: NZ + 1]
-    cot, cosine, sine, gram, grads, norms, acc = refs[NZ + 1 :]
-    blocks = [w[r][...] for r in range(4)]
-    blocks += [jnp.concatenate([w[4][...], w[5][...]], 0)]
-    blocks += [w[r][...] for r in range(6, 9)]
-    for m in range(NZ // 2):
-        pair = jnp.concatenate(blocks[2 * m : 2 * m + 2], 0)
+def project_kernel(x_tok, *refs):
+    w, total = refs[: NZ - 2], refs[NZ - 2]
+    for m in range(NZ // 2 - 1):
+        pair = jnp.concatenate([w[2 * m][...], w[2 * m + 1][...]], 0)
         part = dot(x_tok[:, m * CHUNK : (m + 1) * CHUNK], pair)
-        acc[...] = part if m == 0 else acc[...] + part
+        total[...] = part if m == 0 else total[...] + part
+
+
+def project(x_tok, w):
+    vmem = pl.BlockSpec(memory_space=pltpu.VMEM)
+    return pl.pallas_call(
+        project_kernel,
+        in_specs=[vmem] * (NZ - 1),
+        out_specs=vmem,
+        out_shape=jax.ShapeDtypeStruct((TOKENS, 4 * HD), F32),
+        compiler_params=pltpu.CompilerParams(vmem_limit_bytes=VMEM),
+        cost_estimate=pl.CostEstimate(
+            flops=2 * TOKENS * 3 * HD * D, bytes_accessed=3 * D * TOKENS, transcendentals=0
+        ),
+        name="project",
+    )(x_tok, *w)
+
+
+def attend_kernel(info, total, x_tok, w, w_a, w_b, cot, cosine, sine, gram, grads, norms, acc):
+    pair = jnp.concatenate([w[...], w_a[...], w_b[...]], 0)
+    acc[...] = total[...] + dot(x_tok[:, D - CHUNK :], pair)
 
     cos = cosine[...]
     sin = sine[...]
@@ -133,11 +150,11 @@
             norms[2 * i + s : 2 * i + s + 1] = folded[:, :HD] + folded[:, HD:]
 
 
-def attend(info, x_tok, w, cot, cosine, sine, gram):
+def attend(info, total, x_tok, w, cot, cosine, sine, gram):
     vmem = pl.BlockSpec(memory_space=pltpu.VMEM)
     return pl.pallas_call(
         attend_kernel,
-        in_specs=[pl.BlockSpec(memory_space=pltpu.SMEM)] + [vmem] * (NZ + 6),
+        in_specs=[pl.BlockSpec(memory_space=pltpu.SMEM)] + [vmem] * 9,
         out_specs=[vmem] * 2,
         out_shape=[
             jax.ShapeDtypeStruct((TOKENS, 2 * HD), BF16),
@@ -151,7 +168,7 @@
             transcendentals=8 * L * L,
         ),
         name="attend",
-    )(info, x_tok, *w, cot, cosine, sine, gram)
+    )(info, total, x_tok, *w, cot, cosine, sine, gram)
 
 
 def clip_kernel(place, norms, *refs):
@@ -181,41 +198,53 @@
     )(place, norms, *grads)
 
 
-def gradient_kernel(features, own, scaled, out, held, sems):
+def stage_kernel(features, out, sems):
     def fetch(j, s):
         columns = pl.ds((2 * (j - 1) + s) * L, L)
         return pltpu.make_async_copy(
-            features.at[:, s, j - 1], held.at[:, :, columns], sems.at[2 * (j - 1) + s]
+            features.at[:, s, j - 1], out.at[:, :, columns], sems.at[2 * (j - 1) + s]
         )
 
     for j in range(1, NX):
         for s in range(2):
             fetch(j, s).start()
-    total = dot(own[...].reshape(NZ * ROWS, TOKENS), scaled[:TOKENS])
     for j in range(1, NX):
         for s in range(2):
             fetch(j, s).wait()
-    total += dot(held[...].reshape(NZ * ROWS, (NX - 1) * TOKENS), scaled[TOKENS:])
+
+
+def stage(features):
+    return pl.pallas_call(
+        stage_kernel,
+        in_specs=[pl.BlockSpec(memory_space=pl.ANY)],
+        out_specs=pl.BlockSpec(memory_space=pltpu.VMEM),
+        out_shape=jax.ShapeDtypeStruct((NZ, ROWS, (NX - 1) * TOKENS), BF16),
+        scratch_shapes=[pltpu.SemaphoreType.DMA((2 * (NX - 1),))],
+        compiler_params=pltpu.CompilerParams(vmem_limit_bytes=VMEM),
+        cost_estimate=pl.CostEstimate(flops=0, bytes_accessed=4 * D * TOKENS, transcendentals=0),
+        name="stage",
+    )(features)
+
+
+def gradient_kernel(staged, own, scaled, out):
+    total = dot(own[...].reshape(NZ * ROWS, TOKENS), scaled[:TOKENS])
+    total += dot(staged[...].reshape(NZ * ROWS, (NX - 1) * TOKENS), scaled[TOKENS:])
     out[...] = total.astype(BF16).reshape(NZ, ROWS, 2 * HD)
 
 
-def gradient(features, own, scaled):
+def gradient(staged, own, scaled):
     vmem = pl.BlockSpec(memory_space=pltpu.VMEM)
     return pl.pallas_call(
         gradient_kernel,
-        in_specs=[pl.BlockSpec(memory_space=pl.ANY)] + [vmem] * 2,
+        in_specs=[vmem] * 3,
         out_specs=vmem,
         out_shape=jax.ShapeDtypeStruct((NZ, ROWS, 2 * HD), BF16),
-        scratch_shapes=[
-            pltpu.VMEM((NZ, ROWS, (NX - 1) * TOKENS), BF16),
-            pltpu.SemaphoreType.DMA((2 * (NX - 1),)),
-        ],
         compiler_params=pltpu.CompilerParams(vmem_limit_bytes=VMEM),
         cost_estimate=pl.CostEstimate(
             flops=2 * D * TOKENS * 2 * HD, bytes_accessed=3 * D * TOKENS, transcendentals=0
         ),
         name="gradient",
-    )(features, own, scaled)
+    )(staged, own, scaled)
 
 
 def hop(a, axis, size, k):
@@ -246,25 +275,28 @@
     owned = lax.all_gather(jnp.stack(owned), ("y", "core"), axis=0)
 
     v3, e3 = together(above(v2), below(e2))
+    place = jnp.stack([lax.axis_index(a) for a in ("y", "core", "x", "z")]).astype(jnp.int32)
+    x_tok, gram, own = arrange(place, x_t)
+    v3, e3, gram = together(v3, e3, gram)
     far = [above(v3[:SHARD]), below(e3[SHARD:])]
-    return [w, v1, v2, v3, *far, e3, e2, e1], x_t, owned.reshape(NY, NC, NX - 1, ROWS, L)
+    total = project(x_tok, [w, v1, v2, v3, e3, e2])
+    owned = owned.reshape(NY, NC, NX - 1, ROWS, L)
+    return total, x_tok, [e1, *far], gram, own, owned, place
 
 
 def body(inputs, w_query, w_key, w_value, cotangent, lengths, sampled, step, tree_noise):
     w = jnp.concatenate([w_query, w_key, w_value], 1)
-    w, x_t, owned = gather(w, inputs.T)
-    place = jnp.stack([lax.axis_index(a) for a in ("y", "core", "x", "z")]).astype(jnp.int32)
-    x_tok, gram, own = arrange(place, x_t)
+    total, x_tok, w, gram, own, owned, place = gather(w, inputs.T)
 
     cosine, sine = rope_tables(L, HD)
     grads, norms = attend(
-        jnp.concatenate([lengths, sampled]), x_tok, w, cotangent, cosine, sine, gram
+        jnp.concatenate([lengths, sampled]), total, x_tok, w, cotangent, cosine, sine, gram
     )
     grads = [grads] + [hop(grads, "x", NX, k) for k in range(1, NX)]
     norms, owned = together(lax.psum(norms, "core"), owned)
     norms = lax.all_to_all(jnp.broadcast_to(norms, (NX * NY, 4, HD)), ("x", "y"), 0, 0)
     scaled = clip(place, norms.reshape(NX, NY, 4, HD), grads)
-    terms = gradient(owned, own, scaled)
+    terms = gradient(stage(owned), own, scaled)
     terms = lax.all_to_all(terms, "z", 0, 0)
     summed = jnp.sum(terms.astype(F32), 0)
 

time: 171 us -> 168 us (0.982)
  waiting for transfers between devices: 48.6 us -> 43.1 us
  local copies, waits for them, and re-layouts: 5.15 us -> 7.13 us
    all_to_all x1, waiting for transfers between devices: 8.93 us -> 6.56 us  [body(): lax.all_to_all(jnp.broadcast_to(norms, (NX * NY, 4, HD)), ('x', 'y'), 0, 0)]
    pallas_call x1, Pallas kernels: 6.08 us -> 4.02 us  [attend(): pl.pallas_call(attend_kernel, in_specs=[pl.BlockSpec(memory_space=pltpu.S...]
    ppermute x15, waiting for transfers between devices: 22.2 us -> 20.1 us  [hop(): return lax.ppermute(a, axis, ring(size, k))]
    unnamed x24 -> x20, local copies, waits for them, and re-layouts: 4.44 us -> 6.43 us
    pallas_call x1 -> x3, Pallas kernels: 2.62 us -> 3.91 us  [the longest x1 2.19 us: project(): pl.pallas_call(project_kernel, in_specs=[vmem] * (NZ - 1), out_specs=vmem...]
  transfers between devices with their start and end apart: 19 -> 19, of which waited for: 10 -> 11; matrix products, arithmetic and copies ran while one was open for 2% -> 3% of each run, Pallas kernels for 5% -> 5%
where the time goes in v5:
time: 168 us; the launch traced here: 167 us
  starting transfers between devices  65.1 us (39%)
  waiting for transfers between devices  43.1 us (26%)
  blocking collectives  19.7 us (12%)
  between operations  15.1 us (9%)
  Pallas kernels  11.7 us (7%)
  local copies, waits for them, and re-layouts  7.13 us (4%)
  other arithmetic  5.69 us (3%)
    ppermute x15, starting transfers between devices, hop(): return lax.ppermute(a, axis, ring(size, k))  52.2 us
    ppermute x15, waiting for transfers between devices, hop(): return lax.ppermute(a, axis, ring(size, k))  20.1 us
    all_to_all x1, waiting for transfers between devices, body(): terms = lax.all_to_all(terms, 'z', 0, 0)  15.7 us
    all_gather x1, blocking collectives, gather(): w, part = together(lax.all_gather(w, 'x', axis=0, tiled=True), shard)  11.2 us
    all_to_all x1, starting transfers between devices, body(): lax.all_to_all(jnp.broadcast_to(norms, (NX * NY, 4, HD)), ('x', 'y'), 0, 0)  9.26 us
    psum x1, blocking collectives, body(): norms, owned = together(lax.psum(norms, 'core'), owned)  8.5 us
    all_to_all x1, waiting for transfers between devices, body(): lax.all_to_all(jnp.broadcast_to(norms, (NX * NY, 4, HD)), ('x', 'y'), 0, 0)  6.56 us
    unnamed x20, local copies, waits for them, and re-layouts  6.43 us
  transfers between devices with their start and end apart: 19, of which 11 were waited for; matrix products, arithmetic and copies ran while one was open for 3% of the time, Pallas kernels for 5%

profile of v5, /device:TPU:1, one launch (start us, length us, event | category | flops | bytes accessed | tf_op | source)
XLA Modules:
  0.0 167.5 jit_solution(9243235479721522051)
XLA Ops:
  8.9 11.2 %all_gather.12.refs_0_ = bf16[576,512]{1,0:T(8,128)(2,1)S(1)} all-gather(bf16[144,512]{1,0:T(8,128)(2,1)S(1)} %pad_maximum_fusion.1), channel_id=1, replica_groups=mesh['z'=8,'x'=4,'y'=8,'core'=2] {'x'}, dimensions={0}, use_global_device_ids=true | all-gather | bytes 737280 | tf_op jit(solution)/shard_map/all_gather | solution.py:264
  20.1 11.9 %collective-permute-start = (bf16[576,512]{1,0:T(8,128)(2,1)S(1)}, bf16[576,512]{1,0:T(8,128)(2,1)S(1)}, u32[]{:S(2)}, u32[]{:S(2)}) collective-permute-start(bf16[576,512]{1,0:T(8,128)(2,1)S(1)} %all_gather.12.refs_0_), channel_id=1, source_target_pairs={{64,0},{128,64},{192,128},{256,192},{320,256},{384,320},{448,384},... | collective-permute-start | bytes 1769480 | tf_op jit(solution)/shard_map/ppermute | solution.py:251
  35.0 4.5 %collective-permute-start.2 = (bf16[288,256]{1,0:T(8,128)(2,1)S(1)}, bf16[288,256]{1,0:T(8,128)(2,1)S(1)}, u32[]{:S(2)}, u32[]{:S(2)}) collective-permute-start(bf16[288,256]{1,0:T(8,128)(2,1)S(1)} %get-tuple-element.54), channel_id=1, source_target_pairs={{1,0},{0,1},{3,2},{2,3},{5,4},{4,5},{7,6},{6,7},{9,8},{8,9},{11,10... | collective-permute-start | bytes 442376 | tf_op jit(solution)/shard_map/ppermute | solution.py:251
  42.4 5.2 %collective-permute-done.1.w = bf16[576,512]{1,0:T(8,128)(2,1)S(1)} collective-permute-done((bf16[576,512]{1,0:T(8,128)(2,1)S(1)}, bf16[576,512]{1,0:T(8,128)(2,1)S(1)}, u32[]{:S(2)}, u32[]{:S(2)}) %collective-permute-start.1) | collective-permute-done | bytes 589856 | tf_op jit(solution)/shard_map/ppermute | solution.py:251
  49.4 3.4 %collective-permute-start.4 = (bf16[576,512]{1,0:T(8,128)(2,1)S(1)}, bf16[576,512]{1,0:T(8,128)(2,1)S(1)}, u32[]{:S(2)}, u32[]{:S(2)}) collective-permute-start(bf16[576,512]{1,0:T(8,128)(2,1)S(1)} %collective-permute-done.1.w), channel_id=1, source_target_pairs={{448,0},{0,64},{64,128},{128,192},{192,256},{256,320},{320,384},{3... | collective-permute-start | bytes 1769480 | tf_op jit(solution)/shard_map/ppermute | solution.py:251
  55.1 3.0 %collective-permute-start.6 = (bf16[144,256]{1,0:T(8,128)(2,1)S(1)}, bf16[144,256]{1,0:T(8,128)(2,1)S(1)}, u32[]{:S(2)}, u32[]{:S(2)}) collective-permute-start(bf16[144,256]{1,0:T(8,128)(2,1)S(1)} %get-tuple-element.51), channel_id=1, source_target_pairs={{32,0},{48,16},{0,32},{16,48},{33,1},{49,17},{1,33},{17,49},{34,2}... | collective-permute-start | bytes 221192 | tf_op jit(solution)/shard_map/ppermute | solution.py:251
  58.0 2.8 %collective-permute-start.7 = (bf16[144,256]{1,0:T(8,128)(2,1)S(1)}, bf16[144,256]{1,0:T(8,128)(2,1)S(1)}, u32[]{:S(2)}, u32[]{:S(2)}) collective-permute-start(bf16[144,256]{1,0:T(8,128)(2,1)S(1)} %get-tuple-element.50), channel_id=1, source_target_pairs={{48,0},{0,16},{16,32},{32,48},{49,1},{1,17},{17,33},{33,49},{50,2}... | collective-permute-start | bytes 221192 | tf_op jit(solution)/shard_map/ppermute | solution.py:251
  61.7 3.1 %collective-permute-done.7 = bf16[144,256]{1,0:T(8,128)(2,1)S(1)} collective-permute-done((bf16[144,256]{1,0:T(8,128)(2,1)S(1)}, bf16[144,256]{1,0:T(8,128)(2,1)S(1)}, u32[]{:S(2)}, u32[]{:S(2)}) %collective-permute-start.7) | collective-permute-done | bytes 73760 | tf_op jit(solution)/shard_map/ppermute | solution.py:251
  65.5 3.1 %collective-permute-start.8 = (bf16[576,512]{1,0:T(8,128)(2,1)S(1)}, bf16[576,512]{1,0:T(8,128)(2,1)S(1)}, u32[]{:S(2)}, u32[]{:S(2)}) collective-permute-start(bf16[576,512]{1,0:T(8,128)(2,1)S(1)} %collective-permute-done.3.refs_2_), channel_id=1, source_target_pairs={{64,0},{128,64},{192,128},{256,192},{320,256},{384,320},{448,384},... | collective-permute-start | bytes 1769480 | tf_op jit(solution)/shard_map/ppermute | solution.py:251
  71.5 2.3 %copy-done = bf16[4608,512]{1,0:T(8,128)(2,1)S(1)} copy-done((bf16[4608,512]{1,0:T(8,128)(2,1)S(1)}, bf16[4608,512]{1,0:T(8,128)(2,1)}, u32[]{:S(2)}) %copy-start) | copy-done | bytes 4718616
  73.8 2.2 %arrange.1 = (bf16[512,4608]{1,0:T(8,128)(2,1)S(1)}, f32[2,256,256]{2,1,0:T(8,128)S(1)}, bf16[8,144,512]{2,1,0:T(8,128)(2,1)S(1)}) custom-call(s32[4]{0:T(128)S(1)} %pad_add_fusion.1.place, bf16[4608,512]{1,0:T(8,128)(2,1)S(1)} %copy-done), custom_call_target="tpu_custom_call" | custom-call | flops 1207959552 | bytes 9437184 | tf_op jit(solution)/shard_map/arrange/pallas_call | solution.py:72
  76.8 4.2 %collective-permute-done.9.refs_4_ = bf16[576,512]{1,0:T(8,128)(2,1)S(1)} collective-permute-done((bf16[576,512]{1,0:T(8,128)(2,1)S(1)}, bf16[576,512]{1,0:T(8,128)(2,1)S(1)}, u32[]{:S(2)}, u32[]{:S(2)}) %collective-permute-start.9) | collective-permute-done | bytes 589856 | tf_op jit(solution)/shard_map/ppermute | solution.py:251
  83.0 3.4 %collective-permute-start.11 = (bf16[288,512]{1,0:T(8,128)(2,1)S(1)}, bf16[288,512]{1,0:T(8,128)(2,1)S(1)}, u32[]{:S(2)}, u32[]{:S(2)}) collective-permute-start(bf16[288,512]{1,0:T(8,128)(2,1)S(1)} %slice.27), channel_id=1, source_target_pairs={{448,0},{0,64},{64,128},{128,192},{192,256},{256,320},{320,384},{3... | collective-permute-start | bytes 884744 | tf_op jit(solution)/shard_map/ppermute | solution.py:251
  86.6 2.2 %project.1.total = f32[512,512]{1,0:T(8,128)S(1)} custom-call(bf16[512,4608]{1,0:T(8,128)(2,1)S(1)} %get-tuple-element.31.x_tok, bf16[576,512]{1,0:T(8,128)(2,1)S(1)} %all_gather.12.refs_0_, bf16[576,512]{1,0:T(8,128)(2,1)S(1)} %collective-permute-done.refs_1_, bf16[576,512]{1,0:T(8,128)(2,1)S(1)} %collective-permute-done.3.refs_2_, ...), custom_call_target="tpu_custom_call" | custom-call | flops 1811939328 | bytes 7077888 | tf_op jit(solution)/shard_map/project/pallas_call | solution.py:99
  88.9 3.1 %collective-permute-done.11.w_b = bf16[288,512]{1,0:T(8,128)(2,1)S(1)} collective-permute-done((bf16[288,512]{1,0:T(8,128)(2,1)S(1)}, bf16[288,512]{1,0:T(8,128)(2,1)S(1)}, u32[]{:S(2)}, u32[]{:S(2)}) %collective-permute-start.11) | collective-permute-done | bytes 294944 | tf_op jit(solution)/shard_map/ppermute | solution.py:251
  92.0 4.0 %attend.1 = (bf16[512,256]{1,0:T(8,128)(2,1)}, f32[4,128]{1,0:T(4,128)S(1)}) custom-call(s32[4]{0:T(128)S(1)} %pad_add_fusion.info, f32[512,512]{1,0:T(8,128)S(1)} %project.1.total, bf16[512,4608]{1,0:T(8,128)(2,1)S(1)} %get-tuple-element.31.x_tok, bf16[576,512]{1,0:T(8,128)(2,1)S(1)} %copy-done.6, bf16[288,512]{1,0:T(8,128)(2,1)S(1)} %collective-permute-done.10.w_a, ...), custom_call_target="tpu_custom_call" | custom-call | flops 2818572288 | bytes 9437184 | tf_op jit(solution)/shard_map/attend/pallas_call | solution.py:155
  96.0 5.4 %collective-permute-start.12 = (bf16[512,256]{1,0:T(8,128)(2,1)}, bf16[512,256]{1,0:T(8,128)(2,1)}, u32[]{:S(2)}, u32[]{:S(2)}) collective-permute-start(bf16[512,256]{1,0:T(8,128)(2,1)} %get-tuple-element.47.refs_0_), channel_id=1, source_target_pairs={{16,0},{32,16},{48,32},{0,48},{17,1},{33,17},{49,33},{1,49},{18,2}... | collective-permute-start | bytes 786440 | tf_op jit(solution)/shard_map/ppermute | solution.py:251
  101.4 2.7 %collective-permute-start.13 = (bf16[512,256]{1,0:T(8,128)(2,1)}, bf16[512,256]{1,0:T(8,128)(2,1)}, u32[]{:S(2)}, u32[]{:S(2)}) collective-permute-start(bf16[512,256]{1,0:T(8,128)(2,1)} %get-tuple-element.47.refs_0_), channel_id=1, source_target_pairs={{32,0},{48,16},{0,32},{16,48},{33,1},{49,17},{1,33},{17,49},{34,2}... | collective-permute-start | bytes 786440 | tf_op jit(solution)/shard_map/ppermute | solution.py:251
  104.1 2.2 %collective-permute-start.14 = (bf16[512,256]{1,0:T(8,128)(2,1)}, bf16[512,256]{1,0:T(8,128)(2,1)}, u32[]{:S(2)}, u32[]{:S(2)}) collective-permute-start(bf16[512,256]{1,0:T(8,128)(2,1)} %get-tuple-element.47.refs_0_), channel_id=1, source_target_pairs={{48,0},{0,16},{16,32},{32,48},{49,1},{1,17},{17,33},{33,49},{50,2}... | collective-permute-start | bytes 786440 | tf_op jit(solution)/shard_map/ppermute | solution.py:251
  106.3 8.5 %psum.7 = f32[4,128]{1,0:T(4,128)S(1)} all-reduce(f32[4,128]{1,0:T(4,128)S(1)} %get-tuple-element.40), channel_id=1, replica_groups=mesh['z'=8,'x'=4,'y'=8,'core'=2] {'core'}, use_global_device_ids=true, to_apply=%region_0.1 | all-reduce | flops 512 | bytes 4096 | tf_op jit(solution)/shard_map/psum | solution.py:296
  115.4 9.3 %all-to-all-start = ((f32[32,4,128]{2,1,0:T(4,128)}), f32[32,4,128]{2,1,0:T(4,128)}, u32[]{:S(2)}, u32[]{:S(2)}) async-start(f32[32,4,128]{2,1,0:T(4,128)} %broadcast_in_dim.4), calls=%async_computation | async-start | bytes 131072 | tf_op jit(solution)/shard_map/all_to_all | solution.py:297
  127.1 6.6 %all-to-all-done = f32[32,4,128]{2,1,0:T(4,128)} async-done(((f32[32,4,128]{2,1,0:T(4,128)}), f32[32,4,128]{2,1,0:T(4,128)}, u32[]{:S(2)}, u32[]{:S(2)}) %all-to-all-start) | async-done | bytes 65568 | tf_op jit(solution)/shard_map/all_to_all | solution.py:297
  138.7 3.5 %all-to-all-start.1 = ((bf16[8,144,256]{2,1,0:T(8,128)(2,1)}), bf16[8,144,256]{2,1,0:T(8,128)(2,1)S(1)}, u32[]{:S(2)}, u32[]{:S(2)}) async-start(bf16[8,144,256]{2,1,0:T(8,128)(2,1)} %copy-done.2), calls=%async_computation.1 | async-start | bytes 1179648 | tf_op jit(solution)/shard_map/all_to_all | solution.py:300
  144.2 15.7 %all-to-all-done.1 = bf16[8,144,256]{2,1,0:T(8,128)(2,1)S(1)} async-done(((bf16[8,144,256]{2,1,0:T(8,128)(2,1)}), bf16[8,144,256]{2,1,0:T(8,128)(2,1)S(1)}, u32[]{:S(2)}, u32[]{:S(2)}) %all-to-all-start.1) | async-done | bytes 589856 | tf_op jit(solution)/shard_map/all_to_all | solution.py:300
  (61 shorter events, 29.1 us)
Async XLA Ops:
  7.2 57.6 %all-gather.4.cloned.1.call-start = ((), (), s32[]{:S(2)}) async-start(), calls=%async_computation.2 | async-start | bytes 5013504 | tf_op jit(solution)/shard_map/all_gather | solution.py:263
  7.9 106.9 %all-gather.6.cloned.1.call-start = ((), (), s32[]{:S(2)}) async-start(), calls=%async_computation.3 | async-start | bytes 3760128 | tf_op jit(solution)/shard_map/all_gather | solution.py:275
  20.1 22.3 %collective-permute-start = (bf16[576,512]{1,0:T(8,128)(2,1)S(1)}, bf16[576,512]{1,0:T(8,128)(2,1)S(1)}, u32[]{:S(2)}, u32[]{:S(2)}) collective-permute-start(bf16[576,512]{1,0:T(8,128)(2,1)S(1)} %all_gather.12.refs_0_), channel_id=1, source_target_pairs={{64,0},{128,64},{192,128},{256,192},{320,256},{384,320},{448,384},... | collective-permute-start | bytes 1769480 | tf_op jit(solution)/shard_map/ppermute | solution.py:251
  32.0 15.5 %collective-permute-start.1 = (bf16[576,512]{1,0:T(8,128)(2,1)S(1)}, bf16[576,512]{1,0:T(8,128)(2,1)S(1)}, u32[]{:S(2)}, u32[]{:S(2)}) collective-permute-start(bf16[576,512]{1,0:T(8,128)(2,1)S(1)} %all_gather.12.refs_0_), channel_id=1, source_target_pairs={{448,0},{0,64},{64,128},{128,192},{192,256},{256,320},{320,384},{3... | collective-permute-start | bytes 1769480 | tf_op jit(solution)/shard_map/ppermute | solution.py:251
  35.0 5.5 %collective-permute-start.2 = (bf16[288,256]{1,0:T(8,128)(2,1)S(1)}, bf16[288,256]{1,0:T(8,128)(2,1)S(1)}, u32[]{:S(2)}, u32[]{:S(2)}) collective-permute-start(bf16[288,256]{1,0:T(8,128)(2,1)S(1)} %get-tuple-element.54), channel_id=1, source_target_pairs={{1,0},{0,1},{3,2},{2,3},{5,4},{4,5},{7,6},{6,7},{9,8},{8,9},{11,10... | collective-permute-start | bytes 442376 | tf_op jit(solution)/shard_map/ppermute | solution.py:251
  47.5 18.0 %copy-start.5 = (bf16[576,512]{1,0:T(8,128)(2,1)}, bf16[576,512]{1,0:T(8,128)(2,1)S(1)}, u32[]{:S(2)}) copy-start(bf16[576,512]{1,0:T(8,128)(2,1)S(1)} %collective-permute-done.1.w) | copy-start | bytes 1769476
  47.5 17.3 %collective-permute-start.3 = (bf16[576,512]{1,0:T(8,128)(2,1)S(1)}, bf16[576,512]{1,0:T(8,128)(2,1)S(1)}, u32[]{:S(2)}, u32[]{:S(2)}) collective-permute-start(bf16[576,512]{1,0:T(8,128)(2,1)S(1)} %collective-permute-done.refs_1_), channel_id=1, source_target_pairs={{64,0},{128,64},{192,128},{256,192},{320,256},{384,320},{448,384},... | collective-permute-start | bytes 1769480 | tf_op jit(solution)/shard_map/ppermute | solution.py:251
  49.4 15.3 %collective-permute-start.4 = (bf16[576,512]{1,0:T(8,128)(2,1)S(1)}, bf16[576,512]{1,0:T(8,128)(2,1)S(1)}, u32[]{:S(2)}, u32[]{:S(2)}) collective-permute-start(bf16[576,512]{1,0:T(8,128)(2,1)S(1)} %collective-permute-done.1.w), channel_id=1, source_target_pairs={{448,0},{0,64},{64,128},{128,192},{192,256},{256,320},{320,384},{3... | collective-permute-start | bytes 1769480 | tf_op jit(solution)/shard_map/ppermute | solution.py:251
  53.0 33.4 %copy-start.8 = (s32[2]{0:T(128)S(1)}, s32[2]{0:T(128)}, u32[]{:S(2)}) copy-start(s32[2]{0:T(128)} %param.15) | copy-start | bytes 28
  53.0 33.4 %copy-start.9 = (s32[2]{0:T(128)S(1)}, s32[2]{0:T(128)}, u32[]{:S(2)}) copy-start(s32[2]{0:T(128)} %param.14) | copy-start | bytes 28
  53.0 7.8 %collective-permute-start.5 = (bf16[144,256]{1,0:T(8,128)(2,1)S(1)}, bf16[144,256]{1,0:T(8,128)(2,1)S(1)}, u32[]{:S(2)}, u32[]{:S(2)}) collective-permute-start(bf16[144,256]{1,0:T(8,128)(2,1)S(1)} %get-tuple-element.52), channel_id=1, source_target_pairs={{16,0},{32,16},{48,32},{0,48},{17,1},{33,17},{49,33},{1,49},{18,2}... | collective-permute-start | bytes 221192 | tf_op jit(solution)/shard_map/ppermute | solution.py:251
  55.1 6.6 %collective-permute-start.6 = (bf16[144,256]{1,0:T(8,128)(2,1)S(1)}, bf16[144,256]{1,0:T(8,128)(2,1)S(1)}, u32[]{:S(2)}, u32[]{:S(2)}) collective-permute-start(bf16[144,256]{1,0:T(8,128)(2,1)S(1)} %get-tuple-element.51), channel_id=1, source_target_pairs={{32,0},{48,16},{0,32},{16,48},{33,1},{49,17},{1,33},{17,49},{34,2}... | collective-permute-start | bytes 221192 | tf_op jit(solution)/shard_map/ppermute | solution.py:251
  58.0 6.7 %collective-permute-start.7 = (bf16[144,256]{1,0:T(8,128)(2,1)S(1)}, bf16[144,256]{1,0:T(8,128)(2,1)S(1)}, u32[]{:S(2)}, u32[]{:S(2)}) collective-permute-start(bf16[144,256]{1,0:T(8,128)(2,1)S(1)} %get-tuple-element.50), channel_id=1, source_target_pairs={{48,0},{0,16},{16,32},{32,48},{49,1},{1,17},{17,33},{33,49},{50,2}... | collective-permute-start | bytes 221192 | tf_op jit(solution)/shard_map/ppermute | solution.py:251
  65.5 11.3 %collective-permute-start.8 = (bf16[576,512]{1,0:T(8,128)(2,1)S(1)}, bf16[576,512]{1,0:T(8,128)(2,1)S(1)}, u32[]{:S(2)}, u32[]{:S(2)}) collective-permute-start(bf16[576,512]{1,0:T(8,128)(2,1)S(1)} %collective-permute-done.3.refs_2_), channel_id=1, source_target_pairs={{64,0},{128,64},{192,128},{256,192},{320,256},{384,320},{448,384},... | collective-permute-start | bytes 1769480 | tf_op jit(solution)/shard_map/ppermute | solution.py:251
  68.7 12.3 %collective-permute-start.9 = (bf16[576,512]{1,0:T(8,128)(2,1)S(1)}, bf16[576,512]{1,0:T(8,128)(2,1)S(1)}, u32[]{:S(2)}, u32[]{:S(2)}) collective-permute-start(bf16[576,512]{1,0:T(8,128)(2,1)S(1)} %collective-permute-done.4.refs_5_), channel_id=1, source_target_pairs={{448,0},{0,64},{64,128},{128,192},{192,256},{256,320},{320,384},{3... | collective-permute-start | bytes 1769480 | tf_op jit(solution)/shard_map/ppermute | solution.py:251
  76.0 12.8 %copy-start.3 = (bf16[8,144,512]{2,1,0:T(8,128)(2,1)}, bf16[8,144,512]{2,1,0:T(8,128)(2,1)S(1)}, u32[]{:S(2)}) copy-start(bf16[8,144,512]{2,1,0:T(8,128)(2,1)S(1)} %get-tuple-element.45.own) | copy-start | bytes 3538948
  81.0 7.9 %collective-permute-start.10 = (bf16[288,512]{1,0:T(8,128)(2,1)S(1)}, bf16[288,512]{1,0:T(8,128)(2,1)S(1)}, u32[]{:S(2)}, u32[]{:S(2)}) collective-permute-start(bf16[288,512]{1,0:T(8,128)(2,1)S(1)} %slice.26), channel_id=1, source_target_pairs={{64,0},{128,64},{192,128},{256,192},{320,256},{384,320},{448,384},... | collective-permute-start | bytes 884744 | tf_op jit(solution)/shard_map/ppermute | solution.py:251
  83.0 9.0 %collective-permute-start.11 = (bf16[288,512]{1,0:T(8,128)(2,1)S(1)}, bf16[288,512]{1,0:T(8,128)(2,1)S(1)}, u32[]{:S(2)}, u32[]{:S(2)}) collective-permute-start(bf16[288,512]{1,0:T(8,128)(2,1)S(1)} %slice.27), channel_id=1, source_target_pairs={{448,0},{0,64},{64,128},{128,192},{192,256},{256,320},{320,384},{3... | collective-permute-start | bytes 884744 | tf_op jit(solution)/shard_map/ppermute | solution.py:251
  86.6 5.4 %copy-start.6 = (bf16[576,512]{1,0:T(8,128)(2,1)S(1)}, bf16[576,512]{1,0:T(8,128)(2,1)}, u32[]{:S(2)}) copy-start(bf16[576,512]{1,0:T(8,128)(2,1)} %copy-done.5) | copy-start | bytes 1769476
  96.0 31.0 %collective-permute-start.12 = (bf16[512,256]{1,0:T(8,128)(2,1)}, bf16[512,256]{1,0:T(8,128)(2,1)}, u32[]{:S(2)}, u32[]{:S(2)}) collective-permute-start(bf16[512,256]{1,0:T(8,128)(2,1)} %get-tuple-element.47.refs_0_), channel_id=1, source_target_pairs={{16,0},{32,16},{48,32},{0,48},{17,1},{33,17},{49,33},{1,49},{18,2}... | collective-permute-start | bytes 786440 | tf_op jit(solution)/shard_map/ppermute | solution.py:251
  101.4 25.7 %collective-permute-start.13 = (bf16[512,256]{1,0:T(8,128)(2,1)}, bf16[512,256]{1,0:T(8,128)(2,1)}, u32[]{:S(2)}, u32[]{:S(2)}) collective-permute-start(bf16[512,256]{1,0:T(8,128)(2,1)} %get-tuple-element.47.refs_0_), channel_id=1, source_target_pairs={{32,0},{48,16},{0,32},{16,48},{33,1},{49,17},{1,33},{17,49},{34,2}... | collective-permute-start | bytes 786440 | tf_op jit(solution)/shard_map/ppermute | solution.py:251
  104.1 23.0 %collective-permute-start.14 = (bf16[512,256]{1,0:T(8,128)(2,1)}, bf16[512,256]{1,0:T(8,128)(2,1)}, u32[]{:S(2)}, u32[]{:S(2)}) collective-permute-start(bf16[512,256]{1,0:T(8,128)(2,1)} %get-tuple-element.47.refs_0_), channel_id=1, source_target_pairs={{48,0},{0,16},{16,32},{32,48},{49,1},{1,17},{17,33},{33,49},{50,2}... | collective-permute-start | bytes 786440 | tf_op jit(solution)/shard_map/ppermute | solution.py:251
  115.4 18.2 %all-to-all-start = ((f32[32,4,128]{2,1,0:T(4,128)}), f32[32,4,128]{2,1,0:T(4,128)}, u32[]{:S(2)}, u32[]{:S(2)}) async-start(f32[32,4,128]{2,1,0:T(4,128)} %broadcast_in_dim.4), calls=%async_computation | async-start | bytes 131072 | tf_op jit(solution)/shard_map/all_to_all | solution.py:297
  138.7 21.2 %all-to-all-start.1 = ((bf16[8,144,256]{2,1,0:T(8,128)(2,1)}), bf16[8,144,256]{2,1,0:T(8,128)(2,1)S(1)}, u32[]{:S(2)}, u32[]{:S(2)}) async-start(bf16[8,144,256]{2,1,0:T(8,128)(2,1)} %copy-done.2), calls=%async_computation.1 | async-start | bytes 1179648 | tf_op jit(solution)/shard_map/all_to_all | solution.py:300
  (5 other events, 11.8 us)
Sparse Core Ops, SparseCore 0:
  10.1 51.2 all-gather.3
  65.7 44.1 all-gather.5

commit v6 on v5

--- a/solution.py
+++ b/solution.py
@@ -269,10 +269,10 @@
     v1, e1, come = together(above(w), below(w), come)
 
     pair = jnp.where(at_first, jnp.concatenate([keep, come], 0), jnp.concatenate([come, keep], 0))
-    piece = lambda k: lax.dynamic_slice_in_dim(pair, lax.rem(x + k, NX) * ROWS, ROWS, 0)
-    owned = [hop(piece(NX - k), "x", NX, k) for k in range(1, NX)]
-    v2, e2, x_t, *owned = together(above(v1), below(e1), x_t, *owned)
-    owned = lax.all_gather(jnp.stack(owned), ("y", "core"), axis=0)
+    owned = lax.all_to_all(pair.reshape(NX, ROWS, L), "x", 0, 0)
+    v2, e2, x_t, owned = together(above(v1), below(e1), x_t, owned)
+    owned = jnp.stack([lax.dynamic_index_in_dim(owned, lax.rem(x + j, NX), 0, False) for j in range(1, NX)])
+    owned = lax.all_gather(owned, ("y", "core"), axis=0)
 
     v3, e3 = together(above(v2), below(e2))
     place = jnp.stack([lax.axis_index(a) for a in ("y", "core", "x", "z")]).astype(jnp.int32)

time: 168 us -> 167 us (level)
  waiting for transfers between devices: 43.1 us -> 48.1 us
  starting transfers between devices: 65.1 us -> 60.4 us
  blocking collectives: 19.7 us -> 16.6 us
    all_to_all x0 -> x1, waiting for transfers between devices: none -> 5.6 us  [gather(): owned = lax.all_to_all(pair.reshape(NX, ROWS, L), 'x', 0, 0)]
    ppermute x15 -> x12, starting transfers between devices: 52.2 us -> 46.9 us  [hop(): return lax.ppermute(a, axis, ring(size, k))]
    all_to_all x0 -> x1, starting transfers between devices: none -> 3.45 us  [gather(): owned = lax.all_to_all(pair.reshape(NX, ROWS, L), 'x', 0, 0)]
    psum x1, blocking collectives: 8.5 us -> 5.36 us  [body(): norms, owned = together(lax.psum(norms, 'core'), owned)]
    all_to_all x1, starting transfers between devices: 9.26 us -> 6.22 us  [body(): lax.all_to_all(jnp.broadcast_to(norms, (NX * NY, 4, HD)), ('x', 'y'), 0, 0)]
    ppermute x15 -> x12, waiting for transfers between devices: 20.1 us -> 20 us  [hop(): return lax.ppermute(a, axis, ring(size, k))]
  transfers between devices with their start and end apart: 19 -> 17, of which waited for: 11 -> 11; matrix products, arithmetic and copies ran while one was open for 3% -> 3% of each run, Pallas kernels for 5% -> 5%
where the time goes in v6:
time: 167 us; the launch traced here: 165 us
  starting transfers between devices  60.4 us (36%)
  waiting for transfers between devices  48.1 us (29%)
  blocking collectives  16.6 us (10%)
  between operations  15 us (9%)
  Pallas kernels  11.8 us (7%)
  local copies, waits for them, and re-layouts  7.13 us (4%)
  other arithmetic  6.4 us (4%)
    ppermute x12, starting transfers between devices, hop(): return lax.ppermute(a, axis, ring(size, k))  46.9 us
    ppermute x12, waiting for transfers between devices, hop(): return lax.ppermute(a, axis, ring(size, k))  20 us
    all_to_all x1, waiting for transfers between devices, body(): terms = lax.all_to_all(terms, 'z', 0, 0)  15.2 us
    all_gather x1, blocking collectives, gather(): w, part = together(lax.all_gather(w, 'x', axis=0, tiled=True), shard)  11.2 us
    all_to_all x1, waiting for transfers between devices, body(): lax.all_to_all(jnp.broadcast_to(norms, (NX * NY, 4, HD)), ('x', 'y'), 0, 0)  6.56 us
    unnamed x20, local copies, waits for them, and re-layouts  6.44 us
    all_to_all x1, starting transfers between devices, body(): lax.all_to_all(jnp.broadcast_to(norms, (NX * NY, 4, HD)), ('x', 'y'), 0, 0)  6.22 us
    all_to_all x1, waiting for transfers between devices, gather(): owned = lax.all_to_all(pair.reshape(NX, ROWS, L), 'x', 0, 0)  5.6 us
  transfers between devices with their start and end apart: 17, of which 11 were waited for; matrix products, arithmetic and copies ran while one was open for 3% of the time, Pallas kernels for 5%

profile of v6, /device:TPU:1, one launch (start us, length us, event | category | flops | bytes accessed | tf_op | source)
XLA Modules:
  0.0 165.5 jit_solution(14255054767846738560)
XLA Ops:
  8.8 11.2 %all_gather.12.refs_0_ = bf16[576,512]{1,0:T(8,128)(2,1)S(1)} all-gather(bf16[144,512]{1,0:T(8,128)(2,1)S(1)} %pad_maximum_fusion.1), channel_id=1, replica_groups=mesh['z'=8,'x'=4,'y'=8,'core'=2] {'x'}, dimensions={0}, use_global_device_ids=true | all-gather | bytes 737280 | tf_op jit(solution)/shard_map/all_gather | solution.py:264
  20.1 11.9 %collective-permute-start = (bf16[576,512]{1,0:T(8,128)(2,1)S(1)}, bf16[576,512]{1,0:T(8,128)(2,1)S(1)}, u32[]{:S(2)}, u32[]{:S(2)}) collective-permute-start(bf16[576,512]{1,0:T(8,128)(2,1)S(1)} %all_gather.12.refs_0_), channel_id=1, source_target_pairs={{64,0},{128,64},{192,128},{256,192},{320,256},{384,320},{448,384},... | collective-permute-start | bytes 1769480 | tf_op jit(solution)/shard_map/ppermute | solution.py:251
  34.9 4.5 %collective-permute-start.2 = (bf16[288,256]{1,0:T(8,128)(2,1)S(1)}, bf16[288,256]{1,0:T(8,128)(2,1)S(1)}, u32[]{:S(2)}, u32[]{:S(2)}) collective-permute-start(bf16[288,256]{1,0:T(8,128)(2,1)S(1)} %get-tuple-element.50), channel_id=1, source_target_pairs={{1,0},{0,1},{3,2},{2,3},{5,4},{4,5},{7,6},{6,7},{9,8},{8,9},{11,10... | collective-permute-start | bytes 442376 | tf_op jit(solution)/shard_map/ppermute | solution.py:251
  42.3 5.2 %collective-permute-done.1.w = bf16[576,512]{1,0:T(8,128)(2,1)S(1)} collective-permute-done((bf16[576,512]{1,0:T(8,128)(2,1)S(1)}, bf16[576,512]{1,0:T(8,128)(2,1)S(1)}, u32[]{:S(2)}, u32[]{:S(2)}) %collective-permute-start.1) | collective-permute-done | bytes 589856 | tf_op jit(solution)/shard_map/ppermute | solution.py:251
  49.4 3.4 %collective-permute-start.4 = (bf16[576,512]{1,0:T(8,128)(2,1)S(1)}, bf16[576,512]{1,0:T(8,128)(2,1)S(1)}, u32[]{:S(2)}, u32[]{:S(2)}) collective-permute-start(bf16[576,512]{1,0:T(8,128)(2,1)S(1)} %collective-permute-done.1.w), channel_id=1, source_target_pairs={{448,0},{0,64},{64,128},{128,192},{192,256},{256,320},{320,384},{3... | collective-permute-start | bytes 1769480 | tf_op jit(solution)/shard_map/ppermute | solution.py:251
  53.6 3.5 %all-to-all-start = ((bf16[4,144,256]{2,1,0:T(8,128)(2,1)}), bf16[4,144,256]{2,1,0:T(8,128)(2,1)S(1)}, u32[]{:S(2)}, u32[]{:S(2)}) async-start(bf16[4,144,256]{2,1,0:T(8,128)(2,1)} %bitcast.5), calls=%async_computation | async-start | bytes 589824 | tf_op jit(solution)/shard_map/all_to_all | solution.py:272
  57.1 5.6 %all-to-all-done = bf16[4,144,256]{2,1,0:T(8,128)(2,1)S(1)} async-done(((bf16[4,144,256]{2,1,0:T(8,128)(2,1)}), bf16[4,144,256]{2,1,0:T(8,128)(2,1)S(1)}, u32[]{:S(2)}, u32[]{:S(2)}) %all-to-all-start) | async-done | bytes 294944 | tf_op jit(solution)/shard_map/all_to_all | solution.py:272
  64.7 3.1 %collective-permute-start.5 = (bf16[576,512]{1,0:T(8,128)(2,1)S(1)}, bf16[576,512]{1,0:T(8,128)(2,1)S(1)}, u32[]{:S(2)}, u32[]{:S(2)}) collective-permute-start(bf16[576,512]{1,0:T(8,128)(2,1)S(1)} %collective-permute-done.3.refs_2_), channel_id=1, source_target_pairs={{64,0},{128,64},{192,128},{256,192},{320,256},{384,320},{448,384},... | collective-permute-start | bytes 1769480 | tf_op jit(solution)/shard_map/ppermute | solution.py:251
  70.6 2.3 %copy-done = bf16[4608,512]{1,0:T(8,128)(2,1)S(1)} copy-done((bf16[4608,512]{1,0:T(8,128)(2,1)S(1)}, bf16[4608,512]{1,0:T(8,128)(2,1)}, u32[]{:S(2)}) %copy-start) | copy-done | bytes 4718616
  73.0 2.2 %arrange.1 = (bf16[512,4608]{1,0:T(8,128)(2,1)S(1)}, f32[2,256,256]{2,1,0:T(8,128)S(1)}, bf16[8,144,512]{2,1,0:T(8,128)(2,1)S(1)}) custom-call(s32[4]{0:T(128)S(1)} %pad_add_fusion.1.place, bf16[4608,512]{1,0:T(8,128)(2,1)S(1)} %copy-done), custom_call_target="tpu_custom_call" | custom-call | flops 1207959552 | bytes 9437184 | tf_op jit(solution)/shard_map/arrange/pallas_call | solution.py:72
  77.1 4.8 %collective-permute-done.6.refs_4_ = bf16[576,512]{1,0:T(8,128)(2,1)S(1)} collective-permute-done((bf16[576,512]{1,0:T(8,128)(2,1)S(1)}, bf16[576,512]{1,0:T(8,128)(2,1)S(1)}, u32[]{:S(2)}, u32[]{:S(2)}) %collective-permute-start.6) | collective-permute-done | bytes 589856 | tf_op jit(solution)/shard_map/ppermute | solution.py:251
  81.9 2.9 %collective-permute-start.7 = (bf16[288,512]{1,0:T(8,128)(2,1)S(1)}, bf16[288,512]{1,0:T(8,128)(2,1)S(1)}, u32[]{:S(2)}, u32[]{:S(2)}) collective-permute-start(bf16[288,512]{1,0:T(8,128)(2,1)S(1)} %slice.26), channel_id=1, source_target_pairs={{64,0},{128,64},{192,128},{256,192},{320,256},{384,320},{448,384},... | collective-permute-start | bytes 884744 | tf_op jit(solution)/shard_map/ppermute | solution.py:251
  84.8 2.4 %collective-permute-start.8 = (bf16[288,512]{1,0:T(8,128)(2,1)S(1)}, bf16[288,512]{1,0:T(8,128)(2,1)S(1)}, u32[]{:S(2)}, u32[]{:S(2)}) collective-permute-start(bf16[288,512]{1,0:T(8,128)(2,1)S(1)} %slice.27), channel_id=1, source_target_pairs={{448,0},{0,64},{64,128},{128,192},{192,256},{256,320},{320,384},{3... | collective-permute-start | bytes 884744 | tf_op jit(solution)/shard_map/ppermute | solution.py:251
  87.5 2.2 %project.1.total = f32[512,512]{1,0:T(8,128)S(1)} custom-call(bf16[512,4608]{1,0:T(8,128)(2,1)S(1)} %get-tuple-element.29.x_tok, bf16[576,512]{1,0:T(8,128)(2,1)S(1)} %all_gather.12.refs_0_, bf16[576,512]{1,0:T(8,128)(2,1)S(1)} %collective-permute-done.refs_1_, bf16[576,512]{1,0:T(8,128)(2,1)S(1)} %collective-permute-done.3.refs_2_, ...), custom_call_target="tpu_custom_call" | custom-call | flops 1811939328 | bytes 7077888 | tf_op jit(solution)/shard_map/project/pallas_call | solution.py:99
  89.8 4.1 %collective-permute-done.8.w_b = bf16[288,512]{1,0:T(8,128)(2,1)S(1)} collective-permute-done((bf16[288,512]{1,0:T(8,128)(2,1)S(1)}, bf16[288,512]{1,0:T(8,128)(2,1)S(1)}, u32[]{:S(2)}, u32[]{:S(2)}) %collective-permute-start.8) | collective-permute-done | bytes 294944 | tf_op jit(solution)/shard_map/ppermute | solution.py:251
  93.9 4.1 %attend.1 = (bf16[512,256]{1,0:T(8,128)(2,1)}, f32[4,128]{1,0:T(4,128)S(1)}) custom-call(s32[4]{0:T(128)S(1)} %pad_add_fusion.info, f32[512,512]{1,0:T(8,128)S(1)} %project.1.total, bf16[512,4608]{1,0:T(8,128)(2,1)S(1)} %get-tuple-element.29.x_tok, bf16[576,512]{1,0:T(8,128)(2,1)S(1)} %copy-done.6, bf16[288,512]{1,0:T(8,128)(2,1)S(1)} %collective-permute-done.7.w_a, ...), custom_call_target="tpu_custom_call" | custom-call | flops 2818572288 | bytes 9437184 | tf_op jit(solution)/shard_map/attend/pallas_call | solution.py:155
  97.9 6.3 %collective-permute-start.9 = (bf16[512,256]{1,0:T(8,128)(2,1)}, bf16[512,256]{1,0:T(8,128)(2,1)}, u32[]{:S(2)}, u32[]{:S(2)}) collective-permute-start(bf16[512,256]{1,0:T(8,128)(2,1)} %get-tuple-element.43.refs_0_), channel_id=1, source_target_pairs={{16,0},{32,16},{48,32},{0,48},{17,1},{33,17},{49,33},{1,49},{18,2}... | collective-permute-start | bytes 786440 | tf_op jit(solution)/shard_map/ppermute | solution.py:251
  104.2 3.6 %collective-permute-start.10 = (bf16[512,256]{1,0:T(8,128)(2,1)}, bf16[512,256]{1,0:T(8,128)(2,1)}, u32[]{:S(2)}, u32[]{:S(2)}) collective-permute-start(bf16[512,256]{1,0:T(8,128)(2,1)} %get-tuple-element.43.refs_0_), channel_id=1, source_target_pairs={{32,0},{48,16},{0,32},{16,48},{33,1},{49,17},{1,33},{17,49},{34,2}... | collective-permute-start | bytes 786440 | tf_op jit(solution)/shard_map/ppermute | solution.py:251
  107.9 2.8 %collective-permute-start.11 = (bf16[512,256]{1,0:T(8,128)(2,1)}, bf16[512,256]{1,0:T(8,128)(2,1)}, u32[]{:S(2)}, u32[]{:S(2)}) collective-permute-start(bf16[512,256]{1,0:T(8,128)(2,1)} %get-tuple-element.43.refs_0_), channel_id=1, source_target_pairs={{48,0},{0,16},{16,32},{32,48},{49,1},{1,17},{17,33},{33,49},{50,2}... | collective-permute-start | bytes 786440 | tf_op jit(solution)/shard_map/ppermute | solution.py:251
  110.6 5.4 %psum.7 = f32[4,128]{1,0:T(4,128)S(1)} all-reduce(f32[4,128]{1,0:T(4,128)S(1)} %get-tuple-element.38), channel_id=1, replica_groups=mesh['z'=8,'x'=4,'y'=8,'core'=2] {'core'}, use_global_device_ids=true, to_apply=%region_0.1 | all-reduce | flops 512 | bytes 4096 | tf_op jit(solution)/shard_map/psum | solution.py:296
  116.6 6.2 %all-to-all-start.1 = ((f32[32,4,128]{2,1,0:T(4,128)}), f32[32,4,128]{2,1,0:T(4,128)}, u32[]{:S(2)}, u32[]{:S(2)}) async-start(f32[32,4,128]{2,1,0:T(4,128)} %broadcast_in_dim.4), calls=%async_computation.1 | async-start | bytes 131072 | tf_op jit(solution)/shard_map/all_to_all | solution.py:297
  125.2 6.6 %all-to-all-done.1 = f32[32,4,128]{2,1,0:T(4,128)} async-done(((f32[32,4,128]{2,1,0:T(4,128)}), f32[32,4,128]{2,1,0:T(4,128)}, u32[]{:S(2)}, u32[]{:S(2)}) %all-to-all-start.1) | async-done | bytes 65568 | tf_op jit(solution)/shard_map/all_to_all | solution.py:297
  136.8 3.8 %all-to-all-start.2 = ((bf16[8,144,256]{2,1,0:T(8,128)(2,1)}), bf16[8,144,256]{2,1,0:T(8,128)(2,1)S(1)}, u32[]{:S(2)}, u32[]{:S(2)}) async-start(bf16[8,144,256]{2,1,0:T(8,128)(2,1)} %copy-done.2), calls=%async_computation.2 | async-start | bytes 1179648 | tf_op jit(solution)/shard_map/all_to_all | solution.py:300
  142.6 15.2 %all-to-all-done.2 = bf16[8,144,256]{2,1,0:T(8,128)(2,1)S(1)} async-done(((bf16[8,144,256]{2,1,0:T(8,128)(2,1)}), bf16[8,144,256]{2,1,0:T(8,128)(2,1)S(1)}, u32[]{:S(2)}, u32[]{:S(2)}) %all-to-all-start.2) | async-done | bytes 589856 | tf_op jit(solution)/shard_map/all_to_all | solution.py:300
  (57 shorter events, 27.3 us)
Async XLA Ops:
  7.2 56.8 %all-gather.4.cloned.1.call-start = ((), (), s32[]{:S(2)}) async-start(), calls=%async_computation.3 | async-start | bytes 5013504 | tf_op jit(solution)/shard_map/all_gather | solution.py:263
  20.1 22.3 %collective-permute-start = (bf16[576,512]{1,0:T(8,128)(2,1)S(1)}, bf16[576,512]{1,0:T(8,128)(2,1)S(1)}, u32[]{:S(2)}, u32[]{:S(2)}) collective-permute-start(bf16[576,512]{1,0:T(8,128)(2,1)S(1)} %all_gather.12.refs_0_), channel_id=1, source_target_pairs={{64,0},{128,64},{192,128},{256,192},{320,256},{384,320},{448,384},... | collective-permute-start | bytes 1769480 | tf_op jit(solution)/shard_map/ppermute | solution.py:251
  32.0 15.5 %collective-permute-start.1 = (bf16[576,512]{1,0:T(8,128)(2,1)S(1)}, bf16[576,512]{1,0:T(8,128)(2,1)S(1)}, u32[]{:S(2)}, u32[]{:S(2)}) collective-permute-start(bf16[576,512]{1,0:T(8,128)(2,1)S(1)} %all_gather.12.refs_0_), channel_id=1, source_target_pairs={{448,0},{0,64},{64,128},{128,192},{192,256},{256,320},{320,384},{3... | collective-permute-start | bytes 1769480 | tf_op jit(solution)/shard_map/ppermute | solution.py:251
  34.9 5.5 %collective-permute-start.2 = (bf16[288,256]{1,0:T(8,128)(2,1)S(1)}, bf16[288,256]{1,0:T(8,128)(2,1)S(1)}, u32[]{:S(2)}, u32[]{:S(2)}) collective-permute-start(bf16[288,256]{1,0:T(8,128)(2,1)S(1)} %get-tuple-element.50), channel_id=1, source_target_pairs={{1,0},{0,1},{3,2},{2,3},{5,4},{4,5},{7,6},{6,7},{9,8},{8,9},{11,10... | collective-permute-start | bytes 442376 | tf_op jit(solution)/shard_map/ppermute | solution.py:251
  47.5 17.2 %copy-start.5 = (bf16[576,512]{1,0:T(8,128)(2,1)}, bf16[576,512]{1,0:T(8,128)(2,1)S(1)}, u32[]{:S(2)}) copy-start(bf16[576,512]{1,0:T(8,128)(2,1)S(1)} %collective-permute-done.1.w) | copy-start | bytes 1769476
  47.5 15.3 %collective-permute-start.3 = (bf16[576,512]{1,0:T(8,128)(2,1)S(1)}, bf16[576,512]{1,0:T(8,128)(2,1)S(1)}, u32[]{:S(2)}, u32[]{:S(2)}) collective-permute-start(bf16[576,512]{1,0:T(8,128)(2,1)S(1)} %collective-permute-done.refs_1_), channel_id=1, source_target_pairs={{64,0},{128,64},{192,128},{256,192},{320,256},{384,320},{448,384},... | collective-permute-start | bytes 1769480 | tf_op jit(solution)/shard_map/ppermute | solution.py:251
  49.4 14.5 %collective-permute-start.4 = (bf16[576,512]{1,0:T(8,128)(2,1)S(1)}, bf16[576,512]{1,0:T(8,128)(2,1)S(1)}, u32[]{:S(2)}, u32[]{:S(2)}) collective-permute-start(bf16[576,512]{1,0:T(8,128)(2,1)S(1)} %collective-permute-done.1.w), channel_id=1, source_target_pairs={{448,0},{0,64},{64,128},{128,192},{192,256},{256,320},{320,384},{3... | collective-permute-start | bytes 1769480 | tf_op jit(solution)/shard_map/ppermute | solution.py:251
  53.6 9.1 %all-to-all-start = ((bf16[4,144,256]{2,1,0:T(8,128)(2,1)}), bf16[4,144,256]{2,1,0:T(8,128)(2,1)S(1)}, u32[]{:S(2)}, u32[]{:S(2)}) async-start(bf16[4,144,256]{2,1,0:T(8,128)(2,1)} %bitcast.5), calls=%async_computation | async-start | bytes 589824 | tf_op jit(solution)/shard_map/all_to_all | solution.py:272
  57.0 58.9 %all-gather.6.cloned.1.call-start = ((), (), s32[]{:S(2)}) async-start(), calls=%async_computation.4 | async-start | bytes 3760128 | tf_op jit(solution)/shard_map/all_gather | solution.py:275
  63.9 23.3 %copy-start.8 = (s32[2]{0:T(128)S(1)}, s32[2]{0:T(128)}, u32[]{:S(2)}) copy-start(s32[2]{0:T(128)} %param.15) | copy-start | bytes 28
  64.0 23.3 %copy-start.9 = (s32[2]{0:T(128)S(1)}, s32[2]{0:T(128)}, u32[]{:S(2)}) copy-start(s32[2]{0:T(128)} %param.14) | copy-start | bytes 28
  64.7 12.4 %collective-permute-start.5 = (bf16[576,512]{1,0:T(8,128)(2,1)S(1)}, bf16[576,512]{1,0:T(8,128)(2,1)S(1)}, u32[]{:S(2)}, u32[]{:S(2)}) collective-permute-start(bf16[576,512]{1,0:T(8,128)(2,1)S(1)} %collective-permute-done.3.refs_2_), channel_id=1, source_target_pairs={{64,0},{128,64},{192,128},{256,192},{320,256},{384,320},{448,384},... | collective-permute-start | bytes 1769480 | tf_op jit(solution)/shard_map/ppermute | solution.py:251
  67.8 14.1 %collective-permute-start.6 = (bf16[576,512]{1,0:T(8,128)(2,1)S(1)}, bf16[576,512]{1,0:T(8,128)(2,1)S(1)}, u32[]{:S(2)}, u32[]{:S(2)}) collective-permute-start(bf16[576,512]{1,0:T(8,128)(2,1)S(1)} %collective-permute-done.4.refs_5_), channel_id=1, source_target_pairs={{448,0},{0,64},{64,128},{128,192},{192,256},{256,320},{320,384},{3... | collective-permute-start | bytes 1769480 | tf_op jit(solution)/shard_map/ppermute | solution.py:251
  70.6 2.3 %copy-start = (bf16[4608,512]{1,0:T(8,128)(2,1)S(1)}, bf16[4608,512]{1,0:T(8,128)(2,1)}, u32[]{:S(2)}) copy-start(bf16[4608,512]{1,0:T(8,128)(2,1)} %all-gather.4.cloned.1.call-done.x_t) | copy-start | bytes 14155780
  75.2 14.5 %copy-start.3 = (bf16[8,144,512]{2,1,0:T(8,128)(2,1)}, bf16[8,144,512]{2,1,0:T(8,128)(2,1)S(1)}, u32[]{:S(2)}) copy-start(bf16[8,144,512]{2,1,0:T(8,128)(2,1)S(1)} %get-tuple-element.41.own) | copy-start | bytes 3538948
  81.9 7.9 %collective-permute-start.7 = (bf16[288,512]{1,0:T(8,128)(2,1)S(1)}, bf16[288,512]{1,0:T(8,128)(2,1)S(1)}, u32[]{:S(2)}, u32[]{:S(2)}) collective-permute-start(bf16[288,512]{1,0:T(8,128)(2,1)S(1)} %slice.26), channel_id=1, source_target_pairs={{64,0},{128,64},{192,128},{256,192},{320,256},{384,320},{448,384},... | collective-permute-start | bytes 884744 | tf_op jit(solution)/shard_map/ppermute | solution.py:251
  84.8 9.1 %collective-permute-start.8 = (bf16[288,512]{1,0:T(8,128)(2,1)S(1)}, bf16[288,512]{1,0:T(8,128)(2,1)S(1)}, u32[]{:S(2)}, u32[]{:S(2)}) collective-permute-start(bf16[288,512]{1,0:T(8,128)(2,1)S(1)} %slice.27), channel_id=1, source_target_pairs={{448,0},{0,64},{64,128},{128,192},{192,256},{256,320},{320,384},{3... | collective-permute-start | bytes 884744 | tf_op jit(solution)/shard_map/ppermute | solution.py:251
  87.5 6.4 %copy-start.6 = (bf16[576,512]{1,0:T(8,128)(2,1)S(1)}, bf16[576,512]{1,0:T(8,128)(2,1)}, u32[]{:S(2)}) copy-start(bf16[576,512]{1,0:T(8,128)(2,1)} %copy-done.5) | copy-start | bytes 1769476
  87.5 6.4 %copy-start.7 = (bf16[512,256]{1,0:T(8,128)(2,1)S(1)}, bf16[512,256]{1,0:T(8,128)(2,1)}, u32[]{:S(2)}) copy-start(bf16[512,256]{1,0:T(8,128)(2,1)} %cot.1) | copy-start | bytes 786436
  97.9 27.3 %collective-permute-start.9 = (bf16[512,256]{1,0:T(8,128)(2,1)}, bf16[512,256]{1,0:T(8,128)(2,1)}, u32[]{:S(2)}, u32[]{:S(2)}) collective-permute-start(bf16[512,256]{1,0:T(8,128)(2,1)} %get-tuple-element.43.refs_0_), channel_id=1, source_target_pairs={{16,0},{32,16},{48,32},{0,48},{17,1},{33,17},{49,33},{1,49},{18,2}... | collective-permute-start | bytes 786440 | tf_op jit(solution)/shard_map/ppermute | solution.py:251
  104.2 21.0 %collective-permute-start.10 = (bf16[512,256]{1,0:T(8,128)(2,1)}, bf16[512,256]{1,0:T(8,128)(2,1)}, u32[]{:S(2)}, u32[]{:S(2)}) collective-permute-start(bf16[512,256]{1,0:T(8,128)(2,1)} %get-tuple-element.43.refs_0_), channel_id=1, source_target_pairs={{32,0},{48,16},{0,32},{16,48},{33,1},{49,17},{1,33},{17,49},{34,2}... | collective-permute-start | bytes 786440 | tf_op jit(solution)/shard_map/ppermute | solution.py:251
  107.9 17.4 %collective-permute-start.11 = (bf16[512,256]{1,0:T(8,128)(2,1)}, bf16[512,256]{1,0:T(8,128)(2,1)}, u32[]{:S(2)}, u32[]{:S(2)}) collective-permute-start(bf16[512,256]{1,0:T(8,128)(2,1)} %get-tuple-element.43.refs_0_), channel_id=1, source_target_pairs={{48,0},{0,16},{16,32},{32,48},{49,1},{1,17},{17,33},{33,49},{50,2}... | collective-permute-start | bytes 786440 | tf_op jit(solution)/shard_map/ppermute | solution.py:251
  116.6 15.2 %all-to-all-start.1 = ((f32[32,4,128]{2,1,0:T(4,128)}), f32[32,4,128]{2,1,0:T(4,128)}, u32[]{:S(2)}, u32[]{:S(2)}) async-start(f32[32,4,128]{2,1,0:T(4,128)} %broadcast_in_dim.4), calls=%async_computation.1 | async-start | bytes 131072 | tf_op jit(solution)/shard_map/all_to_all | solution.py:297
  136.8 21.0 %all-to-all-start.2 = ((bf16[8,144,256]{2,1,0:T(8,128)(2,1)}), bf16[8,144,256]{2,1,0:T(8,128)(2,1)S(1)}, u32[]{:S(2)}, u32[]{:S(2)}) async-start(bf16[8,144,256]{2,1,0:T(8,128)(2,1)} %copy-done.2), calls=%async_computation.2 | async-start | bytes 1179648 | tf_op jit(solution)/shard_map/all_to_all | solution.py:300
  (3 other events, 4.1 us)
Sparse Core Ops, SparseCore 0:
  10.1 51.1 all-gather.3
  64.8 42.6 all-gather.5

commit v7 on v6

--- a/solution.py
+++ b/solution.py
@@ -171,8 +171,36 @@
     )(info, total, x_tok, *w, cot, cosine, sine, gram)
 
 
-def clip_kernel(place, norms, *refs):
-    grads, scaled = refs[:NX], refs[NX]
+def stage_kernel(features, out, sems):
+    def fetch(j, s):
+        columns = pl.ds((2 * (j - 1) + s) * L, L)
+        return pltpu.make_async_copy(
+            features.at[:, s, j - 1], out.at[:, :, columns], sems.at[2 * (j - 1) + s]
+        )
+
+    for j in range(1, NX):
+        for s in range(2):
+            fetch(j, s).start()
+    for j in range(1, NX):
+        for s in range(2):
+            fetch(j, s).wait()
+
+
+def stage(features):
+    return pl.pallas_call(
+        stage_kernel,
+        in_specs=[pl.BlockSpec(memory_space=pl.ANY)],
+        out_specs=pl.BlockSpec(memory_space=pltpu.VMEM),
+        out_shape=jax.ShapeDtypeStruct((NZ, ROWS, (NX - 1) * TOKENS), BF16),
+        scratch_shapes=[pltpu.SemaphoreType.DMA((2 * (NX - 1),))],
+        compiler_params=pltpu.CompilerParams(vmem_limit_bytes=VMEM),
+        cost_estimate=pl.CostEstimate(flops=0, bytes_accessed=4 * D * TOKENS, transcendentals=0),
+        name="stage",
+    )(features)
+
+
+def gradient_kernel(place, norms, staged, own, *refs):
+    grads, (out, scaled) = refs[:NX], refs[NX:]
     for j in range(NX):
         x = lax.rem(place[2] + j, NX)
         sums = jnp.sum(jnp.sum(norms[x], 0), 1, keepdims=True)
@@ -184,67 +212,25 @@
                 factor = factors[2 * i + s : 2 * i + s + 1, :]
                 part = factor * grads[j][rows, columns].astype(F32)
                 scaled[j * TOKENS + s * L : j * TOKENS + (s + 1) * L, columns] = part.astype(BF16)
-
-
-def clip(place, norms, grads):
-    vmem = pl.BlockSpec(memory_space=pltpu.VMEM)
-    return pl.pallas_call(
-        clip_kernel,
-        in_specs=[pl.BlockSpec(memory_space=pltpu.SMEM)] + [vmem] * (NX + 1),
-        out_specs=vmem,
-        out_shape=jax.ShapeDtypeStruct((NX * TOKENS, 2 * HD), BF16),
-        compiler_params=pltpu.CompilerParams(vmem_limit_bytes=VMEM),
-        name="clip",
-    )(place, norms, *grads)
-
-
-def stage_kernel(features, out, sems):
-    def fetch(j, s):
-        columns = pl.ds((2 * (j - 1) + s) * L, L)
-        return pltpu.make_async_copy(
-            features.at[:, s, j - 1], out.at[:, :, columns], sems.at[2 * (j - 1) + s]
-        )
-
-    for j in range(1, NX):
-        for s in range(2):
-            fetch(j, s).start()
-    for j in range(1, NX):
-        for s in range(2):
-            fetch(j, s).wait()
-
-
-def stage(features):
-    return pl.pallas_call(
-        stage_kernel,
-        in_specs=[pl.BlockSpec(memory_space=pl.ANY)],
-        out_specs=pl.BlockSpec(memory_space=pltpu.VMEM),
-        out_shape=jax.ShapeDtypeStruct((NZ, ROWS, (NX - 1) * TOKENS), BF16),
-        scratch_shapes=[pltpu.SemaphoreType.DMA((2 * (NX - 1),))],
-        compiler_params=pltpu.CompilerParams(vmem_limit_bytes=VMEM),
-        cost_estimate=pl.CostEstimate(flops=0, bytes_accessed=4 * D * TOKENS, transcendentals=0),
-        name="stage",
-    )(features)
-
-
-def gradient_kernel(staged, own, scaled, out):
     total = dot(own[...].reshape(NZ * ROWS, TOKENS), scaled[:TOKENS])
     total += dot(staged[...].reshape(NZ * ROWS, (NX - 1) * TOKENS), scaled[TOKENS:])
     out[...] = total.astype(BF16).reshape(NZ, ROWS, 2 * HD)
 
 
-def gradient(staged, own, scaled):
+def gradient(place, norms, staged, own, grads):
     vmem = pl.BlockSpec(memory_space=pltpu.VMEM)
     return pl.pallas_call(
         gradient_kernel,
-        in_specs=[vmem] * 3,
+        in_specs=[pl.BlockSpec(memory_space=pltpu.SMEM)] + [vmem] * (NX + 3),
         out_specs=vmem,
         out_shape=jax.ShapeDtypeStruct((NZ, ROWS, 2 * HD), BF16),
+        scratch_shapes=[pltpu.VMEM((NX * TOKENS, 2 * HD), BF16)],
         compiler_params=pltpu.CompilerParams(vmem_limit_bytes=VMEM),
         cost_estimate=pl.CostEstimate(
             flops=2 * D * TOKENS * 2 * HD, bytes_accessed=3 * D * TOKENS, transcendentals=0
         ),
         name="gradient",
-    )(staged, own, scaled)
+    )(place, norms, staged, own, *grads)
 
 
 def hop(a, axis, size, k):
@@ -295,8 +281,7 @@
     grads = [grads] + [hop(grads, "x", NX, k) for k in range(1, NX)]
     norms, owned = together(lax.psum(norms, "core"), owned)
     norms = lax.all_to_all(jnp.broadcast_to(norms, (NX * NY, 4, HD)), ("x", "y"), 0, 0)
-    scaled = clip(place, norms.reshape(NX, NY, 4, HD), grads)
-    terms = gradient(stage(owned), own, scaled)
+    terms = gradient(place, norms.reshape(NX, NY, 4, HD), stage(owned), own, grads)
     terms = lax.all_to_all(terms, "z", 0, 0)
     summed = jnp.sum(terms.astype(F32), 0)
 

time: 167 us -> 167 us (level)
  no operation moved by 1% of the time
where the time goes in v7:
time: 167 us; the launch traced here: 165 us
  starting transfers between devices  60.4 us (36%)
  waiting for transfers between devices  48.1 us (29%)
  blocking collectives  16.6 us (10%)
  between operations  15 us (9%)
  Pallas kernels  11.6 us (7%)
  local copies, waits for them, and re-layouts  7.14 us (4%)
  other arithmetic  6.4 us (4%)
    ppermute x12, starting transfers between devices, hop(): return lax.ppermute(a, axis, ring(size, k))  46.9 us
    ppermute x12, waiting for transfers between devices, hop(): return lax.ppermute(a, axis, ring(size, k))  20 us
    all_to_all x1, waiting for transfers between devices, body(): terms = lax.all_to_all(terms, 'z', 0, 0)  15.2 us
    all_gather x1, blocking collectives, gather(): w, part = together(lax.all_gather(w, 'x', axis=0, tiled=True), shard)  11.2 us
    all_to_all x1, waiting for transfers between devices, body(): lax.all_to_all(jnp.broadcast_to(norms, (NX * NY, 4, HD)), ('x', 'y'), 0, 0)  6.56 us
    unnamed x20, local copies, waits for them, and re-layouts  6.45 us
    all_to_all x1, starting transfers between devices, body(): lax.all_to_all(jnp.broadcast_to(norms, (NX * NY, 4, HD)), ('x', 'y'), 0, 0)  6.22 us
    all_to_all x1, waiting for transfers between devices, gather(): owned = lax.all_to_all(pair.reshape(NX, ROWS, L), 'x', 0, 0)  5.6 us
  transfers between devices with their start and end apart: 17, of which 11 were waited for; matrix products, arithmetic and copies ran while one was open for 3% of the time, Pallas kernels for 5%

profile of v7, /device:TPU:1, one launch (start us, length us, event | category | flops | bytes accessed | tf_op | source)
XLA Modules:
  0.0 165.3 jit_solution(17392090071546129659)
XLA Ops:
  8.8 11.2 %all_gather.12.refs_0_ = bf16[576,512]{1,0:T(8,128)(2,1)S(1)} all-gather(bf16[144,512]{1,0:T(8,128)(2,1)S(1)} %pad_maximum_fusion.1), channel_id=1, replica_groups=mesh['z'=8,'x'=4,'y'=8,'core'=2] {'x'}, dimensions={0}, use_global_device_ids=true | all-gather | bytes 737280 | tf_op jit(solution)/shard_map/all_gather | solution.py:250
  20.1 11.9 %collective-permute-start = (bf16[576,512]{1,0:T(8,128)(2,1)S(1)}, bf16[576,512]{1,0:T(8,128)(2,1)S(1)}, u32[]{:S(2)}, u32[]{:S(2)}) collective-permute-start(bf16[576,512]{1,0:T(8,128)(2,1)S(1)} %all_gather.12.refs_0_), channel_id=1, source_target_pairs={{64,0},{128,64},{192,128},{256,192},{320,256},{384,320},{448,384},... | collective-permute-start | bytes 1769480 | tf_op jit(solution)/shard_map/ppermute | solution.py:237
  34.9 4.5 %collective-permute-start.2 = (bf16[288,256]{1,0:T(8,128)(2,1)S(1)}, bf16[288,256]{1,0:T(8,128)(2,1)S(1)}, u32[]{:S(2)}, u32[]{:S(2)}) collective-permute-start(bf16[288,256]{1,0:T(8,128)(2,1)S(1)} %get-tuple-element.50), channel_id=1, source_target_pairs={{1,0},{0,1},{3,2},{2,3},{5,4},{4,5},{7,6},{6,7},{9,8},{8,9},{11,10... | collective-permute-start | bytes 442376 | tf_op jit(solution)/shard_map/ppermute | solution.py:237
  42.3 5.2 %collective-permute-done.1.w = bf16[576,512]{1,0:T(8,128)(2,1)S(1)} collective-permute-done((bf16[576,512]{1,0:T(8,128)(2,1)S(1)}, bf16[576,512]{1,0:T(8,128)(2,1)S(1)}, u32[]{:S(2)}, u32[]{:S(2)}) %collective-permute-start.1) | collective-permute-done | bytes 589856 | tf_op jit(solution)/shard_map/ppermute | solution.py:237
  49.4 3.4 %collective-permute-start.4 = (bf16[576,512]{1,0:T(8,128)(2,1)S(1)}, bf16[576,512]{1,0:T(8,128)(2,1)S(1)}, u32[]{:S(2)}, u32[]{:S(2)}) collective-permute-start(bf16[576,512]{1,0:T(8,128)(2,1)S(1)} %collective-permute-done.1.w), channel_id=1, source_target_pairs={{448,0},{0,64},{64,128},{128,192},{192,256},{256,320},{320,384},{3... | collective-permute-start | bytes 1769480 | tf_op jit(solution)/shard_map/ppermute | solution.py:237
  53.6 3.5 %all-to-all-start = ((bf16[4,144,256]{2,1,0:T(8,128)(2,1)}), bf16[4,144,256]{2,1,0:T(8,128)(2,1)S(1)}, u32[]{:S(2)}, u32[]{:S(2)}) async-start(bf16[4,144,256]{2,1,0:T(8,128)(2,1)} %bitcast.5), calls=%async_computation | async-start | bytes 589824 | tf_op jit(solution)/shard_map/all_to_all | solution.py:258
  57.1 5.6 %all-to-all-done = bf16[4,144,256]{2,1,0:T(8,128)(2,1)S(1)} async-done(((bf16[4,144,256]{2,1,0:T(8,128)(2,1)}), bf16[4,144,256]{2,1,0:T(8,128)(2,1)S(1)}, u32[]{:S(2)}, u32[]{:S(2)}) %all-to-all-start) | async-done | bytes 294944 | tf_op jit(solution)/shard_map/all_to_all | solution.py:258
  64.7 3.1 %collective-permute-start.5 = (bf16[576,512]{1,0:T(8,128)(2,1)S(1)}, bf16[576,512]{1,0:T(8,128)(2,1)S(1)}, u32[]{:S(2)}, u32[]{:S(2)}) collective-permute-start(bf16[576,512]{1,0:T(8,128)(2,1)S(1)} %collective-permute-done.3.refs_2_), channel_id=1, source_target_pairs={{64,0},{128,64},{192,128},{256,192},{320,256},{384,320},{448,384},... | collective-permute-start | bytes 1769480 | tf_op jit(solution)/shard_map/ppermute | solution.py:237
  70.6 2.3 %copy-done = bf16[4608,512]{1,0:T(8,128)(2,1)S(1)} copy-done((bf16[4608,512]{1,0:T(8,128)(2,1)S(1)}, bf16[4608,512]{1,0:T(8,128)(2,1)}, u32[]{:S(2)}) %copy-start) | copy-done | bytes 4718616
  73.0 2.2 %arrange.1 = (bf16[512,4608]{1,0:T(8,128)(2,1)S(1)}, f32[2,256,256]{2,1,0:T(8,128)S(1)}, bf16[8,144,512]{2,1,0:T(8,128)(2,1)S(1)}) custom-call(s32[4]{0:T(128)S(1)} %pad_add_fusion.place, bf16[4608,512]{1,0:T(8,128)(2,1)S(1)} %copy-done), custom_call_target="tpu_custom_call" | custom-call | flops 1207959552 | bytes 9437184 | tf_op jit(solution)/shard_map/arrange/pallas_call | solution.py:72
  77.1 4.8 %collective-permute-done.6.refs_4_ = bf16[576,512]{1,0:T(8,128)(2,1)S(1)} collective-permute-done((bf16[576,512]{1,0:T(8,128)(2,1)S(1)}, bf16[576,512]{1,0:T(8,128)(2,1)S(1)}, u32[]{:S(2)}, u32[]{:S(2)}) %collective-permute-start.6) | collective-permute-done | bytes 589856 | tf_op jit(solution)/shard_map/ppermute | solution.py:237
  81.9 2.9 %collective-permute-start.7 = (bf16[288,512]{1,0:T(8,128)(2,1)S(1)}, bf16[288,512]{1,0:T(8,128)(2,1)S(1)}, u32[]{:S(2)}, u32[]{:S(2)}) collective-permute-start(bf16[288,512]{1,0:T(8,128)(2,1)S(1)} %slice.26), channel_id=1, source_target_pairs={{64,0},{128,64},{192,128},{256,192},{320,256},{384,320},{448,384},... | collective-permute-start | bytes 884744 | tf_op jit(solution)/shard_map/ppermute | solution.py:237
  84.8 2.4 %collective-permute-start.8 = (bf16[288,512]{1,0:T(8,128)(2,1)S(1)}, bf16[288,512]{1,0:T(8,128)(2,1)S(1)}, u32[]{:S(2)}, u32[]{:S(2)}) collective-permute-start(bf16[288,512]{1,0:T(8,128)(2,1)S(1)} %slice.27), channel_id=1, source_target_pairs={{448,0},{0,64},{64,128},{128,192},{192,256},{256,320},{320,384},{3... | collective-permute-start | bytes 884744 | tf_op jit(solution)/shard_map/ppermute | solution.py:237
  89.8 4.1 %collective-permute-done.8.w_b = bf16[288,512]{1,0:T(8,128)(2,1)S(1)} collective-permute-done((bf16[288,512]{1,0:T(8,128)(2,1)S(1)}, bf16[288,512]{1,0:T(8,128)(2,1)S(1)}, u32[]{:S(2)}, u32[]{:S(2)}) %collective-permute-start.8) | collective-permute-done | bytes 294944 | tf_op jit(solution)/shard_map/ppermute | solution.py:237
  93.9 4.1 %attend.1 = (bf16[512,256]{1,0:T(8,128)(2,1)}, f32[4,128]{1,0:T(4,128)S(1)}) custom-call(s32[4]{0:T(128)S(1)} %pad_add_fusion.1.info, f32[512,512]{1,0:T(8,128)S(1)} %project.1.total, bf16[512,4608]{1,0:T(8,128)(2,1)S(1)} %get-tuple-element.29.x_tok, bf16[576,512]{1,0:T(8,128)(2,1)S(1)} %copy-done.6, bf16[288,512]{1,0:T(8,128)(2,1)S(1)} %collective-permute-done.7.w_a, ...), custom_call_target="tpu_custom_call" | custom-call | flops 2818572288 | bytes 9437184 | tf_op jit(solution)/shard_map/attend/pallas_call | solution.py:155
  97.9 6.3 %collective-permute-start.9 = (bf16[512,256]{1,0:T(8,128)(2,1)}, bf16[512,256]{1,0:T(8,128)(2,1)}, u32[]{:S(2)}, u32[]{:S(2)}) collective-permute-start(bf16[512,256]{1,0:T(8,128)(2,1)} %get-tuple-element.43.refs_0_), channel_id=1, source_target_pairs={{16,0},{32,16},{48,32},{0,48},{17,1},{33,17},{49,33},{1,49},{18,2}... | collective-permute-start | bytes 786440 | tf_op jit(solution)/shard_map/ppermute | solution.py:237
  104.2 3.6 %collective-permute-start.10 = (bf16[512,256]{1,0:T(8,128)(2,1)}, bf16[512,256]{1,0:T(8,128)(2,1)}, u32[]{:S(2)}, u32[]{:S(2)}) collective-permute-start(bf16[512,256]{1,0:T(8,128)(2,1)} %get-tuple-element.43.refs_0_), channel_id=1, source_target_pairs={{32,0},{48,16},{0,32},{16,48},{33,1},{49,17},{1,33},{17,49},{34,2}... | collective-permute-start | bytes 786440 | tf_op jit(solution)/shard_map/ppermute | solution.py:237
  107.9 2.8 %collective-permute-start.11 = (bf16[512,256]{1,0:T(8,128)(2,1)}, bf16[512,256]{1,0:T(8,128)(2,1)}, u32[]{:S(2)}, u32[]{:S(2)}) collective-permute-start(bf16[512,256]{1,0:T(8,128)(2,1)} %get-tuple-element.43.refs_0_), channel_id=1, source_target_pairs={{48,0},{0,16},{16,32},{32,48},{49,1},{1,17},{17,33},{33,49},{50,2}... | collective-permute-start | bytes 786440 | tf_op jit(solution)/shard_map/ppermute | solution.py:237
  110.6 5.4 %psum.7 = f32[4,128]{1,0:T(4,128)S(1)} all-reduce(f32[4,128]{1,0:T(4,128)S(1)} %get-tuple-element.38), channel_id=1, replica_groups=mesh['z'=8,'x'=4,'y'=8,'core'=2] {'core'}, use_global_device_ids=true, to_apply=%region_0.1 | all-reduce | flops 512 | bytes 4096 | tf_op jit(solution)/shard_map/psum | solution.py:282
  116.6 6.2 %all-to-all-start.1 = ((f32[32,4,128]{2,1,0:T(4,128)}), f32[32,4,128]{2,1,0:T(4,128)}, u32[]{:S(2)}, u32[]{:S(2)}) async-start(f32[32,4,128]{2,1,0:T(4,128)} %broadcast_in_dim.4), calls=%async_computation.1 | async-start | bytes 131072 | tf_op jit(solution)/shard_map/all_to_all | solution.py:283
  125.2 6.6 %all-to-all-done.1 = f32[32,4,128]{2,1,0:T(4,128)} async-done(((f32[32,4,128]{2,1,0:T(4,128)}), f32[32,4,128]{2,1,0:T(4,128)}, u32[]{:S(2)}, u32[]{:S(2)}) %all-to-all-start.1) | async-done | bytes 65568 | tf_op jit(solution)/shard_map/all_to_all | solution.py:283
  133.1 2.8 %gradient.1 = bf16[8,144,256]{2,1,0:T(8,128)(2,1)S(1)} custom-call(s32[4]{0:T(128)S(1)} %pad_add_fusion.place, f32[4,8,4,128]{3,2,1,0:T(4,128)} %bitcast.7.norms, bf16[8,144,1536]{2,1,0:T(8,128)(2,1)S(1)} %stage.1.staged, bf16[8,144,512]{2,1,0:T(8,128)(2,1)S(1)} %copy-done.4, bf16[512,256]{1,0:T(8,128)(2,1)} %get-tuple-element.43.refs_0_, ...), custom_call_target="tpu_custom_call" | custom-call | flops 1207959552 | bytes 7077888 | tf_op jit(solution)/shard_map/gradient/pallas_call | solution.py:222
  136.7 3.8 %all-to-all-start.2 = ((bf16[8,144,256]{2,1,0:T(8,128)(2,1)}), bf16[8,144,256]{2,1,0:T(8,128)(2,1)S(1)}, u32[]{:S(2)}, u32[]{:S(2)}) async-start(bf16[8,144,256]{2,1,0:T(8,128)(2,1)} %copy-done.2), calls=%async_computation.2 | async-start | bytes 1179648 | tf_op jit(solution)/shard_map/all_to_all | solution.py:285
  142.5 15.2 %all-to-all-done.2 = bf16[8,144,256]{2,1,0:T(8,128)(2,1)S(1)} async-done(((bf16[8,144,256]{2,1,0:T(8,128)(2,1)}), bf16[8,144,256]{2,1,0:T(8,128)(2,1)S(1)}, u32[]{:S(2)}, u32[]{:S(2)}) %all-to-all-start.2) | async-done | bytes 589856 | tf_op jit(solution)/shard_map/all_to_all | solution.py:285
  (56 shorter events, 26.6 us)
Async XLA Ops:
  7.2 56.8 %all-gather.4.cloned.1.call-start = ((), (), s32[]{:S(2)}) async-start(), calls=%async_computation.3 | async-start | bytes 5013504 | tf_op jit(solution)/shard_map/all_gather | solution.py:249
  20.1 22.3 %collective-permute-start = (bf16[576,512]{1,0:T(8,128)(2,1)S(1)}, bf16[576,512]{1,0:T(8,128)(2,1)S(1)}, u32[]{:S(2)}, u32[]{:S(2)}) collective-permute-start(bf16[576,512]{1,0:T(8,128)(2,1)S(1)} %all_gather.12.refs_0_), channel_id=1, source_target_pairs={{64,0},{128,64},{192,128},{256,192},{320,256},{384,320},{448,384},... | collective-permute-start | bytes 1769480 | tf_op jit(solution)/shard_map/ppermute | solution.py:237
  32.0 15.5 %collective-permute-start.1 = (bf16[576,512]{1,0:T(8,128)(2,1)S(1)}, bf16[576,512]{1,0:T(8,128)(2,1)S(1)}, u32[]{:S(2)}, u32[]{:S(2)}) collective-permute-start(bf16[576,512]{1,0:T(8,128)(2,1)S(1)} %all_gather.12.refs_0_), channel_id=1, source_target_pairs={{448,0},{0,64},{64,128},{128,192},{192,256},{256,320},{320,384},{3... | collective-permute-start | bytes 1769480 | tf_op jit(solution)/shard_map/ppermute | solution.py:237
  34.9 5.5 %collective-permute-start.2 = (bf16[288,256]{1,0:T(8,128)(2,1)S(1)}, bf16[288,256]{1,0:T(8,128)(2,1)S(1)}, u32[]{:S(2)}, u32[]{:S(2)}) collective-permute-start(bf16[288,256]{1,0:T(8,128)(2,1)S(1)} %get-tuple-element.50), channel_id=1, source_target_pairs={{1,0},{0,1},{3,2},{2,3},{5,4},{4,5},{7,6},{6,7},{9,8},{8,9},{11,10... | collective-permute-start | bytes 442376 | tf_op jit(solution)/shard_map/ppermute | solution.py:237
  47.5 17.2 %copy-start.5 = (bf16[576,512]{1,0:T(8,128)(2,1)}, bf16[576,512]{1,0:T(8,128)(2,1)S(1)}, u32[]{:S(2)}) copy-start(bf16[576,512]{1,0:T(8,128)(2,1)S(1)} %collective-permute-done.1.w) | copy-start | bytes 1769476
  47.5 15.3 %collective-permute-start.3 = (bf16[576,512]{1,0:T(8,128)(2,1)S(1)}, bf16[576,512]{1,0:T(8,128)(2,1)S(1)}, u32[]{:S(2)}, u32[]{:S(2)}) collective-permute-start(bf16[576,512]{1,0:T(8,128)(2,1)S(1)} %collective-permute-done.refs_1_), channel_id=1, source_target_pairs={{64,0},{128,64},{192,128},{256,192},{320,256},{384,320},{448,384},... | collective-permute-start | bytes 1769480 | tf_op jit(solution)/shard_map/ppermute | solution.py:237
  49.4 14.5 %collective-permute-start.4 = (bf16[576,512]{1,0:T(8,128)(2,1)S(1)}, bf16[576,512]{1,0:T(8,128)(2,1)S(1)}, u32[]{:S(2)}, u32[]{:S(2)}) collective-permute-start(bf16[576,512]{1,0:T(8,128)(2,1)S(1)} %collective-permute-done.1.w), channel_id=1, source_target_pairs={{448,0},{0,64},{64,128},{128,192},{192,256},{256,320},{320,384},{3... | collective-permute-start | bytes 1769480 | tf_op jit(solution)/shard_map/ppermute | solution.py:237
  53.6 9.1 %all-to-all-start = ((bf16[4,144,256]{2,1,0:T(8,128)(2,1)}), bf16[4,144,256]{2,1,0:T(8,128)(2,1)S(1)}, u32[]{:S(2)}, u32[]{:S(2)}) async-start(bf16[4,144,256]{2,1,0:T(8,128)(2,1)} %bitcast.5), calls=%async_computation | async-start | bytes 589824 | tf_op jit(solution)/shard_map/all_to_all | solution.py:258
  57.0 58.9 %all-gather.6.cloned.1.call-start = ((), (), s32[]{:S(2)}) async-start(), calls=%async_computation.4 | async-start | bytes 3760128 | tf_op jit(solution)/shard_map/all_gather | solution.py:261
  63.9 23.3 %copy-start.8 = (s32[2]{0:T(128)S(1)}, s32[2]{0:T(128)}, u32[]{:S(2)}) copy-start(s32[2]{0:T(128)} %param.15) | copy-start | bytes 28
  64.0 23.3 %copy-start.9 = (s32[2]{0:T(128)S(1)}, s32[2]{0:T(128)}, u32[]{:S(2)}) copy-start(s32[2]{0:T(128)} %param.14) | copy-start | bytes 28
  64.7 12.4 %collective-permute-start.5 = (bf16[576,512]{1,0:T(8,128)(2,1)S(1)}, bf16[576,512]{1,0:T(8,128)(2,1)S(1)}, u32[]{:S(2)}, u32[]{:S(2)}) collective-permute-start(bf16[576,512]{1,0:T(8,128)(2,1)S(1)} %collective-permute-done.3.refs_2_), channel_id=1, source_target_pairs={{64,0},{128,64},{192,128},{256,192},{320,256},{384,320},{448,384},... | collective-permute-start | bytes 1769480 | tf_op jit(solution)/shard_map/ppermute | solution.py:237
  67.8 14.1 %collective-permute-start.6 = (bf16[576,512]{1,0:T(8,128)(2,1)S(1)}, bf16[576,512]{1,0:T(8,128)(2,1)S(1)}, u32[]{:S(2)}, u32[]{:S(2)}) collective-permute-start(bf16[576,512]{1,0:T(8,128)(2,1)S(1)} %collective-permute-done.4.refs_5_), channel_id=1, source_target_pairs={{448,0},{0,64},{64,128},{128,192},{192,256},{256,320},{320,384},{3... | collective-permute-start | bytes 1769480 | tf_op jit(solution)/shard_map/ppermute | solution.py:237
  70.6 2.3 %copy-start = (bf16[4608,512]{1,0:T(8,128)(2,1)S(1)}, bf16[4608,512]{1,0:T(8,128)(2,1)}, u32[]{:S(2)}) copy-start(bf16[4608,512]{1,0:T(8,128)(2,1)} %all-gather.4.cloned.1.call-done.x_t) | copy-start | bytes 14155780
  75.2 14.5 %copy-start.3 = (bf16[8,144,512]{2,1,0:T(8,128)(2,1)}, bf16[8,144,512]{2,1,0:T(8,128)(2,1)S(1)}, u32[]{:S(2)}) copy-start(bf16[8,144,512]{2,1,0:T(8,128)(2,1)S(1)} %get-tuple-element.42.own) | copy-start | bytes 3538948
  81.9 7.9 %collective-permute-start.7 = (bf16[288,512]{1,0:T(8,128)(2,1)S(1)}, bf16[288,512]{1,0:T(8,128)(2,1)S(1)}, u32[]{:S(2)}, u32[]{:S(2)}) collective-permute-start(bf16[288,512]{1,0:T(8,128)(2,1)S(1)} %slice.26), channel_id=1, source_target_pairs={{64,0},{128,64},{192,128},{256,192},{320,256},{384,320},{448,384},... | collective-permute-start | bytes 884744 | tf_op jit(solution)/shard_map/ppermute | solution.py:237
  84.8 9.1 %collective-permute-start.8 = (bf16[288,512]{1,0:T(8,128)(2,1)S(1)}, bf16[288,512]{1,0:T(8,128)(2,1)S(1)}, u32[]{:S(2)}, u32[]{:S(2)}) collective-permute-start(bf16[288,512]{1,0:T(8,128)(2,1)S(1)} %slice.27), channel_id=1, source_target_pairs={{448,0},{0,64},{64,128},{128,192},{192,256},{256,320},{320,384},{3... | collective-permute-start | bytes 884744 | tf_op jit(solution)/shard_map/ppermute | solution.py:237
  87.5 6.4 %copy-start.6 = (bf16[576,512]{1,0:T(8,128)(2,1)S(1)}, bf16[576,512]{1,0:T(8,128)(2,1)}, u32[]{:S(2)}) copy-start(bf16[576,512]{1,0:T(8,128)(2,1)} %copy-done.5) | copy-start | bytes 1769476
  87.5 6.4 %copy-start.7 = (bf16[512,256]{1,0:T(8,128)(2,1)S(1)}, bf16[512,256]{1,0:T(8,128)(2,1)}, u32[]{:S(2)}) copy-start(bf16[512,256]{1,0:T(8,128)(2,1)} %cot.1) | copy-start | bytes 786436
  97.9 27.3 %collective-permute-start.9 = (bf16[512,256]{1,0:T(8,128)(2,1)}, bf16[512,256]{1,0:T(8,128)(2,1)}, u32[]{:S(2)}, u32[]{:S(2)}) collective-permute-start(bf16[512,256]{1,0:T(8,128)(2,1)} %get-tuple-element.43.refs_0_), channel_id=1, source_target_pairs={{16,0},{32,16},{48,32},{0,48},{17,1},{33,17},{49,33},{1,49},{18,2}... | collective-permute-start | bytes 786440 | tf_op jit(solution)/shard_map/ppermute | solution.py:237
  104.2 21.0 %collective-permute-start.10 = (bf16[512,256]{1,0:T(8,128)(2,1)}, bf16[512,256]{1,0:T(8,128)(2,1)}, u32[]{:S(2)}, u32[]{:S(2)}) collective-permute-start(bf16[512,256]{1,0:T(8,128)(2,1)} %get-tuple-element.43.refs_0_), channel_id=1, source_target_pairs={{32,0},{48,16},{0,32},{16,48},{33,1},{49,17},{1,33},{17,49},{34,2}... | collective-permute-start | bytes 786440 | tf_op jit(solution)/shard_map/ppermute | solution.py:237
  107.9 17.4 %collective-permute-start.11 = (bf16[512,256]{1,0:T(8,128)(2,1)}, bf16[512,256]{1,0:T(8,128)(2,1)}, u32[]{:S(2)}, u32[]{:S(2)}) collective-permute-start(bf16[512,256]{1,0:T(8,128)(2,1)} %get-tuple-element.43.refs_0_), channel_id=1, source_target_pairs={{48,0},{0,16},{16,32},{32,48},{49,1},{1,17},{17,33},{33,49},{50,2}... | collective-permute-start | bytes 786440 | tf_op jit(solution)/shard_map/ppermute | solution.py:237
  116.6 15.2 %all-to-all-start.1 = ((f32[32,4,128]{2,1,0:T(4,128)}), f32[32,4,128]{2,1,0:T(4,128)}, u32[]{:S(2)}, u32[]{:S(2)}) async-start(f32[32,4,128]{2,1,0:T(4,128)} %broadcast_in_dim.4), calls=%async_computation.1 | async-start | bytes 131072 | tf_op jit(solution)/shard_map/all_to_all | solution.py:283
  136.7 21.0 %all-to-all-start.2 = ((bf16[8,144,256]{2,1,0:T(8,128)(2,1)}), bf16[8,144,256]{2,1,0:T(8,128)(2,1)S(1)}, u32[]{:S(2)}, u32[]{:S(2)}) async-start(bf16[8,144,256]{2,1,0:T(8,128)(2,1)} %copy-done.2), calls=%async_computation.2 | async-start | bytes 1179648 | tf_op jit(solution)/shard_map/all_to_all | solution.py:285
  (3 other events, 4.1 us)
Sparse Core Ops, SparseCore 0:
  10.1 51.1 all-gather.3
  64.8 42.6 all-gather.5
